TPU v7x, 512 devices: a whole 4x8x8 slice. The times are simulated.
512 devices in a mesh: member: 32 (over x, y), space: 16 (over z, core).
Axes of the slice: x: 4, y: 8, z: 8, core: 2. Of those that a mesh axis runs over, the one named last changes fastest.
Arguments:
- ensemble: float32 [32, 3, 32, 48, 128], P('member', None, 'space')
- obs_cell: int32 [8192], P('space'), may hold values from 0 to 12287
- obs_comp: int32 [8192], P('space'), may hold values from 0 to 2
- obs_value: float32 [8192], replicated, may hold values from -6 to 6
- obs_precision: float32 [8192], replicated, may hold values from 0.3 to 5
- loc_obs: int32 [16384, 128], P(('space', 'member')), may hold values from 0 to 8191
- loc_level: int32 [16384, 128], P(('space', 'member')), may hold values from 1 to 8
Outputs:
- analysis: float32 [32, 3, 32, 48, 128], P('member', None, 'space')
Inputs may be any that keep to these rules, and one draw needn't show every extreme that they name: Observation i lies in the slab of index i // 512; obs_cell is x' * 48 * 128 + y * 128 + z with x' counted within that slab.
All inputs are finite; a program needn't handle non-finite values.
Results may differ from a plain program's by a relative error of at most 0.0003.
Values sent between devices are 32-bit elements; how exact they have to be, the bound alone decides.
No kernel may reach another device: no remote copies, remote signals or barrier semaphores. Data moves between devices by JAX's collectives and lax.ppermute only.
A program may use at most 64 MiB of HBM per device.

v0:
```python
import jax
import jax.numpy as jnp
from jax import lax
from jax.sharding import PartitionSpec as P

NS_ITERS = 8
LEVELS = 8


PAIRS = ((0, 0), (1, 1), (2, 2), (0, 1), (0, 2), (1, 2))
HIGH = lax.Precision.HIGHEST


def from_everyone(shard, axis):
    size = lax.axis_size(axis)
    return lax.all_to_all(
        jnp.broadcast_to(shard[None], (size, *shard.shape)), axis, 0, 0, tiled=True
    )


def over_copies(shard, axis):
    everything = from_everyone(shard, axis)
    return jnp.sum(everything, axis=0)


def together(arrays, axis):
    ends = [0]
    for a in arrays:
        ends.append(ends[-1] + a.size)
    running = over_copies(jnp.concatenate([a.ravel() for a in arrays]), axis)
    return tuple((running[b:e].reshape(a.shape) for a, b, e in zip(arrays, ends, ends[1:])))


def with_halo(shard, sides, width):
    for axis, dim in sides:
        size, length = (lax.axis_size(axis), shard.shape[dim])
        up = [(i, (i + 1) % size) for i in range(size)]
        down = [(j, i) for i, j in up]
        last = lax.slice_in_dim(shard, length - width, length, axis=dim)
        initial = lax.slice_in_dim(shard, 0, width, axis=dim)
        before = lax.ppermute(last, axis, up)
        after = lax.ppermute(initial, axis, down)
        shard = jnp.concatenate([before, shard, after], axis=dim)
    return shard


def joined_along(pieces, dim):
    pieces = jnp.moveaxis(pieces, 0, dim)
    dims = pieces.shape
    return pieces.reshape(*dims[:dim], dims[dim] * dims[dim + 1], *dims[dim + 2 :])


def collect(shard, axis, dim):
    pieces = from_everyone(shard, axis)
    return joined_along(pieces, dim)


def pair_index(first, second):
    for place, pair in enumerate(PAIRS):
        if pair == (first, second) or pair == (second, first):
            return place
    return 0


def pair_weights():
    return jnp.array([1.0, 1.0, 1.0, 2.0, 2.0, 2.0], jnp.float32)[:, None, None, None]


def along_x(field):
    return 0.5 * (field[:, 2:] - field[:, :-2])


def along_y(field):
    rim_extended = jnp.pad(field, ((0, 0), (0, 0), (1, 1), (0, 0)))
    return 0.5 * (rim_extended[:, :, 2:] - rim_extended[:, :, :-2])


def along_z(field):
    return 0.5 * (jnp.roll(field, -1, 3) - jnp.roll(field, 1, 3))


def inner(field):
    return field[:, 1:-1]


def test_filter(field):
    smooth = 0.25 * (field[:, :-2] + 2.0 * field[:, 1:-1] + field[:, 2:])
    return 0.25 * (jnp.roll(smooth, 1, 3) + 2.0 * smooth + jnp.roll(smooth, -1, 3))


def strain(velocity):
    grads = (along_x(velocity), inner(along_y(velocity)), inner(along_z(velocity)))
    return jnp.stack([0.5 * (grads[b][a] + grads[a][b]) for a, b in PAIRS])


def magnitude(rate):
    return jnp.sqrt(2.0 * jnp.sum(pair_weights() * rate * rate, 0))


def eddy_substep(rim_extended, plane_sum, count):
    centre = inner(rim_extended)
    rate = strain(rim_extended)
    size = magnitude(rate)
    smooth = test_filter(rim_extended)
    rate_hat = strain(smooth)
    size_hat = magnitude(rate_hat)
    middle = inner(smooth)
    products = jnp.stack([centre[a] * centre[b] for a, b in PAIRS])
    leonard = test_filter(products) - jnp.stack([middle[a] * middle[b] for a, b in PAIRS])
    model = 2.0 * (test_filter(size[None] * rate) - 4.0 * size_hat[None] * rate_hat)
    weights = pair_weights()
    numer = jnp.sum(weights * leonard * model, axis=(0, 1, 3))
    denom = jnp.sum(weights * model * model, axis=(0, 1, 3))
    numer, denom = plane_sum(numer, denom)
    coeff = numer / count / (denom / count + 1e-06)
    stress = 2.0 * coeff[None, None, :, None] * size[None] * rate
    tendency = []
    for a in range(3):
        term = along_x(stress[pair_index(a, 0)][None])[0]
        term = term + inner(along_y(stress[pair_index(a, 1)][None]))[0]
        term = term + inner(along_z(stress[pair_index(a, 2)][None]))[0]
        tendency.append(term)
    return rim_extended[:, 2:-2] + 0.25 * jnp.stack(tendency)


def bmm(left, right):
    return jnp.einsum("mkc,knc->mnc", left, right, precision=HIGH)


def analyse(block, index, level, anomaly, innov, precision):
    member_states = block.shape[0]
    groups, cols_z = (block.shape[2], block.shape[4])
    cols = index.T
    local = jnp.take(anomaly, cols, axis=1)
    weight = level.T.astype(jnp.float32) / LEVELS * jnp.take(precision, cols)
    scaled = local * weight[None]
    eye = jnp.eye(member_states, dtype=jnp.float32)[:, :, None]
    matrix = (
        jnp.einsum("mjc,njc->mnc", scaled, local, precision=HIGH) + (member_states - 1) / 1.1 * eye
    )
    scale = jnp.sqrt(jnp.sum(matrix * matrix, axis=(0, 1)))
    root = matrix / scale
    inverse = jnp.broadcast_to(eye, matrix.shape)
    for sweep in range(NS_ITERS):
        factor = 0.5 * (3.0 * eye - bmm(inverse, root))
        root = bmm(root, factor)
        inverse = bmm(factor, inverse)
    cover = bmm(inverse, inverse) / scale
    drive = jnp.einsum("mjc,jc->mc", scaled, jnp.take(innov, cols), precision=HIGH)
    offset = jnp.einsum("mnc,nc->mc", cover, drive, precision=HIGH)
    transform = jnp.sqrt(member_states - 1.0) * inverse / jnp.sqrt(scale) + offset[:, None, :]
    transform = transform.reshape(member_states, member_states, groups, cols_z // 4)
    transform = jnp.repeat(transform, 4, axis=3)
    centre = jnp.mean(block, axis=0)
    spread = block - centre
    moved = jnp.einsum("mqgyz,mkgz->kqgyz", spread, transform, precision=HIGH)
    return centre + moved


def plane_totals(numer, denom):
    return together((numer, denom), "space")


def shards(ensemble, obs_cell, obs_comp, obs_value, obs_precision, loc_obs, loc_level):
    field = ensemble[0]
    rim_width, slab_depth, slab_extent = (field.shape[1], field.shape[2], field.shape[3])
    slab_parts = lax.axis_size("space")
    rim_extended = with_halo(field, (("space", 1),), 2)
    prior_state = eddy_substep(rim_extended, plane_totals, rim_width * slab_parts * slab_extent)
    grid_cells = rim_width * slab_depth * slab_extent
    slab_position = obs_comp * grid_cells + obs_cell
    local_part = jnp.take(prior_state.reshape(3 * grid_cells), slab_position)
    slab_values = lax.all_gather(local_part, "space", axis=0, tiled=True)
    observed_values = collect(slab_values[None], "member", 0)
    mean = jnp.mean(observed_values, axis=0)
    anomaly = observed_values - mean[None]
    innov = obs_value - mean
    outbound_rims = prior_state.reshape(1, 3, rim_width * slab_depth, slab_extent)
    gathered = lax.all_to_all(outbound_rims, "member", split_axis=2, concat_axis=0, tiled=True)
    member_states, count_rows = (gathered.shape[0], gathered.shape[2])
    block = gathered.reshape(member_states, 3, count_rows // 3, 3, slab_extent)
    result = analyse(block, loc_obs, loc_level, anomaly, innov, obs_precision)
    result = result.reshape(member_states, 3, count_rows, slab_extent)
    returned = lax.all_to_all(result, "member", split_axis=0, concat_axis=2, tiled=True)
    return returned.reshape(1, 3, rim_width, slab_depth, slab_extent)


def solution(mesh):
    in_specs = (
        P("member", None, "space", None, None),
        P("space"),
        P("space"),
        P(),
        P(),
        P(("space", "member"), None),
        P(("space", "member"), None),
    )
    out_specs = P("member", None, "space", None, None)
    return jax.shard_map(shards, mesh=mesh, in_specs=in_specs, out_specs=out_specs, check_vma=False)
```

profile of v0, /device:TPU:8, one launch (start us, length us, event | category | flops | bytes accessed | tf_op | source)
XLA Modules:
  0.0 189.1 jit_solution(16931744484002038471)
XLA Ops:
  0.0 8.5 %collective-permute-start.1 = (f32[3,2,48,128]{3,2,1,0:T(8,128)}, f32[3,2,48,128]{3,2,1,0:T(8,128)S(1)}, u32[]{:S(2)}, u32[]{:S(2)}) collective-permute-start(f32[3,2,48,128]{3,2,1,0:T(8,128)} %bitcast.210), channel_id=1, source_target_pairs={{1,0},{2,1},{3,2},{4,3},{5,4},{6,5},{7,6},{8,7},{9,8},{10,9},{11,1... | collective-permute-start | bytes 442376 | tf_op jit(solution)/shard_map/ppermute | solution.py:42
  8.5 0.7 compare_select_fusion.1
  9.2 2.3 %collective-permute-done.1 = f32[3,2,48,128]{3,2,1,0:T(8,128)S(1)} collective-permute-done((f32[3,2,48,128]{3,2,1,0:T(8,128)}, f32[3,2,48,128]{3,2,1,0:T(8,128)S(1)}, u32[]{:S(2)}, u32[]{:S(2)}) %collective-permute-start.1) | collective-permute-done | bytes 147488 | tf_op jit(solution)/shard_map/ppermute | solution.py:42
  11.5 3.0 %collective-permute-done = f32[3,2,48,128]{3,2,1,0:T(8,128)S(1)} collective-permute-done((f32[3,2,48,128]{3,2,1,0:T(8,128)}, f32[3,2,48,128]{3,2,1,0:T(8,128)S(1)}, u32[]{:S(2)}, u32[]{:S(2)}) %collective-permute-start) | collective-permute-done | bytes 147488 | tf_op jit(solution)/shard_map/ppermute | solution.py:41
  14.5 0.9 pad_maximum_fusion
  15.4 1.0 broadcast_multiply_fusion.2
  20.6 0.6 fusion.42
  22.0 3.5 %all-to-all-start = ((f32[16,1,96]{2,1,0:T(1,128)}), f32[16,1,96]{2,1,0:T(1,128)S(1)}, u32[]{:S(2)}, u32[]{:S(2)}) async-start(f32[16,1,96]{2,1,0:T(1,128)} %broadcast_in_dim.38), calls=%async_computation | async-start | bytes 16384 | tf_op jit(solution)/shard_map/all_to_all | solution.py:16
  25.5 7.4 %all-to-all-done = f32[16,1,96]{2,1,0:T(1,128)S(1)} async-done(((f32[16,1,96]{2,1,0:T(1,128)}), f32[16,1,96]{2,1,0:T(1,128)S(1)}, u32[]{:S(2)}, u32[]{:S(2)}) %all-to-all-start) | async-done | bytes 6176 | tf_op jit(solution)/shard_map/all_to_all | solution.py:16
  33.8 0.8 copy.266
  34.6 10.2 %all-to-all-start.1 = ((f32[1,3,96,128]{3,0,1,2:T(1,128)}), f32[1,3,96,128]{3,0,1,2:T(1,128)S(1)}, u32[]{:S(2)}, u32[]{:S(2)}) async-start(f32[1,3,96,128]{3,0,1,2:T(1,128)} %copy.266), calls=%async_computation.1 | async-start | bytes 294912 | tf_op jit(solution)/shard_map/all_to_all | solution.py:179
  44.8 3.1 %gather_fusion = f32[512]{0:T(512)S(1)} fusion(f32[36864]{0:T(1024)S(1)} %add.227, s32[1024]{0:T(1024)S(1)} %pad_clamp_fusion), kind=kCustom, calls=%fused_computation.2 | custom fusion | bytes 6144 | tf_op jit(solution)/shard_map/jit(_take)/gather | solution.py:172
  48.0 14.8 %all-gather = f32[16,1,512]{2,1,0:T(1,128)S(1)} all-gather(f32[1,1,512]{2,1,0:T(1,128)S(1)} %bitcast.228), channel_id=1, replica_groups=mesh['member'=32,'space'=16] {'space'}, dimensions={0}, use_global_device_ids=true | all-gather | bytes 34816 | tf_op jit(solution)/shard_map/all_gather | solution.py:173
  62.8 1.9 %broadcast_in_dim.70 = f32[32,1,8192]{2,1,0:T(1,128)} broadcast(f32[8192]{0:T(1024)S(1)} %bitcast.224), dimensions={2} | broadcast | bytes 1081344 | tf_op jit(solution)/shard_map/broadcast_in_dim | solution.py:17
  64.7 9.8 %all-to-all-start.2 = ((f32[32,1,8192]{2,1,0:T(1,128)}), f32[32,1,8192]{2,1,0:T(1,128)S(1)}, u32[]{:S(2)}, u32[]{:S(2)}) async-start(f32[32,1,8192]{2,1,0:T(1,128)} %broadcast_in_dim.70), calls=%async_computation.2 | async-start | bytes 2097152 | tf_op jit(solution)/shard_map/all_to_all | solution.py:16
  74.7 23.0 %gather_fusion.2 = f32[4096]{0:T(1024)S(1)} fusion(f32[8192]{0:T(1024)S(1)} %copy-done, s32[4096]{0:T(1024)S(1)} %broadcast_clamp_fusion), kind=kCustom, calls=%fused_computation.clone | custom fusion | bytes 49152 | tf_op jit(solution)/shard_map/jit(_take)/gather | solution.py:135
  98.2 0.9 copy.268
  99.4 3.7 %all-to-all-done.2 = f32[32,1,8192]{2,1,0:T(1,128)S(1)} async-done(((f32[32,1,8192]{2,1,0:T(1,128)}), f32[32,1,8192]{2,1,0:T(1,128)S(1)}, u32[]{:S(2)}, u32[]{:S(2)}) %all-to-all-start.2) | async-done | bytes 1048608 | tf_op jit(solution)/shard_map/all_to_all | solution.py:16
  103.1 0.7 reduce_sum.78
  103.8 3.1 %copy.269 = f32[32,1,8192]{0,2,1:T(8,128)} copy(f32[32,1,8192]{2,1,0:T(1,128)S(1)} %all-to-all-done.2) | data formatting | bytes 2097152 | tf_op jit(solution)/shard_map/all_to_all | solution.py:16
  106.9 4.2 %bitcast_subtract_fusion = f32[32,8192]{0,1:T(8,128)} fusion(f32[32,1,8192]{0,2,1:T(8,128)} %copy.269, f32[8192]{0:T(1024)S(1)} %get-tuple-element.56), kind=kLoop, calls=%fused_computation.4 | loop fusion | flops 262144 | bytes 2129920 | tf_op jit(solution)/shard_map/sub | solution.py:176
  111.1 13.0 %gather_fusion.1 = f32[4096,32]{1,0:T(8,128)S(1)} fusion(f32[32,8192]{0,1:T(8,128)} %bitcast_subtract_fusion, s32[4096]{0:T(1024)S(1)} %broadcast_clamp_fusion), kind=kCustom, calls=%fused_computation.3 | custom fusion | bytes 1064960 | tf_op jit(solution)/shard_map/jit(_take)/gather | solution.py:134
  124.0 1.3 copy.271
  125.3 23.2 %gather_fusion.3 = f32[4096]{0:T(1024)S(1)} fusion(f32[8192]{0:T(1024)S(1)} %get-tuple-element.55, s32[4096]{0:T(1024)S(1)} %broadcast_clamp_fusion), kind=kCustom, calls=%fused_computation.1.clone | custom fusion | bytes 49152 | tf_op jit(solution)/shard_map/jit(_take)/gather | solution.py:149
  148.7 1.2 multiply_reduce_fusion
  149.9 0.7 fusion.18
  151.2 0.7 convolution_bitcast_fusion.21
  151.9 0.6 fusion.16
  152.5 0.6 convolution_bitcast_fusion.19
  153.2 0.6 convolution_bitcast_fusion.18
  153.8 0.6 fusion.14
  155.1 0.6 convolution_bitcast_fusion.15
  155.7 0.6 fusion.12
  156.4 0.6 convolution_bitcast_fusion.13
  157.0 0.6 convolution_bitcast_fusion.12
  157.7 0.6 fusion.10
  159.0 0.6 convolution_bitcast_fusion.9
  159.6 0.6 fusion.8
  160.3 0.9 convolution_bitcast_fusion.7
  161.2 0.6 convolution_bitcast_fusion.6
  161.8 0.6 fusion.6
  163.1 0.6 convolution_bitcast_fusion.3
  163.8 0.6 fusion.4
  165.1 0.9 convolution_bitcast_fusion.25
  166.0 0.6 fusion.2
  168.3 2.8 %fusion.1 = f32[32,3,3,128]{0,2,1,3:T(4,128)S(1)} fusion(f32[32,32,128,1]{1,0,3,2:T(8,128)S(1)} %bitcast.216, f32[32,3,3,128]{0,2,1,3:T(4,128)S(1)} %copy.302, f32[3,3,128]{1,0,2:T(4,128)S(1)} %copy-done.2), kind=kOutput, calls=%fused_computation.7 | convolution fusion | flops 14192640 | bytes 823808 | tf_op jit(solution)/shard_map/mqgyz,mkgz->kqgyz/dot_general | solution.py:156
  171.4 16.8 %all_to_all.41 = f32[32,3,3,128]{3,2,1,0:T(4,128)S(1)} all-to-all(f32[32,3,3,128]{3,2,1,0:T(4,128)S(1)} %copy.303), channel_id=1, replica_groups=mesh['member'=32,'space'=16] {'member'}, dimensions={0} | all-to-all | bytes 294912 | tf_op jit(solution)/shard_map/all_to_all | solution.py:184
  188.3 0.8 copy.304
  (114 shorter events, 11.6 us)
Async XLA Ops:
  0.0 74.7 %copy-start = (f32[8192]{0:T(1024)S(1)}, f32[8192]{0:T(1024)}, u32[]{:S(2)}) copy-start(f32[8192]{0:T(1024)} %param.16) | copy-start | bytes 98308
  0.0 11.5 %collective-permute-start.1 = (f32[3,2,48,128]{3,2,1,0:T(8,128)}, f32[3,2,48,128]{3,2,1,0:T(8,128)S(1)}, u32[]{:S(2)}, u32[]{:S(2)}) collective-permute-start(f32[3,2,48,128]{3,2,1,0:T(8,128)} %bitcast.210), channel_id=1, source_target_pairs={{1,0},{2,1},{3,2},{4,3},{5,4},{6,5},{7,6},{8,7},{9,8},{10,9},{11,1... | collective-permute-start | bytes 442376 | tf_op jit(solution)/shard_map/ppermute | solution.py:42
  8.5 6.0 %collective-permute-start = (f32[3,2,48,128]{3,2,1,0:T(8,128)}, f32[3,2,48,128]{3,2,1,0:T(8,128)S(1)}, u32[]{:S(2)}, u32[]{:S(2)}) collective-permute-start(f32[3,2,48,128]{3,2,1,0:T(8,128)} %bitcast.211), channel_id=1, source_target_pairs={{0,1},{1,2},{2,3},{3,4},{4,5},{5,6},{6,7},{7,8},{8,9},{9,10},{10,1... | collective-permute-start | bytes 442376 | tf_op jit(solution)/shard_map/ppermute | solution.py:41
  17.2 0.9 copy-start.1
  18.7 0.7 copy-start.7
  20.0 0.7 copy-start.8
  22.0 10.9 %all-to-all-start = ((f32[16,1,96]{2,1,0:T(1,128)}), f32[16,1,96]{2,1,0:T(1,128)S(1)}, u32[]{:S(2)}, u32[]{:S(2)}) async-start(f32[16,1,96]{2,1,0:T(1,128)} %broadcast_in_dim.38), calls=%async_computation | async-start | bytes 16384 | tf_op jit(solution)/shard_map/all_to_all | solution.py:16
  34.6 28.2 %all-to-all-start.1 = ((f32[1,3,96,128]{3,0,1,2:T(1,128)}), f32[1,3,96,128]{3,0,1,2:T(1,128)S(1)}, u32[]{:S(2)}, u32[]{:S(2)}) async-start(f32[1,3,96,128]{3,0,1,2:T(1,128)} %copy.266), calls=%async_computation.1 | async-start | bytes 294912 | tf_op jit(solution)/shard_map/all_to_all | solution.py:179
  48.0 26.5 %copy-start.3 = (s32[32,128]{1,0:T(8,128)S(1)}, s32[32,128]{1,0:T(8,128)}, u32[]{:S(2)}) copy-start(s32[32,128]{1,0:T(8,128)} %param.17) | copy-start | bytes 49156
  64.7 38.4 %all-to-all-start.2 = ((f32[32,1,8192]{2,1,0:T(1,128)}), f32[32,1,8192]{2,1,0:T(1,128)S(1)}, u32[]{:S(2)}, u32[]{:S(2)}) async-start(f32[32,1,8192]{2,1,0:T(1,128)} %broadcast_in_dim.70), calls=%async_computation.2 | async-start | bytes 2097152 | tf_op jit(solution)/shard_map/all_to_all | solution.py:16
  97.7 6.1 %copy-start.5 = (f32[8192]{0:T(1024)S(1)}, f32[8192]{0:T(1024)}, u32[]{:S(2)}) copy-start(f32[8192]{0:T(1024)} %param.15) | copy-start | bytes 98308
  125.3 23.4 %copy-start.4 = (s32[32,128]{1,0:T(8,128)S(1)}, s32[32,128]{1,0:T(8,128)}, u32[]{:S(2)}) copy-start(s32[32,128]{1,0:T(8,128)} %param.17) | copy-start | bytes 49156
  125.3 23.4 %copy-start.6 = (s32[32,128]{1,0:T(8,128)S(1)}, s32[32,128]{1,0:T(8,128)}, u32[]{:S(2)}) copy-start(s32[32,128]{1,0:T(8,128)} %param.18) | copy-start | bytes 49156
  167.3 1.0 copy-start.2
where the time goes:
time: 190 us; the launch traced here: 189 us
  local copies, waits for them, and re-layouts  76.6 us (40%)
  starting transfers between devices  31.9 us (17%)
  blocking collectives  31.6 us (17%)
  matrix products  21.1 us (11%)
  waiting for transfers between devices  16.4 us (9%)
  other arithmetic  10.6 us (6%)
    gather x3, local copies, waits for them, and re-layouts, analyse(): jnp.take(innov, cols)  23.3 us
    gather x3, local copies, waits for them, and re-layouts, analyse(): weight = level.T.astype(jnp.float32) / LEVELS * jnp.take(precision, cols)  23.2 us
    all_to_all x1, blocking collectives, shards(): lax.all_to_all(result, 'member', split_axis=0, concat_axis=2, tiled=True)  16.8 us
    dot_general x24, matrix products, bmm(): return jnp.einsum('mkc,knc->mnc', left, right, precision=HIGH)  15.6 us
    all_gather x1, blocking collectives, shards(): slab_values = lax.all_gather(local_part, 'space', axis=0, tiled=True)  14.8 us
    gather x2, local copies, waits for them, and re-layouts, analyse(): local = jnp.take(anomaly, cols, axis=1)  14.2 us
    all_to_all x2, starting transfers between devices, from_everyone(): lax.all_to_all(jnp.broadcast_to(shard[None], (size, *shard.shape)), axis,...  13.3 us
    all_to_all x2, waiting for transfers between devices, from_everyone(): lax.all_to_all(jnp.broadcast_to(shard[None], (size, *shard.shape)), axis,...  11.1 us
  transfers between devices with their start and end apart: 5, of which 4 were waited for; matrix products, arithmetic and copies ran while one was open for 15% of the time, Pallas kernels for 0%

commit v1 on v0

v1 whole, which is shorter than its diff:
```python
import functools

import jax
import jax.numpy as jnp
from jax import lax
from jax.experimental import pallas as pl
from jax.experimental.pallas import tpu as pltpu
from jax.sharding import PartitionSpec as P

NS_ITERS = 8
LEVELS = 8
K = 32
LOC = 128
CHUNKS = 32
ROWS = 16

PAIRS = ((0, 0), (1, 1), (2, 2), (0, 1), (0, 2), (1, 2))
F32 = jnp.float32
BF16 = jnp.bfloat16
VMEM = pl.BlockSpec(memory_space=pltpu.VMEM)
SMEM = pl.BlockSpec(memory_space=pltpu.SMEM)


def iota(shape, dim):
    return lax.broadcasted_iota(jnp.int32, shape, dim)


def pair_index(first, second):
    return PAIRS.index((min(first, second), max(first, second)))


def split2(value):
    high = value.astype(BF16)
    return high, (value - high.astype(F32)).astype(BF16)


def split3(value):
    high = value.astype(BF16)
    rest = value - high.astype(F32)
    middle = rest.astype(BF16)
    return high, middle, (rest - middle.astype(F32)).astype(BF16)


def dot(left, right):
    return jnp.dot(left, right, preferred_element_type=F32)


def dot_t(left, right):
    return lax.dot_general(left, right, (((0,), (0,)), ((), ())), preferred_element_type=F32)


def along_y(plane):
    count = plane.shape[0]
    row = iota(plane.shape, 0)
    later = jnp.where(row == count - 1, 0.0, pltpu.roll(plane, count - 1, 0))
    earlier = jnp.where(row == 0, 0.0, pltpu.roll(plane, 1, 0))
    return 0.5 * (later - earlier)


def along_z(plane):
    count = plane.shape[1]
    return 0.5 * (pltpu.roll(plane, count - 1, 1) - pltpu.roll(plane, 1, 1))


def filter_z(plane):
    count = plane.shape[1]
    return 0.25 * (pltpu.roll(plane, 1, 1) + 2.0 * plane + pltpu.roll(plane, count - 1, 1))


def filter_xz(planes, p):
    return filter_z(0.25 * (planes[p - 1] + 2.0 * planes[p] + planes[p + 1]))


def strain(fields, p):
    grads = []
    for b in range(3):
        if b == 0:
            grads.append([0.5 * (f[p + 1] - f[p - 1]) for f in fields])
        elif b == 1:
            grads.append([along_y(f[p]) for f in fields])
        else:
            grads.append([along_z(f[p]) for f in fields])
    return [0.5 * (grads[b][a] + grads[a][b]) for a, b in PAIRS]


def weighted(terms):
    return terms[0] + terms[1] + terms[2] + 2.0 * (terms[3] + terms[4] + terms[5])


def magnitude(rate):
    return jnp.sqrt(2.0 * weighted([r * r for r in rate]))


def model_kernel(before, own, after, sums, tau):
    fields = [
        {0: before[a, 0], 1: before[a, 1], 2: own[a, 0], 3: own[a, 1], 4: after[a, 0], 5: after[a, 1]}
        for a in range(3)
    ]
    for p in range(1, 5):
        rate = strain(fields, p)
        size = magnitude(rate)
        for i in range(6):
            tau[i, p - 1] = size * rate[i]
    smooth = [{p: filter_xz(f, p) for p in range(1, 5)} for f in fields]
    numer = 0.0
    denom = 0.0
    for p in (2, 3):
        rate = strain(smooth, p)
        size = magnitude(rate)
        top, bottom = [], []
        for i, (a, b) in enumerate(PAIRS):
            product = {q: fields[a][q] * fields[b][q] for q in (p - 1, p, p + 1)}
            leonard = filter_xz(product, p) - smooth[a][p] * smooth[b][p]
            flux = {q: tau[i, q - 1] for q in (p - 1, p, p + 1)}
            model = 2.0 * (filter_xz(flux, p) - 4.0 * size * rate[i])
            top.append(leonard * model)
            bottom.append(model * model)
        numer = numer + weighted(top)
        denom = denom + weighted(bottom)
    pad = jnp.zeros((32, 128), F32)
    both = jnp.concatenate([numer, denom, pad], axis=0).T
    total = jnp.sum(both, axis=0, keepdims=True)
    sums[...] = jnp.broadcast_to(total[None], sums.shape)


def forecast_kernel(count, sums, own, tau, place, lane, send, state):
    total = sums[0]
    for i in range(1, sums.shape[0]):
        total = total + sums[i]
    denom = pltpu.roll(total, 128 - 48, 1)
    coeff = (total / count) / (denom / count + 1e-6)
    coeff = 2.0 * jnp.broadcast_to(coeff, (128, 128)).T[:48]
    stress = [[coeff * tau[i, p] for p in range(4)] for i in range(6)]
    for a in range(3):
        for x in range(2):
            p = x + 1
            along = stress[pair_index(a, 0)]
            term = 0.5 * (along[p + 1] - along[p - 1])
            term = term + along_y(stress[pair_index(a, 1)][p])
            term = term + along_z(stress[pair_index(a, 2)][p])
            start = a * 96 + x * 48
            state[start : start + 48, :] = own[a, x] + 0.25 * term
    values = state[...]
    chosen = (iota((288, 512), 0) == place[...]).astype(F32).astype(BF16)
    first, second, third = split3(values)
    picked = (dot_t(third, chosen) + dot_t(second, chosen)) + dot_t(first, chosen)
    picked = jnp.where(iota((128, 512), 0) == lane[...], picked, 0.0)
    picked = jnp.sum(picked, axis=0, keepdims=True)
    for m in range(K):
        for a in range(3):
            send[m, 3 * a : 3 * a + 3, :] = state[a * 96 + 3 * m : a * 96 + 3 * m + 3, :]
    for q in range(4):
        piece = picked[:, q * 128 : (q + 1) * 128]
        send[:, 9 + q, :] = jnp.broadcast_to(piece, (K, 128))
    send[:, 13:16, :] = jnp.zeros((K, 3, 128), F32)


def table_kernel(received, value, precision, table):
    member = iota((K, 128), 0)
    parts = []
    for q in range(4):
        seen = received[pl.ds(9 + q, K, stride=ROWS), :]
        mean = jnp.sum(seen, axis=0, keepdims=True) * (1.0 / K)
        innov = value[q : q + 1, :] - mean
        root = jnp.sqrt(precision[q : q + 1, :])
        parts.append(jnp.where(member == K - 1, innov, seen - mean) * root)
    block = jnp.concatenate(parts, axis=0).T
    for i in range(table.shape[0]):
        table[i] = block


def block_diagonal(value, mask):
    return jnp.concatenate([value] * 8, axis=0) * mask


def times_blocks(left, right, mask):
    r1, r2 = split2(right)
    l1, l2 = split2(left)
    rows = left.shape[0]
    wide = dot(jnp.concatenate([l1, l2], axis=0), block_diagonal(r1, mask))
    return wide[:rows] + wide[rows:] + dot(l1, block_diagonal(r2, mask))


def exact_times(left, constant):
    rows = left.shape[0]
    wide = dot(jnp.concatenate(split3(left), axis=0), constant)
    return (wide[2 * rows :] + wide[rows : 2 * rows]) + wide[:rows]


def analysis_kernel(places, code, near, far, received, out, table, picked):
    table[0:1024, :] = near[...]
    table[1024:2048, :] = far[...]

    def fetch(c, carry):
        base = pl.multiple_of(c * LOC, LOC)
        target = picked.at[pl.ds(base, LOC)]
        for j in range(LOC):
            target[pl.ds(j, 1), :] = table[pl.ds(places[base + j], 1), :]
        return carry

    lax.fori_loop(0, CHUNKS, fetch, 0)

    columns = jnp.concatenate([code[...], jnp.zeros((96, 128), jnp.int32)], axis=0).T
    quarter = iota((LOC, 128), 1) // 32
    small_quarter = iota((K, 128), 1) // 32
    grams = []
    for c in range(CHUNKS):
        rows = picked[c * LOC : (c + 1) * LOC, :]
        mark = jnp.broadcast_to(columns[:, c : c + 1], (LOC, 128))
        level = (mark & 15).astype(F32) * (1.0 / LEVELS)
        weight = jnp.where((mark >> 4) == quarter, level, 0.0)
        g1, g2 = split2(rows)
        a1, a2 = split2(weight * rows)
        wide = dot_t(a1, jnp.concatenate([g1, g2], axis=1))
        full = wide[:, :128] + wide[:, 128:] + dot_t(a2, g1)
        fold = full[0:32]
        for q in range(1, 4):
            fold = jnp.where(small_quarter == q, full[32 * q : 32 * q + 32], fold)
        fold = fold + pltpu.roll(fold, 64, 1)
        fold = fold + pltpu.roll(fold, 32, 1)
        if c % 4 == 0:
            held = fold
        else:
            held = jnp.where(small_quarter == c % 4, fold, held)
        if c % 4 == 3:
            grams.append(held)
    grams = [jnp.concatenate(grams[2 * g : 2 * g + 2], axis=1) for g in range(4)]

    tall = iota((256, 256), 0)
    wide_lane = iota((256, 256), 1)
    same = (tall // 32) == (wide_lane // 32)
    mask = jnp.where(same, 1.0, 0.0).astype(BF16)
    last = (wide_lane % 32) == 31
    not_last_row = (tall % 32) != 31
    rebuild = jnp.where(last, jnp.where(same & not_last_row, -1.0, 0.0), jnp.where(tall == wide_lane, 1.0, 0.0))
    rebuild = rebuild.astype(BF16)
    member = iota((K, 256), 0)
    eye = jnp.where(member == iota((K, 256), 1) % 32, 1.0, 0.0)

    count = len(grams)
    drive, scale, y, z = [], [], [], []
    for g in range(count):
        gram = grams[g]
        body = jnp.where(member == K - 1, 0.0, gram)
        body = jnp.where(member == K - 1, -jnp.sum(body, axis=0, keepdims=True), body)
        push = jnp.broadcast_to(gram[K - 1 : K, :], (8, 256))
        whole = exact_times(jnp.concatenate([body, push], axis=0), rebuild)
        matrix = whole[:K] + ((K - 1) / 1.1) * eye
        drive.append(whole[K:])
        square = jnp.broadcast_to(jnp.sum(matrix * matrix, axis=0, keepdims=True), (8, 256))
        norm = jnp.sqrt(exact_times(square, mask))
        scale.append(norm)
        y.append(matrix / norm[0:1])
    for sweep in range(NS_ITERS):
        for g in range(count):
            if sweep == 0:
                factor = 1.5 * eye - 0.5 * y[g]
                z[g:] = [factor]
                y[g] = times_blocks(y[g], factor, mask)
                continue
            factor = 1.5 * eye - 0.5 * times_blocks(z[g], y[g], mask)
            if sweep == NS_ITERS - 1:
                z[g] = times_blocks(z[g], factor, mask)
            else:
                both = times_blocks(jnp.concatenate([y[g], z[g]], axis=0), factor, mask)
                y[g], z[g] = both[:K], both[K:]
    total = None
    cells = [received[pl.ds(r, K, stride=ROWS), :] for r in range(9)]
    centres = [jnp.sum(v, axis=0, keepdims=True) * (1.0 / K) for v in cells]
    spreads = [v - m for v, m in zip(cells, centres)]
    spreads = jnp.concatenate(spreads, axis=1)
    h1, h2 = split2(spreads)
    owner = iota((256, 9 * 128), 0) // 32
    chunk = (iota((256, 9 * 128), 1) % 128) // 4
    for g in range(count):
        pull = times_blocks(times_blocks(drive[g], z[g], mask), z[g], mask) / scale[g]
        root = z[g] * (jnp.sqrt(float(K - 1)) / jnp.sqrt(scale[g][0:1]))
        left1, left2 = split2(jnp.concatenate([root, pull], axis=0))
        here = jnp.where(chunk == owner + 8 * g, 1.0, 0.0).astype(BF16)
        right1 = block_diagonal(h1, here)
        right2 = block_diagonal(h2, here)
        rows = left1.shape[0]
        part = dot(jnp.concatenate([left1, left2], axis=0), right1)
        part = part[:rows] + part[rows:] + dot(left1, right2)
        total = part if total is None else total + part
    moved = total[:K] + total[K : K + 1]
    for r in range(9):
        out[pl.ds(r, K, stride=ROWS), :] = moved[:, r * 128 : (r + 1) * 128] + centres[r]
    for r in range(9, ROWS):
        out[pl.ds(r, K, stride=ROWS), :] = jnp.zeros((K, 128), F32)


def call(kernel, shapes, ins, scratch=(), limit=None):
    return pl.pallas_call(
        kernel,
        out_shape=[jax.ShapeDtypeStruct(s, F32) for s in shapes],
        in_specs=ins,
        out_specs=[VMEM] * len(shapes),
        scratch_shapes=list(scratch),
        compiler_params=pltpu.CompilerParams(vmem_limit_bytes=limit),
    )


def shards(ensemble, obs_cell, obs_comp, obs_value, obs_precision, loc_obs, loc_level):
    field = ensemble[0]
    _, depth, height, extent = field.shape
    parts = lax.axis_size("space")
    here = lax.axis_index("space")
    up = [(i, (i + 1) % parts) for i in range(parts)]
    down = [(j, i) for i, j in up]

    slab = loc_obs // 512
    within = loc_obs % 512
    places = (slab // 2) * 128 + ((slab + here) % 2) * 1024 + within % 128
    places = places.reshape(CHUNKS * LOC)
    code = (within // 128) * 16 + loc_level
    place = (obs_comp * (depth * height) + obs_cell // extent).reshape(1, 512)
    lane = (obs_cell % extent).reshape(1, 512)
    value = lax.dynamic_index_in_dim(obs_value.reshape(parts, 4, 128), here, 0, keepdims=False)
    precision = lax.dynamic_index_in_dim(obs_precision.reshape(parts, 4, 128), here, 0, keepdims=False)

    before = lax.ppermute(field, "space", up)
    after = lax.ppermute(field, "space", down)
    sums, tau = call(model_kernel, [(parts, 1, 128), (6, 4, height, extent)], [VMEM] * 3)(before, field, after)
    sums = lax.all_to_all(sums, "space", 0, 0, tiled=True)
    count = depth * parts * extent
    (send,) = call(
        functools.partial(forecast_kernel, count),
        [(K, ROWS, 128)],
        [VMEM] * 5,
        [pltpu.VMEM((3 * depth * height, extent), F32)],
    )(sums, field, tau, place, lane)
    received = lax.all_to_all(send, "member", 0, 0, tiled=True).reshape(K * ROWS, 128)
    (table,) = call(table_kernel, [(parts // 2, 128, 128)], [VMEM] * 3)(received, value, precision)
    same_core = [[2 * i + c for i in range(parts // 2)] for c in range(2)]
    near = lax.all_to_all(table, "space", 0, 0, axis_index_groups=same_core, tiled=True)
    near = near.reshape(parts * 64, 128)
    far = lax.ppermute(near, "space", [(i, i ^ 1) for i in range(parts)])
    (result,) = call(
        analysis_kernel,
        [(K * ROWS, 128)],
        [SMEM] + [VMEM] * 4,
        [pltpu.VMEM((2048, 128), F32), pltpu.VMEM((CHUNKS * LOC, 128), F32)],
        limit=40 * 2**20,
    )(places, code, near, far, received)
    returned = lax.all_to_all(result.reshape(K, ROWS, 128), "member", 0, 0, tiled=True)
    returned = returned[:, :9].reshape(K, 3, 3, 128)
    returned = jnp.transpose(returned, (1, 0, 2, 3))
    return returned.reshape(1, 3, depth, height, extent)


def solution(mesh):
    in_specs = (
        P("member", None, "space", None, None),
        P("space"),
        P("space"),
        P(),
        P(),
        P(("space", "member"), None),
        P(("space", "member"), None),
    )
    out_specs = P("member", None, "space", None, None)
    return jax.shard_map(shards, mesh=mesh, in_specs=in_specs, out_specs=out_specs, check_vma=False)
```

time: 190 us -> 112 us (0.59)
  local copies, waits for them, and re-layouts: 76.6 us -> 4.14 us
  matrix products: 21.1 us -> 0 us
  Pallas kernels: 0 us -> 19.2 us
  other arithmetic: 10.6 us -> 0.64 us
  waiting for transfers between devices: 16.4 us -> 25.7 us
  starting transfers between devices: 31.9 us -> 24.1 us
  blocking collectives: 31.6 us -> 37.4 us
    gather x9 -> x0, local copies, waits for them, and re-layouts: 63.9 us -> none  [the longest x3 23.3 us: analyse(): jnp.take(innov, cols)]
    dot_general x28 -> x0, matrix products: 21.1 us -> none  [the longest x24 15.6 us: bmm(): return jnp.einsum('mkc,knc->mnc', left, right, precision=HIGH)]
    all_to_all x1 -> x2, blocking collectives: 16.8 us -> 37.4 us  [the longest x1 20 us: shards(): lax.all_to_all(table, 'space', 0, 0, axis_index_groups=same_core, tiled=T...]
    pallas_call x0 -> x4, Pallas kernels: none -> 19.2 us  [the longest x1 11.9 us: shards(): call(analysis_kernel, [(K * ROWS, 128)], [SMEM] + [VMEM] * 4, [pltpu.VMEM...]
    all_gather x1 -> x0, blocking collectives: 14.8 us -> none  [shards(): slab_values = lax.all_gather(local_part, 'space', axis=0, tiled=True)]
    all_to_all x3 -> x2, starting transfers between devices: 23.4 us -> 13.7 us  [the longest x1 10.2 us: shards(): lax.all_to_all(send, 'member', 0, 0, tiled=True).reshape(K * ROWS, 128)]
    all_to_all x3 -> x2, waiting for transfers between devices: 11.1 us -> 17.9 us  [the longest x1 11 us: shards(): lax.all_to_all(send, 'member', 0, 0, tiled=True).reshape(K * ROWS, 128)]
    sub x3 -> x0, other arithmetic: 4.18 us -> none  [the longest x1 4.16 us: shards(): anomaly = observed_values - mean[None]]
  transfers between devices with their start and end apart: 5 -> 5, of which waited for: 4 -> 5; matrix products, arithmetic and copies ran while one was open for 15% -> 2% of each run, Pallas kernels for 0% -> 0%
where the time goes in v1:
time: 112 us; the launch traced here: 111 us
  blocking collectives  37.4 us (33%)
  waiting for transfers between devices  25.7 us (23%)
  starting transfers between devices  24.1 us (22%)
  Pallas kernels  19.2 us (17%)
  local copies, waits for them, and re-layouts  4.14 us (4%)
    all_to_all x1, blocking collectives, shards(): lax.all_to_all(table, 'space', 0, 0, axis_index_groups=same_core, tiled=T...  20 us
    all_to_all x1, blocking collectives, shards(): lax.all_to_all(result.reshape(K, ROWS, 128), 'member', 0, 0, tiled=True)  17.3 us
    pallas_call x1, Pallas kernels, shards(): call(analysis_kernel, [(K * ROWS, 128)], [SMEM] + [VMEM] * 4, [pltpu.VMEM...  11.9 us
    all_to_all x1, waiting for transfers between devices, shards(): lax.all_to_all(send, 'member', 0, 0, tiled=True).reshape(K * ROWS, 128)  11 us
    all_to_all x1, starting transfers between devices, shards(): lax.all_to_all(send, 'member', 0, 0, tiled=True).reshape(K * ROWS, 128)  10.2 us
    ppermute x1, starting transfers between devices, shards(): after = lax.ppermute(field, 'space', down)  8.48 us
    all_to_all x1, waiting for transfers between devices, shards(): sums = lax.all_to_all(sums, 'space', 0, 0, tiled=True)  6.91 us
    all_to_all x1, starting transfers between devices, shards(): sums = lax.all_to_all(sums, 'space', 0, 0, tiled=True)  3.55 us
  transfers between devices with their start and end apart: 5, of which 5 were waited for; matrix products, arithmetic and copies ran while one was open for 2% of the time, Pallas kernels for 0%

profile of v1, /device:TPU:8, one launch (start us, length us, event | category | flops | bytes accessed | tf_op | source)
XLA Modules:
  0.0 111.2 jit_solution(1516076022172833716)
XLA Ops:
  0.0 8.5 %collective-permute-start.1 = (f32[3,2,48,128]{3,2,1,0:T(8,128)}, f32[3,2,48,128]{3,2,1,0:T(8,128)S(1)}, u32[]{:S(2)}, u32[]{:S(2)}) collective-permute-start(f32[3,2,48,128]{3,2,1,0:T(8,128)} %bitcast.24), channel_id=1, source_target_pairs={{1,0},{2,1},{3,2},{4,3},{5,4},{6,5},{7,6},{8,7},{9,8},{10,9},{11,1... | collective-permute-start | bytes 442376 | tf_op jit(solution)/shard_map/ppermute | solution.py:323
  8.5 0.0 collective-permute-start
  8.5 3.0 %collective-permute-done.1.after = f32[3,2,48,128]{3,2,1,0:T(8,128)S(1)} collective-permute-done((f32[3,2,48,128]{3,2,1,0:T(8,128)}, f32[3,2,48,128]{3,2,1,0:T(8,128)S(1)}, u32[]{:S(2)}, u32[]{:S(2)}) %collective-permute-start.1) | collective-permute-done | bytes 147488 | tf_op jit(solution)/shard_map/ppermute | solution.py:323
  11.5 0.0 copy-start.2
  11.5 3.0 %collective-permute-done.before = f32[3,2,48,128]{3,2,1,0:T(8,128)S(1)} collective-permute-done((f32[3,2,48,128]{3,2,1,0:T(8,128)}, f32[3,2,48,128]{3,2,1,0:T(8,128)S(1)}, u32[]{:S(2)}, u32[]{:S(2)}) %collective-permute-start) | collective-permute-done | bytes 147488 | tf_op jit(solution)/shard_map/ppermute | solution.py:322
  14.5 0.0 copy-done.2
  14.5 0.0 copy-start.3
  14.5 0.7 copy-done.3
  15.1 2.7 %shard_map.73 = (f32[16,1,128]{2,1,0:T(1,128)}, f32[6,4,48,128]{3,2,1,0:T(8,128)}) custom-call(f32[3,2,48,128]{3,2,1,0:T(8,128)} %copy-done.3, f32[3,2,48,128]{3,2,1,0:T(8,128)} %bitcast.26, f32[3,2,48,128]{3,2,1,0:T(8,128)} %copy-done.2), custom_call_target="tpu_custom_call" | custom-call | tf_op jit(solution)/shard_map/pallas_call | solution.py:324
  17.8 0.0 copy-start.7
  17.8 0.0 copy-start.8
  17.8 3.5 %all-to-all-start = ((f32[16,1,128]{2,1,0:T(1,128)}), f32[16,1,128]{2,1,0:T(1,128)S(1)}, u32[]{:S(2)}, u32[]{:S(2)}) async-start(f32[16,1,128]{2,1,0:T(1,128)} %get-tuple-element.7), calls=%async_computation | async-start | bytes 16384 | tf_op jit(solution)/shard_map/all_to_all | solution.py:325
  21.4 0.0 copy-done.7
  21.4 0.0 copy-done.8
  21.4 0.6 add_select_fusion.6
  22.0 6.9 %all-to-all-done.sums = f32[16,1,128]{2,1,0:T(1,128)S(1)} async-done(((f32[16,1,128]{2,1,0:T(1,128)}), f32[16,1,128]{2,1,0:T(1,128)S(1)}, u32[]{:S(2)}, u32[]{:S(2)}) %all-to-all-start) | async-done | bytes 8224 | tf_op jit(solution)/shard_map/all_to_all | solution.py:325
  28.9 0.0 copy-start.4
  28.9 0.6 copy-done.4
  29.5 2.7 %shard_map.74 = f32[32,16,128]{2,1,0:T(8,128)} custom-call(f32[16,1,128]{2,1,0:T(1,128)} %copy-done.4, f32[3,2,48,128]{3,2,1,0:T(8,128)} %bitcast.27, f32[6,4,48,128]{3,2,1,0:T(8,128)} %get-tuple-element.8.tau, s32[1,512]{1,0:T(1,128)} %bitcast.30, s32[1,512]{1,0:T(1,128)} %bitcast.29), custom_call_target="tpu_custom_call" | custom-call | tf_op jit(solution)/shard_map/pallas_call | solution.py:327
  32.2 10.2 %all-to-all-start.1 = ((f32[32,16,128]{2,1,0:T(8,128)}), f32[32,16,128]{2,1,0:T(8,128)S(1)}, u32[]{:S(2)}, u32[]{:S(2)}) async-start(f32[32,16,128]{2,1,0:T(8,128)} %shard_map.74), calls=%async_computation.1 | async-start | bytes 524288 | tf_op jit(solution)/shard_map/all_to_all | solution.py:333
  42.4 1.3 %dynamic-slice_bitcast_fusion = (f32[4,128]{1,0:T(4,128)}, f32[4,128]{1,0:T(4,128)}) fusion(f32[16,4,128]{2,1,0:T(4,128)} %bitcast.31, s32[]{:T(128)S(6)} %select_n.50, f32[16,4,128]{2,1,0:T(4,128)} %bitcast.32), kind=kLoop, calls=%fused_computation.41 | loop fusion | bytes 8196 | tf_op jit(solution)/shard_map/jit(dynamic_index_in_dim)/squeeze | solution.py:320
  43.6 11.0 %all-to-all-done.1 = f32[32,16,128]{2,1,0:T(8,128)S(1)} async-done(((f32[32,16,128]{2,1,0:T(8,128)}), f32[32,16,128]{2,1,0:T(8,128)S(1)}, u32[]{:S(2)}, u32[]{:S(2)}) %all-to-all-start.1) | async-done | bytes 262176 | tf_op jit(solution)/shard_map/all_to_all | solution.py:333
  54.7 0.0 copy-start
  54.7 0.7 copy-done
  55.3 1.9 %shard_map.75 = f32[8,128,128]{2,1,0:T(8,128)} custom-call(f32[512,128]{1,0:T(8,128)} %bitcast.18, f32[4,128]{1,0:T(4,128)} %get-tuple-element.14.value, f32[4,128]{1,0:T(4,128)} %get-tuple-element.13.precision), custom_call_target="tpu_custom_call" | custom-call | tf_op jit(solution)/shard_map/pallas_call | solution.py:334
  57.2 0.0 copy-start.5
  57.2 0.0 copy-start.6
  57.2 0.0 copy-start.1
  57.2 20.0 %all_to_all.20 = f32[8,128,128]{2,1,0:T(8,128)S(1)} all-to-all(f32[8,128,128]{2,1,0:T(8,128)} %shard_map.75), channel_id=1, replica_groups={{0,2,4,6,8,10,12,14},{1,3,5,7,9,11,13,15},{16,18,20,22,24,26,28,30},{17..., dimensions={0} | all-to-all | bytes 1048576 | tf_op jit(solution)/shard_map/all_to_all | solution.py:336
  77.3 1.9 %collective-permute-start.2 = (f32[1024,128]{1,0:T(8,128)S(1)}, f32[1024,128]{1,0:T(8,128)S(1)}, u32[]{:S(2)}, u32[]{:S(2)}) collective-permute-start(f32[1024,128]{1,0:T(8,128)S(1)} %bitcast.20), channel_id=1, source_target_pairs={{0,1},{1,0},{2,3},{3,2},{4,5},{5,4},{6,7},{7,6},{8,9},{9,8},{10,11... | collective-permute-start | bytes 1572872 | tf_op jit(solution)/shard_map/ppermute | solution.py:338
  79.2 0.0 copy-done.5
  79.2 0.0 copy-done.6
  79.2 0.1 fusion.8
  79.3 1.8 %collective-permute-done.2.far = f32[1024,128]{1,0:T(8,128)S(1)} collective-permute-done((f32[1024,128]{1,0:T(8,128)S(1)}, f32[1024,128]{1,0:T(8,128)S(1)}, u32[]{:S(2)}, u32[]{:S(2)}) %collective-permute-start.2) | collective-permute-done | bytes 524320 | tf_op jit(solution)/shard_map/ppermute | solution.py:338
  81.1 0.0 copy-done.1
  81.1 11.9 %shard_map.76 = f32[512,128]{1,0:T(8,128)S(1)} custom-call(s32[4096]{0:T(1024)S(1)} %get-tuple-element.10.places, s32[32,128]{1,0:T(8,128)S(1)} %get-tuple-element.9.code, f32[1024,128]{1,0:T(8,128)S(1)} %bitcast.21, f32[1024,128]{1,0:T(8,128)S(1)} %collective-permute-done.2.far, f32[512,128]{1,0:T(8,128)S(1)} %bitcast.19), custom_call_target="tpu_custom_call" | custom-call | tf_op jit(solution)/shard_map/pallas_call | solution.py:339
  93.0 17.3 %all_to_all.21 = f32[32,16,128]{2,1,0:T(8,128)S(1)} all-to-all(f32[32,16,128]{2,1,0:T(8,128)S(1)} %bitcast.22), channel_id=1, replica_groups=mesh['member'=32,'space'=16] {'member'}, dimensions={0} | all-to-all | bytes 524288 | tf_op jit(solution)/shard_map/all_to_all | solution.py:346
  110.4 0.1 copy.12
  110.5 0.7 reshape.39
  (1 shorter events, 0.0 us)
Async XLA Ops:
  0.0 11.5 %collective-permute-start.1 = (f32[3,2,48,128]{3,2,1,0:T(8,128)}, f32[3,2,48,128]{3,2,1,0:T(8,128)S(1)}, u32[]{:S(2)}, u32[]{:S(2)}) collective-permute-start(f32[3,2,48,128]{3,2,1,0:T(8,128)} %bitcast.24), channel_id=1, source_target_pairs={{1,0},{2,1},{3,2},{4,3},{5,4},{6,5},{7,6},{8,7},{9,8},{10,9},{11,1... | collective-permute-start | bytes 442376 | tf_op jit(solution)/shard_map/ppermute | solution.py:323
  8.5 6.0 %collective-permute-start = (f32[3,2,48,128]{3,2,1,0:T(8,128)}, f32[3,2,48,128]{3,2,1,0:T(8,128)S(1)}, u32[]{:S(2)}, u32[]{:S(2)}) collective-permute-start(f32[3,2,48,128]{3,2,1,0:T(8,128)} %bitcast.25), channel_id=1, source_target_pairs={{0,1},{1,2},{2,3},{3,4},{4,5},{5,6},{6,7},{7,8},{8,9},{9,10},{10,1... | collective-permute-start | bytes 442376 | tf_op jit(solution)/shard_map/ppermute | solution.py:322
  11.5 3.0 %copy-start.2 = (f32[3,2,48,128]{3,2,1,0:T(8,128)}, f32[3,2,48,128]{3,2,1,0:T(8,128)S(1)}, u32[]{:S(2)}) copy-start(f32[3,2,48,128]{3,2,1,0:T(8,128)S(1)} %collective-permute-done.1.after) | copy-start | bytes 442372
  14.5 0.7 copy-start.3
  17.8 3.6 %copy-start.7 = (s32[512]{0:T(512)S(1)}, s32[512]{0:T(512)}, u32[]{:S(2)}) copy-start(s32[512]{0:T(512)} %param.8) | copy-start | bytes 6148
  17.8 3.6 %copy-start.8 = (s32[512]{0:T(512)S(1)}, s32[512]{0:T(512)}, u32[]{:S(2)}) copy-start(s32[512]{0:T(512)} %param.9) | copy-start | bytes 6148
  17.8 11.1 %all-to-all-start = ((f32[16,1,128]{2,1,0:T(1,128)}), f32[16,1,128]{2,1,0:T(1,128)S(1)}, u32[]{:S(2)}, u32[]{:S(2)}) async-start(f32[16,1,128]{2,1,0:T(1,128)} %get-tuple-element.7), calls=%async_computation | async-start | bytes 16384 | tf_op jit(solution)/shard_map/all_to_all | solution.py:325
  28.9 0.6 copy-start.4
  32.2 22.5 %all-to-all-start.1 = ((f32[32,16,128]{2,1,0:T(8,128)}), f32[32,16,128]{2,1,0:T(8,128)S(1)}, u32[]{:S(2)}, u32[]{:S(2)}) async-start(f32[32,16,128]{2,1,0:T(8,128)} %shard_map.74), calls=%async_computation.1 | async-start | bytes 524288 | tf_op jit(solution)/shard_map/all_to_all | solution.py:333
  54.7 0.7 copy-start
  57.2 22.0 %copy-start.5 = (s32[32,128]{1,0:T(8,128)S(1)}, s32[32,128]{1,0:T(8,128)}, u32[]{:S(2)}) copy-start(s32[32,128]{1,0:T(8,128)} %param.13) | copy-start | bytes 49156
  57.2 22.0 %copy-start.6 = (s32[32,128]{1,0:T(8,128)S(1)}, s32[32,128]{1,0:T(8,128)}, u32[]{:S(2)}) copy-start(s32[32,128]{1,0:T(8,128)} %param.12) | copy-start | bytes 49156
  57.2 23.8 %copy-start.1 = (f32[32,16,128]{2,1,0:T(8,128)S(1)}, f32[32,16,128]{2,1,0:T(8,128)}, u32[]{:S(2)}) copy-start(f32[32,16,128]{2,1,0:T(8,128)} %copy-done) | copy-start | bytes 786436
  77.3 3.8 %collective-permute-start.2 = (f32[1024,128]{1,0:T(8,128)S(1)}, f32[1024,128]{1,0:T(8,128)S(1)}, u32[]{:S(2)}, u32[]{:S(2)}) collective-permute-start(f32[1024,128]{1,0:T(8,128)S(1)} %bitcast.20), channel_id=1, source_target_pairs={{0,1},{1,0},{2,3},{3,2},{4,5},{5,4},{6,7},{7,6},{8,9},{9,8},{10,11... | collective-permute-start | bytes 1572872 | tf_op jit(solution)/shard_map/ppermute | solution.py:338

commit v2 on v1

--- a/solution.py
+++ b/solution.py
@@ -12,7 +12,9 @@
 K = 32
 LOC = 128
 CHUNKS = 32
-ROWS = 16
+ROWS = 41
+LINES = 21
+BACK = 9
 
 PAIRS = ((0, 0), (1, 1), (2, 2), (0, 1), (0, 2), (1, 2))
 F32 = jnp.float32
@@ -91,16 +93,48 @@
     return jnp.sqrt(2.0 * weighted([r * r for r in rate]))
 
 
-def model_kernel(before, own, after, sums, tau):
+def shifted_y(plane, step):
+    count = plane.shape[0]
+    row = iota(plane.shape, 0)
+    if step > 0:
+        return jnp.where(row == count - 1, 0.0, pltpu.roll(plane, count - 1, 0))
+    return jnp.where(row == 0, 0.0, pltpu.roll(plane, 1, 0))
+
+
+def model_kernel(before, own, after, place, lane, level, message, terms):
     fields = [
         {0: before[a, 0], 1: before[a, 1], 2: own[a, 0], 3: own[a, 1], 4: after[a, 0], 5: after[a, 1]}
         for a in range(3)
     ]
+    tau = [{} for _ in PAIRS]
     for p in range(1, 5):
         rate = strain(fields, p)
         size = magnitude(rate)
         for i in range(6):
-            tau[i, p - 1] = size * rate[i]
+            tau[i][p] = size * rate[i]
+    for a in range(3):
+        for x in range(2):
+            p = x + 2
+            start = a * 96 + x * 48
+            along = tau[pair_index(a, 0)]
+            flat = 0.5 * (along[p + 1] - along[p - 1]) + along_z(tau[pair_index(a, 2)][p])
+            upright = 0.25 * tau[pair_index(a, 1)][p]
+            terms[0, start : start + 48, :] = 0.5 * flat
+            terms[1, start : start + 48, :] = shifted_y(upright, 1)
+            terms[2, start : start + 48, :] = -shifted_y(upright, -1)
+    chosen = (iota((288, 512), 0) == place[...]).astype(F32).astype(BF16)
+    spot = iota((128, 512), 0) == lane[...]
+    lines = []
+    for f in range(4):
+        if f == 0:
+            pieces = split3(own[...].reshape(288, 128))
+        else:
+            pieces = split2(terms[f - 1])
+        picked = dot_t(pieces[-1], chosen)
+        for piece in pieces[-2::-1]:
+            picked = picked + dot_t(piece, chosen)
+        lines.append(jnp.sum(jnp.where(spot, picked, 0.0), axis=0, keepdims=True))
+    lines.append(level[...])
     smooth = [{p: filter_xz(f, p) for p in range(1, 5)} for f in fields]
     numer = 0.0
     denom = 0.0
@@ -111,8 +145,7 @@
         for i, (a, b) in enumerate(PAIRS):
             product = {q: fields[a][q] * fields[b][q] for q in (p - 1, p, p + 1)}
             leonard = filter_xz(product, p) - smooth[a][p] * smooth[b][p]
-            flux = {q: tau[i, q - 1] for q in (p - 1, p, p + 1)}
-            model = 2.0 * (filter_xz(flux, p) - 4.0 * size * rate[i])
+            model = 2.0 * (filter_xz(tau[i], p) - 4.0 * size * rate[i])
             top.append(leonard * model)
             bottom.append(model * model)
         numer = numer + weighted(top)
@@ -120,53 +153,67 @@
     pad = jnp.zeros((32, 128), F32)
     both = jnp.concatenate([numer, denom, pad], axis=0).T
     total = jnp.sum(both, axis=0, keepdims=True)
-    sums[...] = jnp.broadcast_to(total[None], sums.shape)
-
-
-def forecast_kernel(count, sums, own, tau, place, lane, send, state):
-    total = sums[0]
-    for i in range(1, sums.shape[0]):
-        total = total + sums[i]
+    rows = [line[:, q * 128 : (q + 1) * 128] for line in lines for q in range(4)]
+    block = jnp.concatenate(rows + [total], axis=0)
+    for i in range(message.shape[0] // LINES):
+        message[i * LINES : (i + 1) * LINES, :] = block
+
+
+def forecast_kernel(count, core, message, own, terms, send, state):
+    parts = message.shape[0] // LINES
+    total = jnp.sum(message[pl.ds(LINES - 1, parts, stride=LINES), :], axis=0, keepdims=True)
     denom = pltpu.roll(total, 128 - 48, 1)
     coeff = (total / count) / (denom / count + 1e-6)
-    coeff = 2.0 * jnp.broadcast_to(coeff, (128, 128)).T[:48]
-    stress = [[coeff * tau[i, p] for p in range(4)] for i in range(6)]
+    coeff = jnp.where(iota((1, 128), 1) < 48, coeff, 0.0)
+    column = jnp.broadcast_to(coeff, (128, 128)).T[:48]
+    upper = shifted_y(column, 1)
+    lower = shifted_y(column, -1)
     for a in range(3):
         for x in range(2):
-            p = x + 1
-            along = stress[pair_index(a, 0)]
-            term = 0.5 * (along[p + 1] - along[p - 1])
-            term = term + along_y(stress[pair_index(a, 1)][p])
-            term = term + along_z(stress[pair_index(a, 2)][p])
             start = a * 96 + x * 48
-            state[start : start + 48, :] = own[a, x] + 0.25 * term
-    values = state[...]
-    chosen = (iota((288, 512), 0) == place[...]).astype(F32).astype(BF16)
-    first, second, third = split3(values)
-    picked = (dot_t(third, chosen) + dot_t(second, chosen)) + dot_t(first, chosen)
-    picked = jnp.where(iota((128, 512), 0) == lane[...], picked, 0.0)
-    picked = jnp.sum(picked, axis=0, keepdims=True)
+            end = start + 48
+            change = column * terms[0, start:end, :]
+            change = change + (upper * terms[1, start:end, :] + lower * terms[2, start:end, :])
+            state[start:end, :] = own[a, x] + change
+    odd = core[0] == 1
+    flow, height = [], []
+
+    def lines(f):
+        pieces = []
+        for i in range(parts // 2):
+            even_at = 2 * i * LINES + 4 * f
+            odd_at = even_at + LINES
+            pieces.append(jnp.where(odd, message[odd_at : odd_at + 4, :], message[even_at : even_at + 4, :]))
+        return jnp.concatenate(pieces, axis=0)
+
+    height = lines(4).astype(jnp.int32)
+    table = jnp.broadcast_to(coeff, height.shape)
+
+    def look(where):
+        where = jnp.clip(where, 0, 127)
+        return jnp.take_along_axis(table, where, axis=1)
+
+    seen = lines(0) + look(height) * lines(1)
+    seen = seen + (look(height + 1) * lines(2) + look(height - 1) * lines(3))
     for m in range(K):
+        base = m * ROWS
         for a in range(3):
-            send[m, 3 * a : 3 * a + 3, :] = state[a * 96 + 3 * m : a * 96 + 3 * m + 3, :]
-    for q in range(4):
-        piece = picked[:, q * 128 : (q + 1) * 128]
-        send[:, 9 + q, :] = jnp.broadcast_to(piece, (K, 128))
-    send[:, 13:16, :] = jnp.zeros((K, 3, 128), F32)
+            send[base + 3 * a : base + 3 * a + 3, :] = state[a * 96 + 3 * m : a * 96 + 3 * m + 3, :]
+        send[base + 9 : base + ROWS, :] = seen
 
 
 def table_kernel(received, value, precision, table):
     member = iota((K, 128), 0)
-    parts = []
-    for q in range(4):
-        seen = received[pl.ds(9 + q, K, stride=ROWS), :]
-        mean = jnp.sum(seen, axis=0, keepdims=True) * (1.0 / K)
-        innov = value[q : q + 1, :] - mean
-        root = jnp.sqrt(precision[q : q + 1, :])
-        parts.append(jnp.where(member == K - 1, innov, seen - mean) * root)
-    block = jnp.concatenate(parts, axis=0).T
-    for i in range(table.shape[0]):
-        table[i] = block
+    for i in range(8):
+        parts = []
+        for q in range(4):
+            r = 4 * i + q
+            seen = received[pl.ds(9 + r, K, stride=ROWS), :]
+            mean = jnp.sum(seen, axis=0, keepdims=True) * (1.0 / K)
+            innov = value[r : r + 1, :] - mean
+            root = jnp.sqrt(precision[r : r + 1, :])
+            parts.append(jnp.where(member == K - 1, innov, seen - mean) * root)
+        table[i * 128 : (i + 1) * 128, :] = jnp.concatenate(parts, axis=0).T
 
 
 def block_diagonal(value, mask):
@@ -285,12 +332,17 @@
         total = part if total is None else total + part
     moved = total[:K] + total[K : K + 1]
     for r in range(9):
-        out[pl.ds(r, K, stride=ROWS), :] = moved[:, r * 128 : (r + 1) * 128] + centres[r]
-    for r in range(9, ROWS):
-        out[pl.ds(r, K, stride=ROWS), :] = jnp.zeros((K, 128), F32)
-
-
-def call(kernel, shapes, ins, scratch=(), limit=None):
+        out[pl.ds(r, K, stride=BACK), :] = moved[:, r * 128 : (r + 1) * 128] + centres[r]
+
+
+def order_kernel(returned, out):
+    for m in range(K):
+        x, y = m // 16, 3 * (m % 16)
+        for a in range(3):
+            out[a, x, y : y + 3, :] = returned[m * BACK + 3 * a : m * BACK + 3 * a + 3, :]
+
+
+def call(kernel, shapes, ins, scratch=(), limit=24 * 2**20):
     return pl.pallas_call(
         kernel,
         out_shape=[jax.ShapeDtypeStruct(s, F32) for s in shapes],
@@ -301,6 +353,12 @@
     )
 
 
+def exchange(rows, axis, count):
+    width = rows.size // count
+    sent = lax.all_to_all(rows.reshape(count, 1, width), axis, 0, 0, tiled=True)
+    return sent.reshape(rows.shape)
+
+
 def shards(ensemble, obs_cell, obs_comp, obs_value, obs_precision, loc_obs, loc_level):
     field = ensemble[0]
     _, depth, height, extent = field.shape
@@ -316,37 +374,38 @@
     code = (within // 128) * 16 + loc_level
     place = (obs_comp * (depth * height) + obs_cell // extent).reshape(1, 512)
     lane = (obs_cell % extent).reshape(1, 512)
-    value = lax.dynamic_index_in_dim(obs_value.reshape(parts, 4, 128), here, 0, keepdims=False)
-    precision = lax.dynamic_index_in_dim(obs_precision.reshape(parts, 4, 128), here, 0, keepdims=False)
+    level = ((obs_cell // extent) % height).astype(F32).reshape(1, 512)
+    core = here & 1
+    value = lax.dynamic_index_in_dim(obs_value.reshape(parts // 2, 2, 4, 128), core, 1, keepdims=False)
+    value = value.reshape(K, 128)
+    precision = lax.dynamic_index_in_dim(obs_precision.reshape(parts // 2, 2, 4, 128), core, 1, keepdims=False)
+    precision = precision.reshape(K, 128)
 
     before = lax.ppermute(field, "space", up)
     after = lax.ppermute(field, "space", down)
-    sums, tau = call(model_kernel, [(parts, 1, 128), (6, 4, height, extent)], [VMEM] * 3)(before, field, after)
-    sums = lax.all_to_all(sums, "space", 0, 0, tiled=True)
-    count = depth * parts * extent
+    message, terms = call(
+        model_kernel, [(parts * LINES, 128), (3, 3 * depth * height, extent)], [VMEM] * 6
+    )(before, field, after, place, lane, level)
+    message = exchange(message, "space", parts)
     (send,) = call(
-        functools.partial(forecast_kernel, count),
-        [(K, ROWS, 128)],
-        [VMEM] * 5,
+        functools.partial(forecast_kernel, depth * parts * extent),
+        [(K * ROWS, 128)],
+        [SMEM] + [VMEM] * 3,
         [pltpu.VMEM((3 * depth * height, extent), F32)],
-    )(sums, field, tau, place, lane)
-    received = lax.all_to_all(send, "member", 0, 0, tiled=True).reshape(K * ROWS, 128)
-    (table,) = call(table_kernel, [(parts // 2, 128, 128)], [VMEM] * 3)(received, value, precision)
-    same_core = [[2 * i + c for i in range(parts // 2)] for c in range(2)]
-    near = lax.all_to_all(table, "space", 0, 0, axis_index_groups=same_core, tiled=True)
-    near = near.reshape(parts * 64, 128)
+    )(core.reshape(1), message, field, terms)
+    received = exchange(send, "member", K)
+    (near,) = call(table_kernel, [(parts * 64, 128)], [VMEM] * 3)(received, value, precision)
     far = lax.ppermute(near, "space", [(i, i ^ 1) for i in range(parts)])
     (result,) = call(
         analysis_kernel,
-        [(K * ROWS, 128)],
+        [(K * BACK, 128)],
         [SMEM] + [VMEM] * 4,
         [pltpu.VMEM((2048, 128), F32), pltpu.VMEM((CHUNKS * LOC, 128), F32)],
         limit=40 * 2**20,
     )(places, code, near, far, received)
-    returned = lax.all_to_all(result.reshape(K, ROWS, 128), "member", 0, 0, tiled=True)
-    returned = returned[:, :9].reshape(K, 3, 3, 128)
-    returned = jnp.transpose(returned, (1, 0, 2, 3))
-    return returned.reshape(1, 3, depth, height, extent)
+    returned = exchange(result, "member", K)
+    (result,) = call(order_kernel, [(3, depth, height, extent)], [VMEM])(returned)
+    return result[None]
 
 
 def solution(mesh):

time: 112 us -> 96.1 us (0.86)
  blocking collectives: 37.4 us -> 15.4 us
  waiting for transfers between devices: 25.7 us -> 38 us
  local copies, waits for them, and re-layouts: 4.14 us -> 0.94 us
  Pallas kernels: 19.2 us -> 16.1 us
    all_to_all x2 -> x1, blocking collectives: 37.4 us -> 15.4 us  [exchange(): sent = lax.all_to_all(rows.reshape(count, 1, width), axis, 0, 0, tiled=True)]
    all_to_all x2, waiting for transfers between devices: 17.9 us -> 30.9 us  [exchange(): sent = lax.all_to_all(rows.reshape(count, 1, width), axis, 0, 0, tiled=True)]
    pallas_call x4 -> x5, Pallas kernels: 19.2 us -> 16.1 us  [the longest x1 11.9 us: shards(): call(analysis_kernel, [(K * BACK, 128)], [SMEM] + [VMEM] * 4, [pltpu.VMEM...]
    squeeze x1 -> x0, local copies, waits for them, and re-layouts: 1.28 us -> none  [shards(): lax.dynamic_index_in_dim(obs_precision.reshape(parts, 4, 128), here, 0, k...]
  transfers between devices with their start and end apart: 5 -> 5, of which waited for: 5 -> 5; matrix products, arithmetic and copies ran while one was open for 2% -> 1% of each run, Pallas kernels for 0% -> 0%
where the time goes in v2:
time: 96.1 us; the launch traced here: 95.7 us
  waiting for transfers between devices  38 us (40%)
  starting transfers between devices  24.3 us (25%)
  Pallas kernels  16.1 us (17%)
  blocking collectives  15.4 us (16%)
    all_to_all x2, waiting for transfers between devices, exchange(): sent = lax.all_to_all(rows.reshape(count, 1, width), axis, 0, 0, tiled=True)  30.9 us
    all_to_all x1, blocking collectives, exchange(): sent = lax.all_to_all(rows.reshape(count, 1, width), axis, 0, 0, tiled=True)  15.4 us
    all_to_all x2, starting transfers between devices, exchange(): sent = lax.all_to_all(rows.reshape(count, 1, width), axis, 0, 0, tiled=True)  13.9 us
    pallas_call x1, Pallas kernels, shards(): call(analysis_kernel, [(K * BACK, 128)], [SMEM] + [VMEM] * 4, [pltpu.VMEM...  11.9 us
    ppermute x1, starting transfers between devices, shards(): after = lax.ppermute(field, 'space', down)  8.48 us
    ppermute x1, waiting for transfers between devices, shards(): before = lax.ppermute(field, 'space', up)  3 us
    ppermute x1, waiting for transfers between devices, shards(): after = lax.ppermute(field, 'space', down)  2.27 us
    pallas_call x1, Pallas kernels, shards(): call(model_kernel, [(parts * LINES, 128), (3, 3 * depth * height, extent)...  2.26 us
  transfers between devices with their start and end apart: 5, of which 5 were waited for; matrix products, arithmetic and copies ran while one was open for 1% of the time, Pallas kernels for 0%

profile of v2, /device:TPU:8, one launch (start us, length us, event | category | flops | bytes accessed | tf_op | source)
XLA Modules:
  0.0 95.7 jit_solution(3729715556177080141)
XLA Ops:
  0.0 8.5 %collective-permute-start.1 = (f32[3,2,48,128]{3,2,1,0:T(8,128)}, f32[3,2,48,128]{3,2,1,0:T(8,128)S(1)}, u32[]{:S(2)}, u32[]{:S(2)}) collective-permute-start(f32[3,2,48,128]{3,2,1,0:T(8,128)} %bitcast.21), channel_id=1, source_target_pairs={{1,0},{2,1},{3,2},{4,3},{5,4},{6,5},{7,6},{8,7},{9,8},{10,9},{11,1... | collective-permute-start | bytes 442376 | tf_op jit(solution)/shard_map/ppermute | solution.py:385
  8.5 0.0 collective-permute-start
  8.5 0.7 fusion.15
  9.2 2.3 %collective-permute-done.1.after = f32[3,2,48,128]{3,2,1,0:T(8,128)S(1)} collective-permute-done((f32[3,2,48,128]{3,2,1,0:T(8,128)}, f32[3,2,48,128]{3,2,1,0:T(8,128)S(1)}, u32[]{:S(2)}, u32[]{:S(2)}) %collective-permute-start.1) | collective-permute-done | bytes 147488 | tf_op jit(solution)/shard_map/ppermute | solution.py:385
  11.5 3.0 %collective-permute-done.before = f32[3,2,48,128]{3,2,1,0:T(8,128)S(1)} collective-permute-done((f32[3,2,48,128]{3,2,1,0:T(8,128)}, f32[3,2,48,128]{3,2,1,0:T(8,128)S(1)}, u32[]{:S(2)}, u32[]{:S(2)}) %collective-permute-start) | collective-permute-done | bytes 147488 | tf_op jit(solution)/shard_map/ppermute | solution.py:384
  14.5 0.0 copy-start
  14.5 0.9 copy-done
  15.4 2.3 %shard_map.73 = (f32[336,128]{1,0:T(8,128)}, f32[3,288,128]{2,1,0:T(8,128)S(1)}) custom-call(f32[3,2,48,128]{3,2,1,0:T(8,128)S(1)} %collective-permute-done.before, f32[3,2,48,128]{3,2,1,0:T(8,128)S(1)} %bitcast.23, f32[3,2,48,128]{3,2,1,0:T(8,128)S(1)} %collective-permute-done.1.after, s32[1,512]{1,0:T(1,128)S(1)} %bitcast.31, s32[1,512]{1,0:T(1,128)S(1)} %bitcast.30, ...), custom_call_target="tpu_custom_call" | custom-call | tf_op jit(solution)/shard_map/pallas_call | solution.py:386
  17.6 0.0 copy-start.1
  17.6 3.6 %all-to-all-start = ((f32[16,1,2688]{2,1,0:T(1,128)}), f32[16,1,2688]{2,1,0:T(1,128)S(1)}, u32[]{:S(2)}, u32[]{:S(2)}) async-start(f32[16,1,2688]{2,1,0:T(1,128)} %bitcast.6), calls=%async_computation | async-start | bytes 344064 | tf_op jit(solution)/shard_map/all_to_all | solution.py:358
  21.3 9.3 %all-to-all-done = f32[16,1,2688]{2,1,0:T(1,128)S(1)} async-done(((f32[16,1,2688]{2,1,0:T(1,128)}), f32[16,1,2688]{2,1,0:T(1,128)S(1)}, u32[]{:S(2)}, u32[]{:S(2)}) %all-to-all-start) | async-done | bytes 172064 | tf_op jit(solution)/shard_map/all_to_all | solution.py:358
  30.6 0.0 copy-done.1
  30.6 1.1 %shard_map.74 = f32[1312,128]{1,0:T(8,128)} custom-call(s32[1]{0:T(128)} %bitcast.1.core, f32[336,128]{1,0:T(8,128)S(1)} %bitcast.20, f32[3,2,48,128]{3,2,1,0:T(8,128)S(1)} %bitcast.24, f32[3,288,128]{2,1,0:T(8,128)S(1)} %get-tuple-element.8.terms), custom_call_target="tpu_custom_call" | custom-call | tf_op jit(solution)/shard_map/pallas_call | solution.py:390
  31.7 0.0 copy-start.4
  31.7 0.0 copy-start.5
  31.7 10.3 %all-to-all-start.1 = ((f32[32,1,5248]{2,1,0:T(1,128)}), f32[32,1,5248]{2,1,0:T(1,128)S(1)}, u32[]{:S(2)}, u32[]{:S(2)}) async-start(f32[32,1,5248]{2,1,0:T(1,128)} %bitcast.8), calls=%async_computation.1 | async-start | bytes 1343488 | tf_op jit(solution)/shard_map/all_to_all | solution.py:358
  42.0 0.0 copy-done.4
  42.0 0.0 copy-done.5
  42.0 21.6 %all-to-all-done.1 = f32[32,1,5248]{2,1,0:T(1,128)S(1)} async-done(((f32[32,1,5248]{2,1,0:T(1,128)}), f32[32,1,5248]{2,1,0:T(1,128)S(1)}, u32[]{:S(2)}, u32[]{:S(2)}) %all-to-all-start.1) | async-done | bytes 671776 | tf_op jit(solution)/shard_map/all_to_all | solution.py:358
  63.7 0.0 copy-start.2
  63.7 0.0 copy-start.3
  63.7 0.2 shard_map.75.near
  63.9 1.9 %collective-permute-start.2 = (f32[1024,128]{1,0:T(8,128)S(1)}, f32[1024,128]{1,0:T(8,128)S(1)}, u32[]{:S(2)}, u32[]{:S(2)}) collective-permute-start(f32[1024,128]{1,0:T(8,128)S(1)} %shard_map.75.near), channel_id=1, source_target_pairs={{0,1},{1,0},{2,3},{3,2},{4,5},{5,4},{6,7},{7,6},{8,9},{9,8},{10,11... | collective-permute-start | bytes 1572872 | tf_op jit(solution)/shard_map/ppermute | solution.py:398
  65.8 0.0 copy-done.2
  65.8 0.0 copy-done.3
  65.8 0.1 fusion.8
  65.9 1.8 %collective-permute-done.2.far = f32[1024,128]{1,0:T(8,128)S(1)} collective-permute-done((f32[1024,128]{1,0:T(8,128)S(1)}, f32[1024,128]{1,0:T(8,128)S(1)}, u32[]{:S(2)}, u32[]{:S(2)}) %collective-permute-start.2) | collective-permute-done | bytes 524320 | tf_op jit(solution)/shard_map/ppermute | solution.py:398
  67.7 11.9 %shard_map.76 = f32[288,128]{1,0:T(8,128)S(1)} custom-call(s32[4096]{0:T(1024)S(1)} %get-tuple-element.10.places, s32[32,128]{1,0:T(8,128)S(1)} %get-tuple-element.9.code, f32[1024,128]{1,0:T(8,128)S(1)} %shard_map.75.near, f32[1024,128]{1,0:T(8,128)S(1)} %collective-permute-done.2.far, f32[1312,128]{1,0:T(8,128)S(1)} %bitcast.19), custom_call_target="tpu_custom_call" | custom-call | tf_op jit(solution)/shard_map/pallas_call | solution.py:399
  79.5 15.4 %all_to_all.15 = f32[32,1,1152]{2,1,0:T(1,128)S(1)} all-to-all(f32[32,1,1152]{2,1,0:T(1,128)S(1)} %bitcast.26), channel_id=1, replica_groups=mesh['member'=32,'space'=16] {'member'}, dimensions={0} | all-to-all | bytes 294912 | tf_op jit(solution)/shard_map/all_to_all | solution.py:358
  95.0 0.7 shard_map.77
  (1 shorter events, 0.0 us)
Async XLA Ops:
  0.0 11.5 %collective-permute-start.1 = (f32[3,2,48,128]{3,2,1,0:T(8,128)}, f32[3,2,48,128]{3,2,1,0:T(8,128)S(1)}, u32[]{:S(2)}, u32[]{:S(2)}) collective-permute-start(f32[3,2,48,128]{3,2,1,0:T(8,128)} %bitcast.21), channel_id=1, source_target_pairs={{1,0},{2,1},{3,2},{4,3},{5,4},{6,5},{7,6},{8,7},{9,8},{10,9},{11,1... | collective-permute-start | bytes 442376 | tf_op jit(solution)/shard_map/ppermute | solution.py:385
  8.5 6.0 %collective-permute-start = (f32[3,2,48,128]{3,2,1,0:T(8,128)}, f32[3,2,48,128]{3,2,1,0:T(8,128)S(1)}, u32[]{:S(2)}, u32[]{:S(2)}) collective-permute-start(f32[3,2,48,128]{3,2,1,0:T(8,128)} %bitcast.22), channel_id=1, source_target_pairs={{0,1},{1,2},{2,3},{3,4},{4,5},{5,6},{6,7},{7,8},{8,9},{9,10},{10,1... | collective-permute-start | bytes 442376 | tf_op jit(solution)/shard_map/ppermute | solution.py:384
  14.5 0.9 copy-start
  17.6 12.9 %copy-start.1 = (f32[1,3,2,48,128]{4,3,2,1,0:T(8,128)S(1)}, f32[1,3,2,48,128]{4,3,2,1,0:T(8,128)}, u32[]{:S(2)}) copy-start(f32[1,3,2,48,128]{4,3,2,1,0:T(8,128)} %param.7) | copy-start | bytes 442372
  17.6 12.9 %all-to-all-start = ((f32[16,1,2688]{2,1,0:T(1,128)}), f32[16,1,2688]{2,1,0:T(1,128)S(1)}, u32[]{:S(2)}, u32[]{:S(2)}) async-start(f32[16,1,2688]{2,1,0:T(1,128)} %bitcast.6), calls=%async_computation | async-start | bytes 344064 | tf_op jit(solution)/shard_map/all_to_all | solution.py:358
  31.7 10.3 %copy-start.4 = (f32[8192]{0:T(1024)S(1)}, f32[8192]{0:T(1024)}, u32[]{:S(2)}) copy-start(f32[8192]{0:T(1024)} %param.11) | copy-start | bytes 98308
  31.7 10.3 %copy-start.5 = (f32[8192]{0:T(1024)S(1)}, f32[8192]{0:T(1024)}, u32[]{:S(2)}) copy-start(f32[8192]{0:T(1024)} %param.10) | copy-start | bytes 98308
  31.7 32.0 %all-to-all-start.1 = ((f32[32,1,5248]{2,1,0:T(1,128)}), f32[32,1,5248]{2,1,0:T(1,128)S(1)}, u32[]{:S(2)}, u32[]{:S(2)}) async-start(f32[32,1,5248]{2,1,0:T(1,128)} %bitcast.8), calls=%async_computation.1 | async-start | bytes 1343488 | tf_op jit(solution)/shard_map/all_to_all | solution.py:358
  63.7 2.2 %copy-start.2 = (s32[32,128]{1,0:T(8,128)S(1)}, s32[32,128]{1,0:T(8,128)}, u32[]{:S(2)}) copy-start(s32[32,128]{1,0:T(8,128)} %param.13) | copy-start | bytes 49156
  63.7 2.2 %copy-start.3 = (s32[32,128]{1,0:T(8,128)S(1)}, s32[32,128]{1,0:T(8,128)}, u32[]{:S(2)}) copy-start(s32[32,128]{1,0:T(8,128)} %param.12) | copy-start | bytes 49156
  63.9 3.8 %collective-permute-start.2 = (f32[1024,128]{1,0:T(8,128)S(1)}, f32[1024,128]{1,0:T(8,128)S(1)}, u32[]{:S(2)}, u32[]{:S(2)}) collective-permute-start(f32[1024,128]{1,0:T(8,128)S(1)} %shard_map.75.near), channel_id=1, source_target_pairs={{0,1},{1,0},{2,3},{3,2},{4,5},{5,4},{6,7},{7,6},{8,9},{9,8},{10,11... | collective-permute-start | bytes 1572872 | tf_op jit(solution)/shard_map/ppermute | solution.py:398

commit v3 on v2

--- a/solution.py
+++ b/solution.py
@@ -13,7 +13,7 @@
 LOC = 128
 CHUNKS = 32
 ROWS = 41
-LINES = 21
+LINES = 24
 BACK = 9
 
 PAIRS = ((0, 0), (1, 1), (2, 2), (0, 1), (0, 2), (1, 2))
@@ -154,14 +154,14 @@
     both = jnp.concatenate([numer, denom, pad], axis=0).T
     total = jnp.sum(both, axis=0, keepdims=True)
     rows = [line[:, q * 128 : (q + 1) * 128] for line in lines for q in range(4)]
-    block = jnp.concatenate(rows + [total], axis=0)
+    block = jnp.concatenate(rows + [total, jnp.zeros((3, 128), F32)], axis=0)
     for i in range(message.shape[0] // LINES):
         message[i * LINES : (i + 1) * LINES, :] = block
 
 
 def forecast_kernel(count, core, message, own, terms, send, state):
     parts = message.shape[0] // LINES
-    total = jnp.sum(message[pl.ds(LINES - 1, parts, stride=LINES), :], axis=0, keepdims=True)
+    total = jnp.sum(message[pl.ds(20, parts, stride=LINES), :], axis=0, keepdims=True)
     denom = pltpu.roll(total, 128 - 48, 1)
     coeff = (total / count) / (denom / count + 1e-6)
     coeff = jnp.where(iota((1, 128), 1) < 48, coeff, 0.0)
@@ -234,44 +234,84 @@
     return (wide[2 * rows :] + wide[rows : 2 * rows]) + wide[:rows]
 
 
-def analysis_kernel(places, code, near, far, received, out, table, picked):
+def copy_kernel(source, target):
+    pltpu.sync_copy(source, target)
+
+
+def weight_kernel(code, weights):
+    columns = jnp.concatenate([code[...], jnp.zeros((96, 128), jnp.int32)], axis=0).T
+    quarter = iota((LOC, 128), 1) // 32
+    for c in range(CHUNKS):
+        mark = jnp.broadcast_to(columns[:, c : c + 1], (LOC, 128))
+        level = jnp.sqrt((mark & 15).astype(F32) * (1.0 / LEVELS))
+        weights[c * LOC : (c + 1) * LOC, :] = jnp.where((mark >> 4) == quarter, level, 0.0)
+
+
+def spread_kernel(received, tiles, centres):
+    cells = [received[pl.ds(r, K, stride=ROWS), :] for r in range(9)]
+    means = [jnp.sum(v, axis=0, keepdims=True) * (1.0 / K) for v in cells]
+    centres[...] = jnp.concatenate(means, axis=0)
+    spreads = [v - m for v, m in zip(cells, means)]
+    owner = iota((256, 288), 0) // 32
+    chunk = (iota((256, 288), 1) % 32) // 4
+    here = jnp.where(chunk == owner, 1.0, 0.0).astype(BF16)
+    for g in range(4):
+        packed = jnp.concatenate([v[:, 32 * g : 32 * g + 32] for v in spreads], axis=1)
+        h1, h2 = split2(packed)
+        tiles[g, :, 0:288] = block_diagonal(h1, here)
+        tiles[g, :, 288:576] = block_diagonal(h2, here)
+
+
+def folded(rows, weights):
+    lone = rows * weights
+    lone = lone + pltpu.roll(lone, 64, 1)
+    return lone + pltpu.roll(lone, 32, 1)
+
+
+def four_gram(pack):
+    quarter = iota((LOC, 128), 1) // 32
+    high, low = split2(pack)
+    blocks = [jnp.where(quarter == i, 1.0, 0.0).astype(BF16) for i in range(4)]
+    right1 = jnp.concatenate([high * b for b in blocks], axis=0)
+    right2 = jnp.concatenate([low * b for b in blocks], axis=0)
+    turned = pack.T
+    turned = jnp.concatenate([turned[32 * i : 32 * i + 32] for i in range(4)], axis=1)
+    left1, left2 = split2(turned)
+    wide = dot(jnp.concatenate([left1, left2], axis=0), right1)
+    return (wide[K:] + dot(left1, right2)) + wide[:K]
+
+
+def analysis_kernel(places, weights, near, far, tiles, centres, out, table, first, second, grams):
     table[0:1024, :] = near[...]
     table[1024:2048, :] = far[...]
 
-    def fetch(c, carry):
-        base = pl.multiple_of(c * LOC, LOC)
-        target = picked.at[pl.ds(base, LOC)]
+    quarter = iota((LOC, 128), 1) // 32
+
+    def fetch(c, target, at):
+        base = c * LOC
         for j in range(LOC):
-            target[pl.ds(j, 1), :] = table[pl.ds(places[base + j], 1), :]
+            target[at + j : at + j + 1, :] = table[pl.ds(places[base + j], 1), :]
+
+    def half(four, source, target):
+        coming = jnp.minimum(4 * four + 4, CHUNKS - 4)
+        pack = None
+        for i in range(4):
+            fetch(coming + i, target, i * LOC)
+            at = pl.multiple_of(four * (4 * LOC) + i * LOC, LOC)
+            lone = folded(source[i * LOC : (i + 1) * LOC, :], weights[pl.ds(at, LOC), :])
+            pack = lone if i == 0 else jnp.where(quarter == i, lone, pack)
+        grams[four] = four_gram(pack)
+
+    for i in range(4):
+        fetch(i, first, i * LOC)
+
+    def step(i, carry):
+        half(2 * i, first, second)
+        half(2 * i + 1, second, first)
         return carry
 
-    lax.fori_loop(0, CHUNKS, fetch, 0)
-
-    columns = jnp.concatenate([code[...], jnp.zeros((96, 128), jnp.int32)], axis=0).T
-    quarter = iota((LOC, 128), 1) // 32
-    small_quarter = iota((K, 128), 1) // 32
-    grams = []
-    for c in range(CHUNKS):
-        rows = picked[c * LOC : (c + 1) * LOC, :]
-        mark = jnp.broadcast_to(columns[:, c : c + 1], (LOC, 128))
-        level = (mark & 15).astype(F32) * (1.0 / LEVELS)
-        weight = jnp.where((mark >> 4) == quarter, level, 0.0)
-        g1, g2 = split2(rows)
-        a1, a2 = split2(weight * rows)
-        wide = dot_t(a1, jnp.concatenate([g1, g2], axis=1))
-        full = wide[:, :128] + wide[:, 128:] + dot_t(a2, g1)
-        fold = full[0:32]
-        for q in range(1, 4):
-            fold = jnp.where(small_quarter == q, full[32 * q : 32 * q + 32], fold)
-        fold = fold + pltpu.roll(fold, 64, 1)
-        fold = fold + pltpu.roll(fold, 32, 1)
-        if c % 4 == 0:
-            held = fold
-        else:
-            held = jnp.where(small_quarter == c % 4, fold, held)
-        if c % 4 == 3:
-            grams.append(held)
-    grams = [jnp.concatenate(grams[2 * g : 2 * g + 2], axis=1) for g in range(4)]
+    lax.fori_loop(0, 4, step, 0)
+    packs = [jnp.concatenate([grams[2 * g], grams[2 * g + 1]], axis=1) for g in range(4)]
 
     tall = iota((256, 256), 0)
     wide_lane = iota((256, 256), 1)
@@ -284,17 +324,17 @@
     member = iota((K, 256), 0)
     eye = jnp.where(member == iota((K, 256), 1) % 32, 1.0, 0.0)
 
-    count = len(grams)
+    count = len(packs)
     drive, scale, y, z = [], [], [], []
     for g in range(count):
-        gram = grams[g]
-        body = jnp.where(member == K - 1, 0.0, gram)
+        pack = packs[g]
+        body = jnp.where(member == K - 1, 0.0, pack)
         body = jnp.where(member == K - 1, -jnp.sum(body, axis=0, keepdims=True), body)
-        push = jnp.broadcast_to(gram[K - 1 : K, :], (8, 256))
+        push = jnp.broadcast_to(pack[K - 1 : K, :], (16, 256))
         whole = exact_times(jnp.concatenate([body, push], axis=0), rebuild)
         matrix = whole[:K] + ((K - 1) / 1.1) * eye
         drive.append(whole[K:])
-        square = jnp.broadcast_to(jnp.sum(matrix * matrix, axis=0, keepdims=True), (8, 256))
+        square = jnp.broadcast_to(jnp.sum(matrix * matrix, axis=0, keepdims=True), (16, 256))
         norm = jnp.sqrt(exact_times(square, mask))
         scale.append(norm)
         y.append(matrix / norm[0:1])
@@ -302,37 +342,37 @@
         for g in range(count):
             if sweep == 0:
                 factor = 1.5 * eye - 0.5 * y[g]
-                z[g:] = [factor]
-                y[g] = times_blocks(y[g], factor, mask)
+                both = times_blocks(jnp.concatenate([y[g], drive[g]], axis=0), factor, mask)
+                y[g], drive[g] = both[:K], both[K:]
+                z.append(factor)
                 continue
             factor = 1.5 * eye - 0.5 * times_blocks(z[g], y[g], mask)
             if sweep == NS_ITERS - 1:
-                z[g] = times_blocks(z[g], factor, mask)
+                both = times_blocks(jnp.concatenate([z[g], drive[g]], axis=0), factor, mask)
+                z[g], drive[g] = both[:K], both[K:]
             else:
-                both = times_blocks(jnp.concatenate([y[g], z[g]], axis=0), factor, mask)
-                y[g], z[g] = both[:K], both[K:]
-    total = None
-    cells = [received[pl.ds(r, K, stride=ROWS), :] for r in range(9)]
-    centres = [jnp.sum(v, axis=0, keepdims=True) * (1.0 / K) for v in cells]
-    spreads = [v - m for v, m in zip(cells, centres)]
-    spreads = jnp.concatenate(spreads, axis=1)
-    h1, h2 = split2(spreads)
-    owner = iota((256, 9 * 128), 0) // 32
-    chunk = (iota((256, 9 * 128), 1) % 128) // 4
+                both = times_blocks(jnp.concatenate([y[g], z[g], drive[g]], axis=0), factor, mask)
+                y[g], z[g], drive[g] = both[:K], both[K : 2 * K], both[2 * K :]
+    moved = []
     for g in range(count):
-        pull = times_blocks(times_blocks(drive[g], z[g], mask), z[g], mask) / scale[g]
+        pull = times_blocks(drive[g], z[g], mask) / scale[g]
         root = z[g] * (jnp.sqrt(float(K - 1)) / jnp.sqrt(scale[g][0:1]))
         left1, left2 = split2(jnp.concatenate([root, pull], axis=0))
-        here = jnp.where(chunk == owner + 8 * g, 1.0, 0.0).astype(BF16)
-        right1 = block_diagonal(h1, here)
-        right2 = block_diagonal(h2, here)
         rows = left1.shape[0]
-        part = dot(jnp.concatenate([left1, left2], axis=0), right1)
-        part = part[:rows] + part[rows:] + dot(left1, right2)
-        total = part if total is None else total + part
-    moved = total[:K] + total[K : K + 1]
+        part = dot(jnp.concatenate([left1, left2], axis=0), tiles[g])
+        part = part[:rows, :288] + part[rows:, :288] + part[:rows, 288:]
+        moved.append(part[:K] + part[K : K + 1])
     for r in range(9):
-        out[pl.ds(r, K, stride=BACK), :] = moved[:, r * 128 : (r + 1) * 128] + centres[r]
+        row = jnp.concatenate([part[:, 32 * r : 32 * r + 32] for part in moved], axis=1)
+        out[pl.ds(r, K, stride=BACK), :] = row + centres[r : r + 1, :]
+
+
+SCRATCH = [
+    pltpu.VMEM((2048, 128), F32),
+    pltpu.VMEM((4 * LOC, 128), F32),
+    pltpu.VMEM((4 * LOC, 128), F32),
+    pltpu.VMEM((CHUNKS // 4, K, 128), F32),
+]
 
 
 def order_kernel(returned, out):
@@ -342,10 +382,10 @@
             out[a, x, y : y + 3, :] = returned[m * BACK + 3 * a : m * BACK + 3 * a + 3, :]
 
 
-def call(kernel, shapes, ins, scratch=(), limit=24 * 2**20):
+def call(kernel, shapes, ins, scratch=(), limit=24 * 2**20, kinds=None):
     return pl.pallas_call(
         kernel,
-        out_shape=[jax.ShapeDtypeStruct(s, F32) for s in shapes],
+        out_shape=[jax.ShapeDtypeStruct(s, t) for s, t in zip(shapes, kinds or [F32] * len(shapes))],
         in_specs=ins,
         out_specs=[VMEM] * len(shapes),
         scratch_shapes=list(scratch),
@@ -372,6 +412,7 @@
     places = (slab // 2) * 128 + ((slab + here) % 2) * 1024 + within % 128
     places = places.reshape(CHUNKS * LOC)
     code = (within // 128) * 16 + loc_level
+    (weights,) = call(weight_kernel, [(CHUNKS * LOC, 128)], [VMEM])(code)
     place = (obs_comp * (depth * height) + obs_cell // extent).reshape(1, 512)
     lane = (obs_cell % extent).reshape(1, 512)
     level = ((obs_cell // extent) % height).astype(F32).reshape(1, 512)
@@ -381,28 +422,27 @@
     precision = lax.dynamic_index_in_dim(obs_precision.reshape(parts // 2, 2, 4, 128), core, 1, keepdims=False)
     precision = precision.reshape(K, 128)
 
+    (own,) = call(copy_kernel, [field.shape], [pl.BlockSpec(memory_space=pl.ANY)])(field)
     before = lax.ppermute(field, "space", up)
     after = lax.ppermute(field, "space", down)
     message, terms = call(
         model_kernel, [(parts * LINES, 128), (3, 3 * depth * height, extent)], [VMEM] * 6
-    )(before, field, after, place, lane, level)
-    message = exchange(message, "space", parts)
+    )(before, own, after, place, lane, level)
+    message = lax.all_to_all(message.reshape(parts, LINES, extent), "space", 0, 0, tiled=True)
+    message = message.reshape(parts * LINES, extent)
     (send,) = call(
         functools.partial(forecast_kernel, depth * parts * extent),
         [(K * ROWS, 128)],
         [SMEM] + [VMEM] * 3,
         [pltpu.VMEM((3 * depth * height, extent), F32)],
-    )(core.reshape(1), message, field, terms)
+    )(core.reshape(1), message, own, terms)
     received = exchange(send, "member", K)
     (near,) = call(table_kernel, [(parts * 64, 128)], [VMEM] * 3)(received, value, precision)
     far = lax.ppermute(near, "space", [(i, i ^ 1) for i in range(parts)])
+    tiles, centres = call(spread_kernel, [(4, 256, 576), (9, 128)], [VMEM], kinds=[BF16, F32])(received)
     (result,) = call(
-        analysis_kernel,
-        [(K * BACK, 128)],
-        [SMEM] + [VMEM] * 4,
-        [pltpu.VMEM((2048, 128), F32), pltpu.VMEM((CHUNKS * LOC, 128), F32)],
-        limit=40 * 2**20,
-    )(places, code, near, far, received)
+        analysis_kernel, [(K * BACK, 128)], [SMEM] + [VMEM] * 5, SCRATCH, 32 * 2**20
+    )(places, weights, near, far, tiles, centres)
     returned = exchange(result, "member", K)
     (result,) = call(order_kernel, [(3, depth, height, extent)], [VMEM])(returned)
     return result[None]

time: 96.1 us -> 95.6 us (level)
  waiting for transfers between devices: 38 us -> 35.4 us
  Pallas kernels: 16.1 us -> 18.2 us
    all_to_all x0 -> x1, waiting for transfers between devices: none -> 9.8 us  [shards(): lax.all_to_all(message.reshape(parts, LINES, extent), 'space', 0, 0, tile...]
    all_to_all x2 -> x1, waiting for transfers between devices: 30.9 us -> 21.5 us  [exchange(): sent = lax.all_to_all(rows.reshape(count, 1, width), axis, 0, 0, tiled=True)]
    all_to_all x2 -> x1, starting transfers between devices: 13.9 us -> 10.2 us  [exchange(): sent = lax.all_to_all(rows.reshape(count, 1, width), axis, 0, 0, tiled=True)]
    all_to_all x0 -> x1, starting transfers between devices: none -> 3.52 us  [shards(): lax.all_to_all(message.reshape(parts, LINES, extent), 'space', 0, 0, tile...]
    pallas_call x1 -> x4, Pallas kernels: 11.9 us -> 13.9 us  [the longest x1 11.9 us: shards(): call(analysis_kernel, [(K * BACK, 128)], [SMEM] + [VMEM] * 5, SCRATCH, 32...]
    ppermute x1, waiting for transfers between devices: 1.79 us -> 0.01 us  [shards(): far = lax.ppermute(near, 'space', [(i, i ^ 1) for i in range(parts)])]
    ppermute x1, waiting for transfers between devices: 2.27 us -> 1.14 us  [shards(): after = lax.ppermute(field, 'space', down)]
  transfers between devices with their start and end apart: 5 -> 5, of which waited for: 5 -> 4; matrix products, arithmetic and copies ran while one was open for 1% -> 1% of each run, Pallas kernels for 0% -> 2%
where the time goes in v3:
time: 95.6 us; the launch traced here: 95.2 us
  waiting for transfers between devices  35.4 us (37%)
  starting transfers between devices  24.1 us (25%)
  Pallas kernels  18.2 us (19%)
  blocking collectives  15.6 us (16%)
  local copies, waits for them, and re-layouts  0.98 us (1%)
    all_to_all x1, waiting for transfers between devices, exchange(): sent = lax.all_to_all(rows.reshape(count, 1, width), axis, 0, 0, tiled=True)  21.5 us
    all_to_all x1, blocking collectives, exchange(): sent = lax.all_to_all(rows.reshape(count, 1, width), axis, 0, 0, tiled=True)  15.6 us
    pallas_call x1, Pallas kernels, shards(): call(analysis_kernel, [(K * BACK, 128)], [SMEM] + [VMEM] * 5, SCRATCH, 32...  11.9 us
    all_to_all x1, starting transfers between devices, exchange(): sent = lax.all_to_all(rows.reshape(count, 1, width), axis, 0, 0, tiled=True)  10.2 us
    all_to_all x1, waiting for transfers between devices, shards(): lax.all_to_all(message.reshape(parts, LINES, extent), 'space', 0, 0, tile...  9.8 us
    ppermute x1, starting transfers between devices, shards(): after = lax.ppermute(field, 'space', down)  8.48 us
    all_to_all x1, starting transfers between devices, shards(): lax.all_to_all(message.reshape(parts, LINES, extent), 'space', 0, 0, tile...  3.52 us
    ppermute x1, waiting for transfers between devices, shards(): before = lax.ppermute(field, 'space', up)  3 us
  transfers between devices with their start and end apart: 5, of which 4 were waited for; matrix products, arithmetic and copies ran while one was open for 1% of the time, Pallas kernels for 2%

profile of v3, /device:TPU:8, one launch (start us, length us, event | category | flops | bytes accessed | tf_op | source)
XLA Modules:
  0.0 95.2 jit_solution(1625605686441090822)
XLA Ops:
  0.0 8.5 %collective-permute-start.1 = (f32[3,2,48,128]{3,2,1,0:T(8,128)}, f32[3,2,48,128]{3,2,1,0:T(8,128)S(1)}, u32[]{:S(2)}, u32[]{:S(2)}) collective-permute-start(f32[3,2,48,128]{3,2,1,0:T(8,128)} %bitcast.23), channel_id=1, source_target_pairs={{1,0},{2,1},{3,2},{4,3},{5,4},{6,5},{7,6},{8,7},{9,8},{10,9},{11,1... | collective-permute-start | bytes 442376 | tf_op jit(solution)/shard_map/ppermute | solution.py:427
  8.5 0.0 collective-permute-start
  8.5 0.0 copy-start
  8.5 0.9 copy-done
  9.4 0.0 copy-start.3
  9.4 0.0 copy-start.4
  9.4 0.2 shard_map.74.own
  9.6 0.7 fusion.15
  10.3 1.1 %collective-permute-done.1.after = f32[3,2,48,128]{3,2,1,0:T(8,128)S(1)} collective-permute-done((f32[3,2,48,128]{3,2,1,0:T(8,128)}, f32[3,2,48,128]{3,2,1,0:T(8,128)S(1)}, u32[]{:S(2)}, u32[]{:S(2)}) %collective-permute-start.1) | collective-permute-done | bytes 147488 | tf_op jit(solution)/shard_map/ppermute | solution.py:427
  11.5 3.0 %collective-permute-done.before = f32[3,2,48,128]{3,2,1,0:T(8,128)S(1)} collective-permute-done((f32[3,2,48,128]{3,2,1,0:T(8,128)}, f32[3,2,48,128]{3,2,1,0:T(8,128)S(1)}, u32[]{:S(2)}, u32[]{:S(2)}) %collective-permute-start) | collective-permute-done | bytes 147488 | tf_op jit(solution)/shard_map/ppermute | solution.py:426
  14.5 2.2 %shard_map.75 = (f32[384,128]{1,0:T(8,128)}, f32[3,288,128]{2,1,0:T(8,128)S(1)}) custom-call(f32[3,2,48,128]{3,2,1,0:T(8,128)S(1)} %collective-permute-done.before, f32[3,2,48,128]{3,2,1,0:T(8,128)S(1)} %shard_map.74.own, f32[3,2,48,128]{3,2,1,0:T(8,128)S(1)} %collective-permute-done.1.after, s32[1,512]{1,0:T(1,128)S(1)} %bitcast.30, s32[1,512]{1,0:T(1,128)S(1)} %bitcast.29, ...), custom_call_target="tpu_custom_call" | custom-call | tf_op jit(solution)/shard_map/pallas_call | solution.py:428
  16.7 3.5 %all-to-all-start = ((f32[16,24,128]{2,1,0:T(8,128)}), f32[16,24,128]{2,1,0:T(8,128)S(1)}, u32[]{:S(2)}, u32[]{:S(2)}) async-start(f32[16,24,128]{2,1,0:T(8,128)} %bitcast.6), calls=%async_computation | async-start | bytes 393216 | tf_op jit(solution)/shard_map/all_to_all | solution.py:431
  20.2 0.0 copy-start.1
  20.3 0.0 copy-start.2
  20.3 9.8 %all-to-all-done = f32[16,24,128]{2,1,0:T(8,128)S(1)} async-done(((f32[16,24,128]{2,1,0:T(8,128)}), f32[16,24,128]{2,1,0:T(8,128)S(1)}, u32[]{:S(2)}, u32[]{:S(2)}) %all-to-all-start) | async-done | bytes 196640 | tf_op jit(solution)/shard_map/all_to_all | solution.py:431
  30.1 1.1 %shard_map.76 = f32[1312,128]{1,0:T(8,128)} custom-call(s32[1]{0:T(128)} %bitcast.1.core, f32[384,128]{1,0:T(8,128)S(1)} %bitcast.20, f32[3,2,48,128]{3,2,1,0:T(8,128)S(1)} %shard_map.74.own, f32[3,288,128]{2,1,0:T(8,128)S(1)} %get-tuple-element.10.terms), custom_call_target="tpu_custom_call" | custom-call | tf_op jit(solution)/shard_map/pallas_call | solution.py:433
  31.2 10.2 %all-to-all-start.1 = ((f32[32,1,5248]{2,1,0:T(1,128)}), f32[32,1,5248]{2,1,0:T(1,128)S(1)}, u32[]{:S(2)}, u32[]{:S(2)}) async-start(f32[32,1,5248]{2,1,0:T(1,128)} %bitcast.8), calls=%async_computation.1 | async-start | bytes 1343488 | tf_op jit(solution)/shard_map/all_to_all | solution.py:398
  41.4 0.0 copy-done.3
  41.4 0.0 copy-done.4
  41.4 21.5 %all-to-all-done.1 = f32[32,1,5248]{2,1,0:T(1,128)S(1)} async-done(((f32[32,1,5248]{2,1,0:T(1,128)}), f32[32,1,5248]{2,1,0:T(1,128)S(1)}, u32[]{:S(2)}, u32[]{:S(2)}) %all-to-all-start.1) | async-done | bytes 671776 | tf_op jit(solution)/shard_map/all_to_all | solution.py:398
  62.9 0.2 shard_map.77.near
  63.1 1.9 %collective-permute-start.2 = (f32[1024,128]{1,0:T(8,128)S(1)}, f32[1024,128]{1,0:T(8,128)S(1)}, u32[]{:S(2)}, u32[]{:S(2)}) collective-permute-start(f32[1024,128]{1,0:T(8,128)S(1)} %shard_map.77.near), channel_id=1, source_target_pairs={{0,1},{1,0},{2,3},{3,2},{4,5},{5,4},{6,7},{7,6},{8,9},{9,8},{10,11... | collective-permute-start | bytes 1572872 | tf_op jit(solution)/shard_map/ppermute | solution.py:441
  65.0 0.0 copy-done.1
  65.0 0.0 copy-done.2
  65.0 0.1 fusion.8
  65.1 1.1 %shard_map.73.weights = f32[4096,128]{1,0:T(8,128)S(1)} custom-call(s32[32,128]{1,0:T(8,128)S(1)} %get-tuple-element.13.code), custom_call_target="tpu_custom_call" | custom-call | tf_op jit(solution)/shard_map/pallas_call | solution.py:415
  66.2 0.8 shard_map.78
  67.0 0.0 collective-permute-done.2.far
  67.0 11.9 %shard_map.79 = f32[288,128]{1,0:T(8,128)S(1)} custom-call(s32[4096]{0:T(1024)S(1)} %get-tuple-element.14.places, f32[4096,128]{1,0:T(8,128)S(1)} %shard_map.73.weights, f32[1024,128]{1,0:T(8,128)S(1)} %shard_map.77.near, f32[1024,128]{1,0:T(8,128)S(1)} %collective-permute-done.2.far, bf16[4,256,576]{2,1,0:T(8,128)(2,1)S(1)} %get-tuple-element.11.tiles, ...), custom_call_target="tpu_custom_call" | custom-call | tf_op jit(solution)/shard_map/pallas_call | solution.py:443
  78.9 15.6 %all_to_all.15 = f32[32,1,1152]{2,1,0:T(1,128)S(1)} all-to-all(f32[32,1,1152]{2,1,0:T(1,128)S(1)} %bitcast.21), channel_id=1, replica_groups=mesh['member'=32,'space'=16] {'member'}, dimensions={0} | all-to-all | bytes 294912 | tf_op jit(solution)/shard_map/all_to_all | solution.py:398
  94.5 0.7 shard_map.80
  (1 shorter events, 0.0 us)
Async XLA Ops:
  0.0 11.5 %collective-permute-start.1 = (f32[3,2,48,128]{3,2,1,0:T(8,128)}, f32[3,2,48,128]{3,2,1,0:T(8,128)S(1)}, u32[]{:S(2)}, u32[]{:S(2)}) collective-permute-start(f32[3,2,48,128]{3,2,1,0:T(8,128)} %bitcast.23), channel_id=1, source_target_pairs={{1,0},{2,1},{3,2},{4,3},{5,4},{6,5},{7,6},{8,7},{9,8},{10,9},{11,1... | collective-permute-start | bytes 442376 | tf_op jit(solution)/shard_map/ppermute | solution.py:427
  8.5 6.0 %collective-permute-start = (f32[3,2,48,128]{3,2,1,0:T(8,128)}, f32[3,2,48,128]{3,2,1,0:T(8,128)S(1)}, u32[]{:S(2)}, u32[]{:S(2)}) collective-permute-start(f32[3,2,48,128]{3,2,1,0:T(8,128)} %bitcast.24), channel_id=1, source_target_pairs={{0,1},{1,2},{2,3},{3,4},{4,5},{5,6},{6,7},{7,8},{8,9},{9,10},{10,1... | collective-permute-start | bytes 442376 | tf_op jit(solution)/shard_map/ppermute | solution.py:426
  8.5 0.9 copy-start
  9.4 31.9 %copy-start.3 = (f32[8192]{0:T(1024)S(1)}, f32[8192]{0:T(1024)}, u32[]{:S(2)}) copy-start(f32[8192]{0:T(1024)} %param.11) | copy-start | bytes 98308
  9.4 31.9 %copy-start.4 = (f32[8192]{0:T(1024)S(1)}, f32[8192]{0:T(1024)}, u32[]{:S(2)}) copy-start(f32[8192]{0:T(1024)} %param.10) | copy-start | bytes 98308
  16.7 13.4 %all-to-all-start = ((f32[16,24,128]{2,1,0:T(8,128)}), f32[16,24,128]{2,1,0:T(8,128)S(1)}, u32[]{:S(2)}, u32[]{:S(2)}) async-start(f32[16,24,128]{2,1,0:T(8,128)} %bitcast.6), calls=%async_computation | async-start | bytes 393216 | tf_op jit(solution)/shard_map/all_to_all | solution.py:431
  20.2 44.8 %copy-start.1 = (s32[32,128]{1,0:T(8,128)S(1)}, s32[32,128]{1,0:T(8,128)}, u32[]{:S(2)}) copy-start(s32[32,128]{1,0:T(8,128)} %param.13) | copy-start | bytes 49156
  20.3 44.8 %copy-start.2 = (s32[32,128]{1,0:T(8,128)S(1)}, s32[32,128]{1,0:T(8,128)}, u32[]{:S(2)}) copy-start(s32[32,128]{1,0:T(8,128)} %param.12) | copy-start | bytes 49156
  31.2 31.7 %all-to-all-start.1 = ((f32[32,1,5248]{2,1,0:T(1,128)}), f32[32,1,5248]{2,1,0:T(1,128)S(1)}, u32[]{:S(2)}, u32[]{:S(2)}) async-start(f32[32,1,5248]{2,1,0:T(1,128)} %bitcast.8), calls=%async_computation.1 | async-start | bytes 1343488 | tf_op jit(solution)/shard_map/all_to_all | solution.py:398
  63.1 3.9 %collective-permute-start.2 = (f32[1024,128]{1,0:T(8,128)S(1)}, f32[1024,128]{1,0:T(8,128)S(1)}, u32[]{:S(2)}, u32[]{:S(2)}) collective-permute-start(f32[1024,128]{1,0:T(8,128)S(1)} %shard_map.77.near), channel_id=1, source_target_pairs={{0,1},{1,0},{2,3},{3,2},{4,5},{5,4},{6,7},{7,6},{8,9},{9,8},{10,11... | collective-permute-start | bytes 1572872 | tf_op jit(solution)/shard_map/ppermute | solution.py:441

commit v4 on v3

--- a/solution.py
+++ b/solution.py
@@ -101,7 +101,26 @@
     return jnp.where(row == 0, 0.0, pltpu.roll(plane, 1, 0))
 
 
-def model_kernel(before, own, after, place, lane, level, message, terms):
+def pick(pieces, choice, spot):
+    picked = dot_t(pieces[-1], choice)
+    for piece in pieces[-2::-1]:
+        picked = picked + dot_t(piece, choice)
+    return jnp.sum(jnp.where(spot, picked, 0.0), axis=0, keepdims=True)
+
+
+def first_kernel(source, cell, comp, own, chosen, ready):
+    pltpu.sync_copy(source, own)
+    level = cell[...] >> 7
+    place = comp[...] * 96 + level
+    choice = (iota((288, 512), 0) == place).astype(F32).astype(BF16)
+    chosen[...] = choice
+    spot = iota((128, 512), 0) == (cell[...] & 127)
+    flow = pick(split3(own[...].reshape(288, 128)), choice, spot)
+    level = jnp.where(level >= 48, level - 48, level).astype(F32)
+    ready[...] = jnp.concatenate([flow, level, jnp.zeros((6, 512), F32)], axis=0)
+
+
+def model_kernel(before, own, after, cell, chosen, ready, message, terms):
     fields = [
         {0: before[a, 0], 1: before[a, 1], 2: own[a, 0], 3: own[a, 1], 4: after[a, 0], 5: after[a, 1]}
         for a in range(3)
@@ -122,19 +141,12 @@
             terms[0, start : start + 48, :] = 0.5 * flat
             terms[1, start : start + 48, :] = shifted_y(upright, 1)
             terms[2, start : start + 48, :] = -shifted_y(upright, -1)
-    chosen = (iota((288, 512), 0) == place[...]).astype(F32).astype(BF16)
-    spot = iota((128, 512), 0) == lane[...]
-    lines = []
-    for f in range(4):
-        if f == 0:
-            pieces = split3(own[...].reshape(288, 128))
-        else:
-            pieces = split2(terms[f - 1])
-        picked = dot_t(pieces[-1], chosen)
-        for piece in pieces[-2::-1]:
-            picked = picked + dot_t(piece, chosen)
-        lines.append(jnp.sum(jnp.where(spot, picked, 0.0), axis=0, keepdims=True))
-    lines.append(level[...])
+    choice = chosen[...]
+    spot = iota((128, 512), 0) == (cell[...] & 127)
+    lines = [ready[0:1, :]]
+    for f in range(3):
+        lines.append(pick(split2(terms[f]), choice, spot))
+    lines.append(ready[1:2, :])
     smooth = [{p: filter_xz(f, p) for p in range(1, 5)} for f in fields]
     numer = 0.0
     denom = 0.0
@@ -234,10 +246,6 @@
     return (wide[2 * rows :] + wide[rows : 2 * rows]) + wide[:rows]
 
 
-def copy_kernel(source, target):
-    pltpu.sync_copy(source, target)
-
-
 def weight_kernel(code, weights):
     columns = jnp.concatenate([code[...], jnp.zeros((96, 128), jnp.int32)], axis=0).T
     quarter = iota((LOC, 128), 1) // 32
@@ -281,36 +289,28 @@
     return (wide[K:] + dot(left1, right2)) + wide[:K]
 
 
-def analysis_kernel(places, weights, near, far, tiles, centres, out, table, first, second, grams):
+def analysis_kernel(places, weights, near, far, tiles, centres, out, table, picked):
     table[0:1024, :] = near[...]
     table[1024:2048, :] = far[...]
 
     quarter = iota((LOC, 128), 1) // 32
 
-    def fetch(c, target, at):
-        base = c * LOC
-        for j in range(LOC):
-            target[at + j : at + j + 1, :] = table[pl.ds(places[base + j], 1), :]
-
-    def half(four, source, target):
-        coming = jnp.minimum(4 * four + 4, CHUNKS - 4)
+    def fetch(four, carry):
+        base = pl.multiple_of(four * (4 * LOC), 4 * LOC)
+        target = picked.at[pl.ds(base, 4 * LOC)]
+        for j in range(4 * LOC):
+            target[j : j + 1, :] = table[pl.ds(places[base + j], 1), :]
+        return carry
+
+    lax.fori_loop(0, CHUNKS // 4, fetch, 0)
+    grams = []
+    for four in range(CHUNKS // 4):
         pack = None
         for i in range(4):
-            fetch(coming + i, target, i * LOC)
-            at = pl.multiple_of(four * (4 * LOC) + i * LOC, LOC)
-            lone = folded(source[i * LOC : (i + 1) * LOC, :], weights[pl.ds(at, LOC), :])
+            at = (4 * four + i) * LOC
+            lone = folded(picked[at : at + LOC, :], weights[at : at + LOC, :])
             pack = lone if i == 0 else jnp.where(quarter == i, lone, pack)
-        grams[four] = four_gram(pack)
-
-    for i in range(4):
-        fetch(i, first, i * LOC)
-
-    def step(i, carry):
-        half(2 * i, first, second)
-        half(2 * i + 1, second, first)
-        return carry
-
-    lax.fori_loop(0, 4, step, 0)
+        grams.append(four_gram(pack))
     packs = [jnp.concatenate([grams[2 * g], grams[2 * g + 1]], axis=1) for g in range(4)]
 
     tall = iota((256, 256), 0)
@@ -367,12 +367,7 @@
         out[pl.ds(r, K, stride=BACK), :] = row + centres[r : r + 1, :]
 
 
-SCRATCH = [
-    pltpu.VMEM((2048, 128), F32),
-    pltpu.VMEM((4 * LOC, 128), F32),
-    pltpu.VMEM((4 * LOC, 128), F32),
-    pltpu.VMEM((CHUNKS // 4, K, 128), F32),
-]
+SCRATCH = [pltpu.VMEM((2048, 128), F32), pltpu.VMEM((CHUNKS * LOC, 128), F32)]
 
 
 def order_kernel(returned, out):
@@ -412,23 +407,27 @@
     places = (slab // 2) * 128 + ((slab + here) % 2) * 1024 + within % 128
     places = places.reshape(CHUNKS * LOC)
     code = (within // 128) * 16 + loc_level
-    (weights,) = call(weight_kernel, [(CHUNKS * LOC, 128)], [VMEM])(code)
-    place = (obs_comp * (depth * height) + obs_cell // extent).reshape(1, 512)
-    lane = (obs_cell % extent).reshape(1, 512)
-    level = ((obs_cell // extent) % height).astype(F32).reshape(1, 512)
     core = here & 1
     value = lax.dynamic_index_in_dim(obs_value.reshape(parts // 2, 2, 4, 128), core, 1, keepdims=False)
     value = value.reshape(K, 128)
     precision = lax.dynamic_index_in_dim(obs_precision.reshape(parts // 2, 2, 4, 128), core, 1, keepdims=False)
     precision = precision.reshape(K, 128)
 
-    (own,) = call(copy_kernel, [field.shape], [pl.BlockSpec(memory_space=pl.ANY)])(field)
+    cell = obs_cell.reshape(1, 512)
+    own, chosen, ready = call(
+        first_kernel,
+        [field.shape, (3 * depth * height, 512), (8, 512)],
+        [pl.BlockSpec(memory_space=pl.ANY), VMEM, VMEM],
+        kinds=[F32, BF16, F32],
+    )(field, cell, obs_comp.reshape(1, 512))
     before = lax.ppermute(field, "space", up)
     after = lax.ppermute(field, "space", down)
     message, terms = call(
         model_kernel, [(parts * LINES, 128), (3, 3 * depth * height, extent)], [VMEM] * 6
-    )(before, own, after, place, lane, level)
+    )(before, own, after, cell, chosen, ready)
     message = lax.all_to_all(message.reshape(parts, LINES, extent), "space", 0, 0, tiled=True)
+    (weights,) = call(weight_kernel, [(CHUNKS * LOC, 128)], [VMEM])(code)
+    message, weights, places = lax.optimization_barrier((message, weights, places))
     message = message.reshape(parts * LINES, extent)
     (send,) = call(
         functools.partial(forecast_kernel, depth * parts * extent),

time: 95.6 us -> 94.7 us (level)
  waiting for transfers between devices: 35.4 us -> 33.6 us
  local copies, waits for them, and re-layouts: 0.98 us -> 2.33 us
    all_to_all x1, waiting for transfers between devices: 9.8 us -> 7.9 us  [shards(): lax.all_to_all(message.reshape(parts, LINES, extent), 'space', 0, 0, tile...]
    unnamed x10, local copies, waits for them, and re-layouts: 0.96 us -> 2.31 us
    ppermute x1, waiting for transfers between devices: 0.01 us -> 1.11 us  [shards(): far = lax.ppermute(near, 'space', [(i, i ^ 1) for i in range(parts)])]
    ppermute x1, waiting for transfers between devices: 1.14 us -> 0.08 us  [shards(): after = lax.ppermute(field, 'space', down)]
  transfers between devices with their start and end apart: 5 -> 5, of which waited for: 4 -> 5; matrix products, arithmetic and copies ran while one was open for 1% -> 1% of each run, Pallas kernels for 2% -> 3%
where the time goes in v4:
time: 94.7 us; the launch traced here: 94.2 us
  waiting for transfers between devices  33.6 us (35%)
  starting transfers between devices  24.1 us (25%)
  Pallas kernels  17.9 us (19%)
  blocking collectives  15.3 us (16%)
  local copies, waits for them, and re-layouts  2.33 us (2%)
    all_to_all x1, waiting for transfers between devices, exchange(): sent = lax.all_to_all(rows.reshape(count, 1, width), axis, 0, 0, tiled=True)  21.5 us
    all_to_all x1, blocking collectives, exchange(): sent = lax.all_to_all(rows.reshape(count, 1, width), axis, 0, 0, tiled=True)  15.3 us
    pallas_call x1, Pallas kernels, shards(): call(analysis_kernel, [(K * BACK, 128)], [SMEM] + [VMEM] * 5, SCRATCH, 32...  11.2 us
    all_to_all x1, starting transfers between devices, exchange(): sent = lax.all_to_all(rows.reshape(count, 1, width), axis, 0, 0, tiled=True)  10.2 us
    ppermute x1, starting transfers between devices, shards(): after = lax.ppermute(field, 'space', down)  8.48 us
    all_to_all x1, waiting for transfers between devices, shards(): lax.all_to_all(message.reshape(parts, LINES, extent), 'space', 0, 0, tile...  7.9 us
    all_to_all x1, starting transfers between devices, shards(): lax.all_to_all(message.reshape(parts, LINES, extent), 'space', 0, 0, tile...  3.52 us
    ppermute x1, waiting for transfers between devices, shards(): before = lax.ppermute(field, 'space', up)  3 us
  transfers between devices with their start and end apart: 5, of which 5 were waited for; matrix products, arithmetic and copies ran while one was open for 1% of the time, Pallas kernels for 3%

profile of v4, /device:TPU:8, one launch (start us, length us, event | category | flops | bytes accessed | tf_op | source)
XLA Modules:
  0.0 94.2 jit_solution(10557481678162734522)
XLA Ops:
  0.0 8.5 %collective-permute-start.1 = (f32[3,2,48,128]{3,2,1,0:T(8,128)}, f32[3,2,48,128]{3,2,1,0:T(8,128)S(1)}, u32[]{:S(2)}, u32[]{:S(2)}) collective-permute-start(f32[3,2,48,128]{3,2,1,0:T(8,128)} %bitcast.22), channel_id=1, source_target_pairs={{1,0},{2,1},{3,2},{4,3},{5,4},{6,5},{7,6},{8,7},{9,8},{10,9},{11,1... | collective-permute-start | bytes 442376 | tf_op jit(solution)/shard_map/ppermute | solution.py:424
  8.5 0.0 collective-permute-start
  8.5 0.0 copy-start
  8.5 0.9 copy-done
  9.4 0.0 copy-start.1
  9.4 0.7 copy-done.1
  10.1 0.0 copy-start.2
  10.1 0.7 copy-done.2
  10.8 0.6 shard_map.73
  11.4 0.1 collective-permute-done.1.after
  11.5 3.0 %collective-permute-done.before = f32[3,2,48,128]{3,2,1,0:T(8,128)S(1)} collective-permute-done((f32[3,2,48,128]{3,2,1,0:T(8,128)}, f32[3,2,48,128]{3,2,1,0:T(8,128)S(1)}, u32[]{:S(2)}, u32[]{:S(2)}) %collective-permute-start) | collective-permute-done | bytes 147488 | tf_op jit(solution)/shard_map/ppermute | solution.py:423
  14.5 2.2 %shard_map.74 = (f32[384,128]{1,0:T(8,128)}, f32[3,288,128]{2,1,0:T(8,128)S(1)}) custom-call(f32[3,2,48,128]{3,2,1,0:T(8,128)S(1)} %collective-permute-done.before, f32[3,2,48,128]{3,2,1,0:T(8,128)S(1)} %get-tuple-element.15.own, f32[3,2,48,128]{3,2,1,0:T(8,128)S(1)} %collective-permute-done.1.after, s32[1,512]{1,0:T(1,128)S(1)} %bitcast.28, ...), custom_call_target="tpu_custom_call" | custom-call | tf_op jit(solution)/shard_map/pallas_call | solution.py:425
  16.7 3.5 %all-to-all-start = ((f32[16,24,128]{2,1,0:T(8,128)}), f32[16,24,128]{2,1,0:T(8,128)S(1)}, u32[]{:S(2)}, u32[]{:S(2)}) async-start(f32[16,24,128]{2,1,0:T(8,128)} %bitcast.3), calls=%async_computation | async-start | bytes 393216 | tf_op jit(solution)/shard_map/all_to_all | solution.py:428
  20.2 0.8 fusion.6
  21.0 0.0 copy-start.3
  21.0 0.0 copy-start.4
  21.0 1.1 %shard_map.75.weights = f32[4096,128]{1,0:T(8,128)S(1)} custom-call(s32[32,128]{1,0:T(8,128)S(1)} %get-tuple-element.26.code), custom_call_target="tpu_custom_call" | custom-call | tf_op jit(solution)/shard_map/pallas_call | solution.py:429
  22.1 7.9 %all-to-all-done = f32[16,24,128]{2,1,0:T(8,128)S(1)} async-done(((f32[16,24,128]{2,1,0:T(8,128)}), f32[16,24,128]{2,1,0:T(8,128)S(1)}, u32[]{:S(2)}, u32[]{:S(2)}) %all-to-all-start) | async-done | bytes 196640 | tf_op jit(solution)/shard_map/all_to_all | solution.py:428
  30.1 1.1 %shard_map.76 = f32[1312,128]{1,0:T(8,128)} custom-call(s32[1]{0:T(128)} %bitcast.5.core, f32[384,128]{1,0:T(8,128)S(1)} %bitcast.19, f32[3,2,48,128]{3,2,1,0:T(8,128)S(1)} %get-tuple-element.15.own, f32[3,288,128]{2,1,0:T(8,128)S(1)} %get-tuple-element.22.terms), custom_call_target="tpu_custom_call" | custom-call | tf_op jit(solution)/shard_map/pallas_call | solution.py:432
  31.2 10.2 %all-to-all-start.1 = ((f32[32,1,5248]{2,1,0:T(1,128)}), f32[32,1,5248]{2,1,0:T(1,128)S(1)}, u32[]{:S(2)}, u32[]{:S(2)}) async-start(f32[32,1,5248]{2,1,0:T(1,128)} %bitcast.7), calls=%async_computation.1 | async-start | bytes 1343488 | tf_op jit(solution)/shard_map/all_to_all | solution.py:393
  41.3 0.0 copy-done.3
  41.3 0.0 copy-done.4
  41.4 21.5 %all-to-all-done.1 = f32[32,1,5248]{2,1,0:T(1,128)S(1)} async-done(((f32[32,1,5248]{2,1,0:T(1,128)}), f32[32,1,5248]{2,1,0:T(1,128)S(1)}, u32[]{:S(2)}, u32[]{:S(2)}) %all-to-all-start.1) | async-done | bytes 671776 | tf_op jit(solution)/shard_map/all_to_all | solution.py:393
  62.8 0.2 shard_map.77.near
  63.1 1.9 %collective-permute-start.2 = (f32[1024,128]{1,0:T(8,128)S(1)}, f32[1024,128]{1,0:T(8,128)S(1)}, u32[]{:S(2)}, u32[]{:S(2)}) collective-permute-start(f32[1024,128]{1,0:T(8,128)S(1)} %shard_map.77.near), channel_id=1, source_target_pairs={{0,1},{1,0},{2,3},{3,2},{4,5},{5,4},{6,7},{7,6},{8,9},{9,8},{10,11... | collective-permute-start | bytes 1572872 | tf_op jit(solution)/shard_map/ppermute | solution.py:440
  65.0 0.8 shard_map.78
  65.8 1.1 %collective-permute-done.2.far = f32[1024,128]{1,0:T(8,128)S(1)} collective-permute-done((f32[1024,128]{1,0:T(8,128)S(1)}, f32[1024,128]{1,0:T(8,128)S(1)}, u32[]{:S(2)}, u32[]{:S(2)}) %collective-permute-start.2) | collective-permute-done | bytes 524320 | tf_op jit(solution)/shard_map/ppermute | solution.py:440
  66.9 11.2 %shard_map.79 = f32[288,128]{1,0:T(8,128)S(1)} custom-call(s32[4096]{0:T(1024)S(1)} %get-tuple-element.19.places, f32[4096,128]{1,0:T(8,128)S(1)} %shard_map.75.weights, f32[1024,128]{1,0:T(8,128)S(1)} %shard_map.77.near, f32[1024,128]{1,0:T(8,128)S(1)} %collective-permute-done.2.far, bf16[4,256,576]{2,1,0:T(8,128)(2,1)S(1)} %get-tuple-element.23.tiles, ...), custom_call_target="tpu_custom_call" | custom-call | tf_op jit(solution)/shard_map/pallas_call | solution.py:442
  78.1 15.3 %all_to_all.15 = f32[32,1,1152]{2,1,0:T(1,128)S(1)} all-to-all(f32[32,1,1152]{2,1,0:T(1,128)S(1)} %bitcast.20), channel_id=1, replica_groups=mesh['member'=32,'space'=16] {'member'}, dimensions={0} | all-to-all | bytes 294912 | tf_op jit(solution)/shard_map/all_to_all | solution.py:393
  93.5 0.7 shard_map.80
  (1 shorter events, 0.0 us)
Async XLA Ops:
  0.0 11.5 %collective-permute-start.1 = (f32[3,2,48,128]{3,2,1,0:T(8,128)}, f32[3,2,48,128]{3,2,1,0:T(8,128)S(1)}, u32[]{:S(2)}, u32[]{:S(2)}) collective-permute-start(f32[3,2,48,128]{3,2,1,0:T(8,128)} %bitcast.22), channel_id=1, source_target_pairs={{1,0},{2,1},{3,2},{4,3},{5,4},{6,5},{7,6},{8,7},{9,8},{10,9},{11,1... | collective-permute-start | bytes 442376 | tf_op jit(solution)/shard_map/ppermute | solution.py:424
  8.5 6.0 %collective-permute-start = (f32[3,2,48,128]{3,2,1,0:T(8,128)}, f32[3,2,48,128]{3,2,1,0:T(8,128)S(1)}, u32[]{:S(2)}, u32[]{:S(2)}) collective-permute-start(f32[3,2,48,128]{3,2,1,0:T(8,128)} %bitcast.23), channel_id=1, source_target_pairs={{0,1},{1,2},{2,3},{3,4},{4,5},{5,6},{6,7},{7,8},{8,9},{9,10},{10,1... | collective-permute-start | bytes 442376 | tf_op jit(solution)/shard_map/ppermute | solution.py:423
  8.5 0.9 copy-start
  9.4 0.7 copy-start.1
  10.1 0.7 copy-start.2
  16.7 13.4 %all-to-all-start = ((f32[16,24,128]{2,1,0:T(8,128)}), f32[16,24,128]{2,1,0:T(8,128)S(1)}, u32[]{:S(2)}, u32[]{:S(2)}) async-start(f32[16,24,128]{2,1,0:T(8,128)} %bitcast.3), calls=%async_computation | async-start | bytes 393216 | tf_op jit(solution)/shard_map/all_to_all | solution.py:428
  21.0 20.3 %copy-start.3 = (f32[8192]{0:T(1024)S(1)}, f32[8192]{0:T(1024)}, u32[]{:S(2)}) copy-start(f32[8192]{0:T(1024)} %param.11) | copy-start | bytes 98308
  21.0 20.3 %copy-start.4 = (f32[8192]{0:T(1024)S(1)}, f32[8192]{0:T(1024)}, u32[]{:S(2)}) copy-start(f32[8192]{0:T(1024)} %param.10) | copy-start | bytes 98308
  31.2 31.7 %all-to-all-start.1 = ((f32[32,1,5248]{2,1,0:T(1,128)}), f32[32,1,5248]{2,1,0:T(1,128)S(1)}, u32[]{:S(2)}, u32[]{:S(2)}) async-start(f32[32,1,5248]{2,1,0:T(1,128)} %bitcast.7), calls=%async_computation.1 | async-start | bytes 1343488 | tf_op jit(solution)/shard_map/all_to_all | solution.py:393
  63.1 3.8 %collective-permute-start.2 = (f32[1024,128]{1,0:T(8,128)S(1)}, f32[1024,128]{1,0:T(8,128)S(1)}, u32[]{:S(2)}, u32[]{:S(2)}) collective-permute-start(f32[1024,128]{1,0:T(8,128)S(1)} %shard_map.77.near), channel_id=1, source_target_pairs={{0,1},{1,0},{2,3},{3,2},{4,5},{5,4},{6,7},{7,6},{8,9},{9,8},{10,11... | collective-permute-start | bytes 1572872 | tf_op jit(solution)/shard_map/ppermute | solution.py:440

commit v5 on v4

--- a/solution.py
+++ b/solution.py
@@ -255,7 +255,16 @@
         weights[c * LOC : (c + 1) * LOC, :] = jnp.where((mark >> 4) == quarter, level, 0.0)
 
 
-def spread_kernel(received, tiles, centres):
+def spread_kernel(received, tiles, centres, masks):
+    tall = iota((256, 256), 0)
+    wide_lane = iota((256, 256), 1)
+    same = (tall // 32) == (wide_lane // 32)
+    mask = jnp.where(same, 1.0, 0.0).astype(BF16)
+    last = (wide_lane % 32) == 31
+    not_last_row = (tall % 32) != 31
+    rebuild = jnp.where(last, jnp.where(same & not_last_row, -1.0, 0.0), jnp.where(tall == wide_lane, 1.0, 0.0))
+    masks[0] = mask
+    masks[1] = rebuild.astype(BF16)
     cells = [received[pl.ds(r, K, stride=ROWS), :] for r in range(9)]
     means = [jnp.sum(v, axis=0, keepdims=True) * (1.0 / K) for v in cells]
     centres[...] = jnp.concatenate(means, axis=0)
@@ -289,20 +298,17 @@
     return (wide[K:] + dot(left1, right2)) + wide[:K]
 
 
-def analysis_kernel(places, weights, near, far, tiles, centres, out, table, picked):
+def analysis_kernel(places, weights, near, far, tiles, centres, masks, out, table, picked):
     table[0:1024, :] = near[...]
     table[1024:2048, :] = far[...]
 
     quarter = iota((LOC, 128), 1) // 32
 
-    def fetch(four, carry):
-        base = pl.multiple_of(four * (4 * LOC), 4 * LOC)
-        target = picked.at[pl.ds(base, 4 * LOC)]
-        for j in range(4 * LOC):
-            target[j : j + 1, :] = table[pl.ds(places[base + j], 1), :]
+    def fetch(at, carry):
+        picked[pl.ds(at, 1), :] = table[pl.ds(places[at], 1), :]
         return carry
 
-    lax.fori_loop(0, CHUNKS // 4, fetch, 0)
+    lax.fori_loop(0, CHUNKS * LOC, fetch, 0, unroll=True)
     grams = []
     for four in range(CHUNKS // 4):
         pack = None
@@ -313,14 +319,8 @@
         grams.append(four_gram(pack))
     packs = [jnp.concatenate([grams[2 * g], grams[2 * g + 1]], axis=1) for g in range(4)]
 
-    tall = iota((256, 256), 0)
-    wide_lane = iota((256, 256), 1)
-    same = (tall // 32) == (wide_lane // 32)
-    mask = jnp.where(same, 1.0, 0.0).astype(BF16)
-    last = (wide_lane % 32) == 31
-    not_last_row = (tall % 32) != 31
-    rebuild = jnp.where(last, jnp.where(same & not_last_row, -1.0, 0.0), jnp.where(tall == wide_lane, 1.0, 0.0))
-    rebuild = rebuild.astype(BF16)
+    mask = masks[0]
+    rebuild = masks[1]
     member = iota((K, 256), 0)
     eye = jnp.where(member == iota((K, 256), 1) % 32, 1.0, 0.0)
 
@@ -438,10 +438,12 @@
     received = exchange(send, "member", K)
     (near,) = call(table_kernel, [(parts * 64, 128)], [VMEM] * 3)(received, value, precision)
     far = lax.ppermute(near, "space", [(i, i ^ 1) for i in range(parts)])
-    tiles, centres = call(spread_kernel, [(4, 256, 576), (9, 128)], [VMEM], kinds=[BF16, F32])(received)
+    tiles, centres, masks = call(
+        spread_kernel, [(4, 256, 576), (9, 128), (2, 256, 256)], [VMEM], kinds=[BF16, F32, BF16]
+    )(received)
     (result,) = call(
-        analysis_kernel, [(K * BACK, 128)], [SMEM] + [VMEM] * 5, SCRATCH, 32 * 2**20
-    )(places, weights, near, far, tiles, centres)
+        analysis_kernel, [(K * BACK, 128)], [SMEM] + [VMEM] * 6, SCRATCH, 32 * 2**20
+    )(places, weights, near, far, tiles, centres, masks)
     returned = exchange(result, "member", K)
     (result,) = call(order_kernel, [(3, depth, height, extent)], [VMEM])(returned)
     return result[None]

time: 94.7 us -> 93.4 us (0.986)
  Pallas kernels: 17.9 us -> 16.6 us
    pallas_call x2, Pallas kernels: 12 us -> 10.7 us  [the longest x1 9.92 us: shards(): call(analysis_kernel, [(K * BACK, 128)], [SMEM] + [VMEM] * 6, SCRATCH, 32...]
where the time goes in v5:
time: 93.4 us; the launch traced here: 92.8 us
  waiting for transfers between devices  33.6 us (36%)
  starting transfers between devices  24.1 us (26%)
  Pallas kernels  16.6 us (18%)
  blocking collectives  15.3 us (16%)
  local copies, waits for them, and re-layouts  2.33 us (2%)
    all_to_all x1, waiting for transfers between devices, exchange(): sent = lax.all_to_all(rows.reshape(count, 1, width), axis, 0, 0, tiled=True)  21.5 us
    all_to_all x1, blocking collectives, exchange(): sent = lax.all_to_all(rows.reshape(count, 1, width), axis, 0, 0, tiled=True)  15.3 us
    all_to_all x1, starting transfers between devices, exchange(): sent = lax.all_to_all(rows.reshape(count, 1, width), axis, 0, 0, tiled=True)  10.2 us
    pallas_call x1, Pallas kernels, shards(): call(analysis_kernel, [(K * BACK, 128)], [SMEM] + [VMEM] * 6, SCRATCH, 32...  9.92 us
    ppermute x1, starting transfers between devices, shards(): after = lax.ppermute(field, 'space', down)  8.48 us
    all_to_all x1, waiting for transfers between devices, shards(): lax.all_to_all(message.reshape(parts, LINES, extent), 'space', 0, 0, tile...  7.9 us
    all_to_all x1, starting transfers between devices, shards(): lax.all_to_all(message.reshape(parts, LINES, extent), 'space', 0, 0, tile...  3.52 us
    ppermute x1, waiting for transfers between devices, shards(): before = lax.ppermute(field, 'space', up)  3 us
  transfers between devices with their start and end apart: 5, of which 5 were waited for; matrix products, arithmetic and copies ran while one was open for 1% of the time, Pallas kernels for 3%

profile of v5, /device:TPU:8, one launch (start us, length us, event | category | flops | bytes accessed | tf_op | source)
XLA Modules:
  0.0 92.8 jit_solution(11016979248032651130)
XLA Ops:
  0.0 8.5 %collective-permute-start.1 = (f32[3,2,48,128]{3,2,1,0:T(8,128)}, f32[3,2,48,128]{3,2,1,0:T(8,128)S(1)}, u32[]{:S(2)}, u32[]{:S(2)}) collective-permute-start(f32[3,2,48,128]{3,2,1,0:T(8,128)} %bitcast.22), channel_id=1, source_target_pairs={{1,0},{2,1},{3,2},{4,3},{5,4},{6,5},{7,6},{8,7},{9,8},{10,9},{11,1... | collective-permute-start | bytes 442376 | tf_op jit(solution)/shard_map/ppermute | solution.py:424
  8.5 0.0 collective-permute-start
  8.5 0.0 copy-start
  8.5 0.9 %copy-done = f32[1,3,2,48,128]{4,3,2,1,0:T(8,128)S(1)} copy-done((f32[1,3,2,48,128]{4,3,2,1,0:T(8,128)S(1)}, f32[1,3,2,48,128]{4,3,2,1,0:T(8,128)}, u32[]{:S(2)}) %copy-start) | copy-done | bytes 147480
  9.4 0.0 copy-start.1
  9.4 0.7 copy-done.1
  10.1 0.0 copy-start.2
  10.1 0.7 copy-done.2
  10.8 0.6 shard_map.73
  11.4 0.1 collective-permute-done.1.after
  11.5 3.0 %collective-permute-done.before = f32[3,2,48,128]{3,2,1,0:T(8,128)S(1)} collective-permute-done((f32[3,2,48,128]{3,2,1,0:T(8,128)}, f32[3,2,48,128]{3,2,1,0:T(8,128)S(1)}, u32[]{:S(2)}, u32[]{:S(2)}) %collective-permute-start) | collective-permute-done | bytes 147488 | tf_op jit(solution)/shard_map/ppermute | solution.py:423
  14.5 2.2 %shard_map.74 = (f32[384,128]{1,0:T(8,128)}, f32[3,288,128]{2,1,0:T(8,128)S(1)}) custom-call(f32[3,2,48,128]{3,2,1,0:T(8,128)S(1)} %collective-permute-done.before, f32[3,2,48,128]{3,2,1,0:T(8,128)S(1)} %get-tuple-element.16.own, f32[3,2,48,128]{3,2,1,0:T(8,128)S(1)} %collective-permute-done.1.after, s32[1,512]{1,0:T(1,128)S(1)} %bitcast.28, ...), custom_call_target="tpu_custom_call" | custom-call | tf_op jit(solution)/shard_map/pallas_call | solution.py:425
  16.7 3.5 %all-to-all-start = ((f32[16,24,128]{2,1,0:T(8,128)}), f32[16,24,128]{2,1,0:T(8,128)S(1)}, u32[]{:S(2)}, u32[]{:S(2)}) async-start(f32[16,24,128]{2,1,0:T(8,128)} %bitcast.3), calls=%async_computation | async-start | bytes 393216 | tf_op jit(solution)/shard_map/all_to_all | solution.py:428
  20.2 0.8 fusion.6
  21.0 0.0 copy-start.3
  21.0 0.0 copy-start.4
  21.0 1.1 %shard_map.75.weights = f32[4096,128]{1,0:T(8,128)S(1)} custom-call(s32[32,128]{1,0:T(8,128)S(1)} %get-tuple-element.28.code), custom_call_target="tpu_custom_call" | custom-call | tf_op jit(solution)/shard_map/pallas_call | solution.py:429
  22.1 7.9 %all-to-all-done = f32[16,24,128]{2,1,0:T(8,128)S(1)} async-done(((f32[16,24,128]{2,1,0:T(8,128)}), f32[16,24,128]{2,1,0:T(8,128)S(1)}, u32[]{:S(2)}, u32[]{:S(2)}) %all-to-all-start) | async-done | bytes 196640 | tf_op jit(solution)/shard_map/all_to_all | solution.py:428
  30.1 1.1 %shard_map.76 = f32[1312,128]{1,0:T(8,128)} custom-call(s32[1]{0:T(128)} %bitcast.5.core, f32[384,128]{1,0:T(8,128)S(1)} %bitcast.19, f32[3,2,48,128]{3,2,1,0:T(8,128)S(1)} %get-tuple-element.16.own, f32[3,288,128]{2,1,0:T(8,128)S(1)} %get-tuple-element.23.terms), custom_call_target="tpu_custom_call" | custom-call | tf_op jit(solution)/shard_map/pallas_call | solution.py:432
  31.2 10.2 %all-to-all-start.1 = ((f32[32,1,5248]{2,1,0:T(1,128)}), f32[32,1,5248]{2,1,0:T(1,128)S(1)}, u32[]{:S(2)}, u32[]{:S(2)}) async-start(f32[32,1,5248]{2,1,0:T(1,128)} %bitcast.7), calls=%async_computation.1 | async-start | bytes 1343488 | tf_op jit(solution)/shard_map/all_to_all | solution.py:393
  41.3 0.0 copy-done.3
  41.3 0.0 copy-done.4
  41.4 21.5 %all-to-all-done.1 = f32[32,1,5248]{2,1,0:T(1,128)S(1)} async-done(((f32[32,1,5248]{2,1,0:T(1,128)}), f32[32,1,5248]{2,1,0:T(1,128)S(1)}, u32[]{:S(2)}, u32[]{:S(2)}) %all-to-all-start.1) | async-done | bytes 671776 | tf_op jit(solution)/shard_map/all_to_all | solution.py:393
  62.8 0.2 shard_map.77.near
  63.1 1.9 %collective-permute-start.2 = (f32[1024,128]{1,0:T(8,128)S(1)}, f32[1024,128]{1,0:T(8,128)S(1)}, u32[]{:S(2)}, u32[]{:S(2)}) collective-permute-start(f32[1024,128]{1,0:T(8,128)S(1)} %shard_map.77.near), channel_id=1, source_target_pairs={{0,1},{1,0},{2,3},{3,2},{4,5},{5,4},{6,7},{7,6},{8,9},{9,8},{10,11... | collective-permute-start | bytes 1572872 | tf_op jit(solution)/shard_map/ppermute | solution.py:440
  65.0 0.8 shard_map.78
  65.8 1.1 %collective-permute-done.2.far = f32[1024,128]{1,0:T(8,128)S(1)} collective-permute-done((f32[1024,128]{1,0:T(8,128)S(1)}, f32[1024,128]{1,0:T(8,128)S(1)}, u32[]{:S(2)}, u32[]{:S(2)}) %collective-permute-start.2) | collective-permute-done | bytes 524320 | tf_op jit(solution)/shard_map/ppermute | solution.py:440
  66.9 9.9 %shard_map.79 = f32[288,128]{1,0:T(8,128)S(1)} custom-call(s32[4096]{0:T(1024)S(1)} %get-tuple-element.20.places, f32[4096,128]{1,0:T(8,128)S(1)} %shard_map.75.weights, f32[1024,128]{1,0:T(8,128)S(1)} %shard_map.77.near, f32[1024,128]{1,0:T(8,128)S(1)} %collective-permute-done.2.far, bf16[4,256,576]{2,1,0:T(8,128)(2,1)S(1)} %get-tuple-element.24.tiles, ...), custom_call_target="tpu_custom_call" | custom-call | tf_op jit(solution)/shard_map/pallas_call | solution.py:444
  76.8 15.3 %all_to_all.15 = f32[32,1,1152]{2,1,0:T(1,128)S(1)} all-to-all(f32[32,1,1152]{2,1,0:T(1,128)S(1)} %bitcast.20), channel_id=1, replica_groups=mesh['member'=32,'space'=16] {'member'}, dimensions={0} | all-to-all | bytes 294912 | tf_op jit(solution)/shard_map/all_to_all | solution.py:393
  92.1 0.7 shard_map.80
  (1 shorter events, 0.0 us)
Async XLA Ops:
  0.0 11.5 %collective-permute-start.1 = (f32[3,2,48,128]{3,2,1,0:T(8,128)}, f32[3,2,48,128]{3,2,1,0:T(8,128)S(1)}, u32[]{:S(2)}, u32[]{:S(2)}) collective-permute-start(f32[3,2,48,128]{3,2,1,0:T(8,128)} %bitcast.22), channel_id=1, source_target_pairs={{1,0},{2,1},{3,2},{4,3},{5,4},{6,5},{7,6},{8,7},{9,8},{10,9},{11,1... | collective-permute-start | bytes 442376 | tf_op jit(solution)/shard_map/ppermute | solution.py:424
  8.5 6.0 %collective-permute-start = (f32[3,2,48,128]{3,2,1,0:T(8,128)}, f32[3,2,48,128]{3,2,1,0:T(8,128)S(1)}, u32[]{:S(2)}, u32[]{:S(2)}) collective-permute-start(f32[3,2,48,128]{3,2,1,0:T(8,128)} %bitcast.23), channel_id=1, source_target_pairs={{0,1},{1,2},{2,3},{3,4},{4,5},{5,6},{6,7},{7,8},{8,9},{9,10},{10,1... | collective-permute-start | bytes 442376 | tf_op jit(solution)/shard_map/ppermute | solution.py:423
  8.5 0.9 %copy-start = (f32[1,3,2,48,128]{4,3,2,1,0:T(8,128)S(1)}, f32[1,3,2,48,128]{4,3,2,1,0:T(8,128)}, u32[]{:S(2)}) copy-start(f32[1,3,2,48,128]{4,3,2,1,0:T(8,128)} %param.7) | copy-start | bytes 442372
  9.4 0.7 copy-start.1
  10.1 0.7 copy-start.2
  16.7 13.4 %all-to-all-start = ((f32[16,24,128]{2,1,0:T(8,128)}), f32[16,24,128]{2,1,0:T(8,128)S(1)}, u32[]{:S(2)}, u32[]{:S(2)}) async-start(f32[16,24,128]{2,1,0:T(8,128)} %bitcast.3), calls=%async_computation | async-start | bytes 393216 | tf_op jit(solution)/shard_map/all_to_all | solution.py:428
  21.0 20.3 %copy-start.3 = (f32[8192]{0:T(1024)S(1)}, f32[8192]{0:T(1024)}, u32[]{:S(2)}) copy-start(f32[8192]{0:T(1024)} %param.11) | copy-start | bytes 98308
  21.0 20.3 %copy-start.4 = (f32[8192]{0:T(1024)S(1)}, f32[8192]{0:T(1024)}, u32[]{:S(2)}) copy-start(f32[8192]{0:T(1024)} %param.10) | copy-start | bytes 98308
  31.2 31.7 %all-to-all-start.1 = ((f32[32,1,5248]{2,1,0:T(1,128)}), f32[32,1,5248]{2,1,0:T(1,128)S(1)}, u32[]{:S(2)}, u32[]{:S(2)}) async-start(f32[32,1,5248]{2,1,0:T(1,128)} %bitcast.7), calls=%async_computation.1 | async-start | bytes 1343488 | tf_op jit(solution)/shard_map/all_to_all | solution.py:393
  63.1 3.8 %collective-permute-start.2 = (f32[1024,128]{1,0:T(8,128)S(1)}, f32[1024,128]{1,0:T(8,128)S(1)}, u32[]{:S(2)}, u32[]{:S(2)}) collective-permute-start(f32[1024,128]{1,0:T(8,128)S(1)} %shard_map.77.near), channel_id=1, source_target_pairs={{0,1},{1,0},{2,3},{3,2},{4,5},{5,4},{6,7},{7,6},{8,9},{9,8},{10,11... | collective-permute-start | bytes 1572872 | tf_op jit(solution)/shard_map/ppermute | solution.py:440

commit v6 on v5

--- a/solution.py
+++ b/solution.py
@@ -255,7 +255,7 @@
         weights[c * LOC : (c + 1) * LOC, :] = jnp.where((mark >> 4) == quarter, level, 0.0)
 
 
-def spread_kernel(received, tiles, centres, masks):
+def spread_kernel(received, tiles, centres, masks, chunks):
     tall = iota((256, 256), 0)
     wide_lane = iota((256, 256), 1)
     same = (tall // 32) == (wide_lane // 32)
@@ -272,6 +272,7 @@
     owner = iota((256, 288), 0) // 32
     chunk = (iota((256, 288), 1) % 32) // 4
     here = jnp.where(chunk == owner, 1.0, 0.0).astype(BF16)
+    chunks[...] = here
     for g in range(4):
         packed = jnp.concatenate([v[:, 32 * g : 32 * g + 32] for v in spreads], axis=1)
         h1, h2 = split2(packed)
@@ -298,7 +299,7 @@
     return (wide[K:] + dot(left1, right2)) + wide[:K]
 
 
-def analysis_kernel(places, weights, near, far, tiles, centres, masks, out, table, picked):
+def analysis_kernel(places, weights, near, far, tiles, centres, masks, chunks, out, table, picked):
     table[0:1024, :] = near[...]
     table[1024:2048, :] = far[...]
 
@@ -333,19 +334,18 @@
         push = jnp.broadcast_to(pack[K - 1 : K, :], (16, 256))
         whole = exact_times(jnp.concatenate([body, push], axis=0), rebuild)
         matrix = whole[:K] + ((K - 1) / 1.1) * eye
-        drive.append(whole[K:])
         square = jnp.broadcast_to(jnp.sum(matrix * matrix, axis=0, keepdims=True), (16, 256))
         norm = jnp.sqrt(exact_times(square, mask))
-        scale.append(norm)
-        y.append(matrix / norm[0:1])
-    for sweep in range(NS_ITERS):
+        rate = 1.0 / norm[0:1]
+        push = whole[K:]
+        both = times_blocks(jnp.concatenate([matrix, push], axis=0), matrix, mask)
+        scaled = matrix * rate
+        y.append(1.5 * scaled - (0.5 * rate * rate) * both[:K])
+        z.append(1.5 * eye - 0.5 * scaled)
+        drive.append(1.5 * push - (0.5 * rate) * both[K:])
+        scale.append(jnp.sqrt(rate))
+    for sweep in range(1, NS_ITERS):
         for g in range(count):
-            if sweep == 0:
-                factor = 1.5 * eye - 0.5 * y[g]
-                both = times_blocks(jnp.concatenate([y[g], drive[g]], axis=0), factor, mask)
-                y[g], drive[g] = both[:K], both[K:]
-                z.append(factor)
-                continue
             factor = 1.5 * eye - 0.5 * times_blocks(z[g], y[g], mask)
             if sweep == NS_ITERS - 1:
                 both = times_blocks(jnp.concatenate([z[g], drive[g]], axis=0), factor, mask)
@@ -355,13 +355,14 @@
                 y[g], z[g], drive[g] = both[:K], both[K : 2 * K], both[2 * K :]
     moved = []
     for g in range(count):
-        pull = times_blocks(drive[g], z[g], mask) / scale[g]
-        root = z[g] * (jnp.sqrt(float(K - 1)) / jnp.sqrt(scale[g][0:1]))
-        left1, left2 = split2(jnp.concatenate([root, pull], axis=0))
-        rows = left1.shape[0]
+        even = jnp.broadcast_to(scale[g] * (1.0 / K), (16, 256))
+        spot = exact_times(jnp.concatenate([eye * drive[g][0:1], even], axis=0), chunks[...])
+        pull, factor = spot[:K], spot[K : K + 1]
+        left1, left2 = split2(z[g])
         part = dot(jnp.concatenate([left1, left2], axis=0), tiles[g])
-        part = part[:rows, :288] + part[rows:, :288] + part[:rows, 288:]
-        moved.append(part[:K] + part[K : K + 1])
+        part = part[:K, :288] + part[K:, :288] + part[:K, 288:]
+        mean = jnp.sum(pull * part, axis=0, keepdims=True) * (factor * factor)
+        moved.append(part * (jnp.sqrt(float(K - 1)) * factor) + mean)
     for r in range(9):
         row = jnp.concatenate([part[:, 32 * r : 32 * r + 32] for part in moved], axis=1)
         out[pl.ds(r, K, stride=BACK), :] = row + centres[r : r + 1, :]
@@ -438,12 +439,15 @@
     received = exchange(send, "member", K)
     (near,) = call(table_kernel, [(parts * 64, 128)], [VMEM] * 3)(received, value, precision)
     far = lax.ppermute(near, "space", [(i, i ^ 1) for i in range(parts)])
-    tiles, centres, masks = call(
-        spread_kernel, [(4, 256, 576), (9, 128), (2, 256, 256)], [VMEM], kinds=[BF16, F32, BF16]
+    spread = call(
+        spread_kernel,
+        [(4, 256, 576), (9, 128), (2, 256, 256), (256, 288)],
+        [VMEM],
+        kinds=[BF16, F32, BF16, BF16],
     )(received)
     (result,) = call(
-        analysis_kernel, [(K * BACK, 128)], [SMEM] + [VMEM] * 6, SCRATCH, 32 * 2**20
-    )(places, weights, near, far, tiles, centres, masks)
+        analysis_kernel, [(K * BACK, 128)], [SMEM] + [VMEM] * 7, SCRATCH, 32 * 2**20
+    )(places, weights, near, far, *spread)
     returned = exchange(result, "member", K)
     (result,) = call(order_kernel, [(3, depth, height, extent)], [VMEM])(returned)
     return result[None]

time: 93.4 us -> 92.9 us (level)
  no operation moved by 1% of the time
where the time goes in v6:
time: 92.9 us; the launch traced here: 92.3 us
  waiting for transfers between devices  33.6 us (36%)
  starting transfers between devices  24.1 us (26%)
  Pallas kernels  16.1 us (17%)
  blocking collectives  15.3 us (16%)
  local copies, waits for them, and re-layouts  2.33 us (3%)
    all_to_all x1, waiting for transfers between devices, exchange(): sent = lax.all_to_all(rows.reshape(count, 1, width), axis, 0, 0, tiled=True)  21.5 us
    all_to_all x1, blocking collectives, exchange(): sent = lax.all_to_all(rows.reshape(count, 1, width), axis, 0, 0, tiled=True)  15.3 us
    all_to_all x1, starting transfers between devices, exchange(): sent = lax.all_to_all(rows.reshape(count, 1, width), axis, 0, 0, tiled=True)  10.2 us
    pallas_call x1, Pallas kernels, shards(): call(analysis_kernel, [(K * BACK, 128)], [SMEM] + [VMEM] * 7, SCRATCH, 32...  9.39 us
    ppermute x1, starting transfers between devices, shards(): after = lax.ppermute(field, 'space', down)  8.48 us
    all_to_all x1, waiting for transfers between devices, shards(): lax.all_to_all(message.reshape(parts, LINES, extent), 'space', 0, 0, tile...  7.9 us
    all_to_all x1, starting transfers between devices, shards(): lax.all_to_all(message.reshape(parts, LINES, extent), 'space', 0, 0, tile...  3.52 us
    ppermute x1, waiting for transfers between devices, shards(): before = lax.ppermute(field, 'space', up)  3 us
  transfers between devices with their start and end apart: 5, of which 5 were waited for; matrix products, arithmetic and copies ran while one was open for 1% of the time, Pallas kernels for 3%

profile of v6, /device:TPU:8, one launch (start us, length us, event | category | flops | bytes accessed | tf_op | source)
XLA Modules:
  0.0 92.3 jit_solution(14889257647286703040)
XLA Ops:
  0.0 8.5 %collective-permute-start.1 = (f32[3,2,48,128]{3,2,1,0:T(8,128)}, f32[3,2,48,128]{3,2,1,0:T(8,128)S(1)}, u32[]{:S(2)}, u32[]{:S(2)}) collective-permute-start(f32[3,2,48,128]{3,2,1,0:T(8,128)} %bitcast.22), channel_id=1, source_target_pairs={{1,0},{2,1},{3,2},{4,3},{5,4},{6,5},{7,6},{8,7},{9,8},{10,9},{11,1... | collective-permute-start | bytes 442376 | tf_op jit(solution)/shard_map/ppermute | solution.py:425
  8.5 0.0 collective-permute-start
  8.5 0.0 copy-start
  8.5 0.9 %copy-done = f32[1,3,2,48,128]{4,3,2,1,0:T(8,128)S(1)} copy-done((f32[1,3,2,48,128]{4,3,2,1,0:T(8,128)S(1)}, f32[1,3,2,48,128]{4,3,2,1,0:T(8,128)}, u32[]{:S(2)}) %copy-start) | copy-done | bytes 147480
  9.4 0.0 copy-start.1
  9.4 0.7 copy-done.1
  10.1 0.0 copy-start.2
  10.1 0.7 copy-done.2
  10.8 0.6 shard_map.73
  11.4 0.1 collective-permute-done.1.after
  11.5 3.0 %collective-permute-done.before = f32[3,2,48,128]{3,2,1,0:T(8,128)S(1)} collective-permute-done((f32[3,2,48,128]{3,2,1,0:T(8,128)}, f32[3,2,48,128]{3,2,1,0:T(8,128)S(1)}, u32[]{:S(2)}, u32[]{:S(2)}) %collective-permute-start) | collective-permute-done | bytes 147488 | tf_op jit(solution)/shard_map/ppermute | solution.py:424
  14.5 2.2 %shard_map.74 = (f32[384,128]{1,0:T(8,128)}, f32[3,288,128]{2,1,0:T(8,128)S(1)}) custom-call(f32[3,2,48,128]{3,2,1,0:T(8,128)S(1)} %collective-permute-done.before, f32[3,2,48,128]{3,2,1,0:T(8,128)S(1)} %get-tuple-element.17.own, f32[3,2,48,128]{3,2,1,0:T(8,128)S(1)} %collective-permute-done.1.after, s32[1,512]{1,0:T(1,128)S(1)} %bitcast.28, ...), custom_call_target="tpu_custom_call" | custom-call | tf_op jit(solution)/shard_map/pallas_call | solution.py:426
  16.7 3.5 %all-to-all-start = ((f32[16,24,128]{2,1,0:T(8,128)}), f32[16,24,128]{2,1,0:T(8,128)S(1)}, u32[]{:S(2)}, u32[]{:S(2)}) async-start(f32[16,24,128]{2,1,0:T(8,128)} %bitcast.3), calls=%async_computation | async-start | bytes 393216 | tf_op jit(solution)/shard_map/all_to_all | solution.py:429
  20.2 0.8 fusion.6
  21.0 0.0 copy-start.3
  21.0 0.0 copy-start.4
  21.0 1.1 %shard_map.75.weights = f32[4096,128]{1,0:T(8,128)S(1)} custom-call(s32[32,128]{1,0:T(8,128)S(1)} %get-tuple-element.30.code), custom_call_target="tpu_custom_call" | custom-call | tf_op jit(solution)/shard_map/pallas_call | solution.py:430
  22.1 7.9 %all-to-all-done = f32[16,24,128]{2,1,0:T(8,128)S(1)} async-done(((f32[16,24,128]{2,1,0:T(8,128)}), f32[16,24,128]{2,1,0:T(8,128)S(1)}, u32[]{:S(2)}, u32[]{:S(2)}) %all-to-all-start) | async-done | bytes 196640 | tf_op jit(solution)/shard_map/all_to_all | solution.py:429
  30.1 1.1 %shard_map.76 = f32[1312,128]{1,0:T(8,128)} custom-call(s32[1]{0:T(128)} %bitcast.5.core, f32[384,128]{1,0:T(8,128)S(1)} %bitcast.19, f32[3,2,48,128]{3,2,1,0:T(8,128)S(1)} %get-tuple-element.17.own, f32[3,288,128]{2,1,0:T(8,128)S(1)} %get-tuple-element.24.terms), custom_call_target="tpu_custom_call" | custom-call | tf_op jit(solution)/shard_map/pallas_call | solution.py:433
  31.2 10.2 %all-to-all-start.1 = ((f32[32,1,5248]{2,1,0:T(1,128)}), f32[32,1,5248]{2,1,0:T(1,128)S(1)}, u32[]{:S(2)}, u32[]{:S(2)}) async-start(f32[32,1,5248]{2,1,0:T(1,128)} %bitcast.7), calls=%async_computation.1 | async-start | bytes 1343488 | tf_op jit(solution)/shard_map/all_to_all | solution.py:394
  41.3 0.0 copy-done.3
  41.3 0.0 copy-done.4
  41.4 21.5 %all-to-all-done.1 = f32[32,1,5248]{2,1,0:T(1,128)S(1)} async-done(((f32[32,1,5248]{2,1,0:T(1,128)}), f32[32,1,5248]{2,1,0:T(1,128)S(1)}, u32[]{:S(2)}, u32[]{:S(2)}) %all-to-all-start.1) | async-done | bytes 671776 | tf_op jit(solution)/shard_map/all_to_all | solution.py:394
  62.8 0.2 shard_map.77.near
  63.1 1.9 %collective-permute-start.2 = (f32[1024,128]{1,0:T(8,128)S(1)}, f32[1024,128]{1,0:T(8,128)S(1)}, u32[]{:S(2)}, u32[]{:S(2)}) collective-permute-start(f32[1024,128]{1,0:T(8,128)S(1)} %shard_map.77.near), channel_id=1, source_target_pairs={{0,1},{1,0},{2,3},{3,2},{4,5},{5,4},{6,7},{7,6},{8,9},{9,8},{10,11... | collective-permute-start | bytes 1572872 | tf_op jit(solution)/shard_map/ppermute | solution.py:441
  65.0 0.8 shard_map.78
  65.8 1.1 %collective-permute-done.2.far = f32[1024,128]{1,0:T(8,128)S(1)} collective-permute-done((f32[1024,128]{1,0:T(8,128)S(1)}, f32[1024,128]{1,0:T(8,128)S(1)}, u32[]{:S(2)}, u32[]{:S(2)}) %collective-permute-start.2) | collective-permute-done | bytes 524320 | tf_op jit(solution)/shard_map/ppermute | solution.py:441
  66.9 9.4 %shard_map.79 = f32[288,128]{1,0:T(8,128)S(1)} custom-call(s32[4096]{0:T(1024)S(1)} %get-tuple-element.21.places, f32[4096,128]{1,0:T(8,128)S(1)} %shard_map.75.weights, f32[1024,128]{1,0:T(8,128)S(1)} %shard_map.77.near, f32[1024,128]{1,0:T(8,128)S(1)} %collective-permute-done.2.far, bf16[4,256,576]{2,1,0:T(8,128)(2,1)S(1)} %get-tuple-element.25.tiles, ...), custom_call_target="tpu_custom_call" | custom-call | tf_op jit(solution)/shard_map/pallas_call | solution.py:448
  76.3 15.3 %all_to_all.15 = f32[32,1,1152]{2,1,0:T(1,128)S(1)} all-to-all(f32[32,1,1152]{2,1,0:T(1,128)S(1)} %bitcast.20), channel_id=1, replica_groups=mesh['member'=32,'space'=16] {'member'}, dimensions={0} | all-to-all | bytes 294912 | tf_op jit(solution)/shard_map/all_to_all | solution.py:394
  91.6 0.7 shard_map.80
  (1 shorter events, 0.0 us)
Async XLA Ops:
  0.0 11.5 %collective-permute-start.1 = (f32[3,2,48,128]{3,2,1,0:T(8,128)}, f32[3,2,48,128]{3,2,1,0:T(8,128)S(1)}, u32[]{:S(2)}, u32[]{:S(2)}) collective-permute-start(f32[3,2,48,128]{3,2,1,0:T(8,128)} %bitcast.22), channel_id=1, source_target_pairs={{1,0},{2,1},{3,2},{4,3},{5,4},{6,5},{7,6},{8,7},{9,8},{10,9},{11,1... | collective-permute-start | bytes 442376 | tf_op jit(solution)/shard_map/ppermute | solution.py:425
  8.5 6.0 %collective-permute-start = (f32[3,2,48,128]{3,2,1,0:T(8,128)}, f32[3,2,48,128]{3,2,1,0:T(8,128)S(1)}, u32[]{:S(2)}, u32[]{:S(2)}) collective-permute-start(f32[3,2,48,128]{3,2,1,0:T(8,128)} %bitcast.23), channel_id=1, source_target_pairs={{0,1},{1,2},{2,3},{3,4},{4,5},{5,6},{6,7},{7,8},{8,9},{9,10},{10,1... | collective-permute-start | bytes 442376 | tf_op jit(solution)/shard_map/ppermute | solution.py:424
  8.5 0.9 %copy-start = (f32[1,3,2,48,128]{4,3,2,1,0:T(8,128)S(1)}, f32[1,3,2,48,128]{4,3,2,1,0:T(8,128)}, u32[]{:S(2)}) copy-start(f32[1,3,2,48,128]{4,3,2,1,0:T(8,128)} %param.7) | copy-start | bytes 442372
  9.4 0.7 copy-start.1
  10.1 0.7 copy-start.2
  16.7 13.4 %all-to-all-start = ((f32[16,24,128]{2,1,0:T(8,128)}), f32[16,24,128]{2,1,0:T(8,128)S(1)}, u32[]{:S(2)}, u32[]{:S(2)}) async-start(f32[16,24,128]{2,1,0:T(8,128)} %bitcast.3), calls=%async_computation | async-start | bytes 393216 | tf_op jit(solution)/shard_map/all_to_all | solution.py:429
  21.0 20.3 %copy-start.3 = (f32[8192]{0:T(1024)S(1)}, f32[8192]{0:T(1024)}, u32[]{:S(2)}) copy-start(f32[8192]{0:T(1024)} %param.11) | copy-start | bytes 98308
  21.0 20.3 %copy-start.4 = (f32[8192]{0:T(1024)S(1)}, f32[8192]{0:T(1024)}, u32[]{:S(2)}) copy-start(f32[8192]{0:T(1024)} %param.10) | copy-start | bytes 98308
  31.2 31.7 %all-to-all-start.1 = ((f32[32,1,5248]{2,1,0:T(1,128)}), f32[32,1,5248]{2,1,0:T(1,128)S(1)}, u32[]{:S(2)}, u32[]{:S(2)}) async-start(f32[32,1,5248]{2,1,0:T(1,128)} %bitcast.7), calls=%async_computation.1 | async-start | bytes 1343488 | tf_op jit(solution)/shard_map/all_to_all | solution.py:394
  63.1 3.8 %collective-permute-start.2 = (f32[1024,128]{1,0:T(8,128)S(1)}, f32[1024,128]{1,0:T(8,128)S(1)}, u32[]{:S(2)}, u32[]{:S(2)}) collective-permute-start(f32[1024,128]{1,0:T(8,128)S(1)} %shard_map.77.near), channel_id=1, source_target_pairs={{0,1},{1,0},{2,3},{3,2},{4,5},{5,4},{6,7},{7,6},{8,9},{9,8},{10,11... | collective-permute-start | bytes 1572872 | tf_op jit(solution)/shard_map/ppermute | solution.py:441

commit v7 on v6

--- a/solution.py
+++ b/solution.py
@@ -428,7 +428,9 @@
     )(before, own, after, cell, chosen, ready)
     message = lax.all_to_all(message.reshape(parts, LINES, extent), "space", 0, 0, tiled=True)
     (weights,) = call(weight_kernel, [(CHUNKS * LOC, 128)], [VMEM])(code)
-    message, weights, places = lax.optimization_barrier((message, weights, places))
+    message, weights, places, value, precision = lax.optimization_barrier(
+        (message, weights, places, value, precision)
+    )
     message = message.reshape(parts * LINES, extent)
     (send,) = call(
         functools.partial(forecast_kernel, depth * parts * extent),

time: 92.9 us -> 90.5 us (0.974)
  blocking collectives: 15.3 us -> 46.8 us
  waiting for transfers between devices: 33.6 us -> 9.22 us
  starting transfers between devices: 24.1 us -> 15.5 us
    all_to_all x1 -> x2, blocking collectives: 15.3 us -> 46.8 us  [exchange(): sent = lax.all_to_all(rows.reshape(count, 1, width), axis, 0, 0, tiled=True)]
    all_to_all x1 -> x0, waiting for transfers between devices: 21.5 us -> none  [exchange(): sent = lax.all_to_all(rows.reshape(count, 1, width), axis, 0, 0, tiled=True)]
    all_to_all x1 -> x0, starting transfers between devices: 10.2 us -> none  [exchange(): sent = lax.all_to_all(rows.reshape(count, 1, width), axis, 0, 0, tiled=True)]
    ppermute x1, waiting for transfers between devices: 3 us -> 0.1 us  [shards(): before = lax.ppermute(field, 'space', up)]
    all_to_all x1, starting transfers between devices: 3.52 us -> 5.14 us  [shards(): lax.all_to_all(message.reshape(parts, LINES, extent), 'space', 0, 0, tile...]
  transfers between devices with their start and end apart: 5 -> 4, of which waited for: 5 -> 3; matrix products, arithmetic and copies ran while one was open for 1% -> 1% of each run, Pallas kernels for 3% -> 3%
where the time goes in v7:
time: 90.5 us; the launch traced here: 90 us
  blocking collectives  46.8 us (52%)
  starting transfers between devices  15.5 us (17%)
  Pallas kernels  15.3 us (17%)
  waiting for transfers between devices  9.22 us (10%)
  local copies, waits for them, and re-layouts  2.33 us (3%)
    all_to_all x2, blocking collectives, exchange(): sent = lax.all_to_all(rows.reshape(count, 1, width), axis, 0, 0, tiled=True)  46.8 us
    pallas_call x1, Pallas kernels, shards(): call(analysis_kernel, [(K * BACK, 128)], [SMEM] + [VMEM] * 7, SCRATCH, 32...  9.38 us
    ppermute x1, starting transfers between devices, shards(): after = lax.ppermute(field, 'space', down)  8.48 us
    all_to_all x1, waiting for transfers between devices, shards(): lax.all_to_all(message.reshape(parts, LINES, extent), 'space', 0, 0, tile...  8.01 us
    all_to_all x1, starting transfers between devices, shards(): lax.all_to_all(message.reshape(parts, LINES, extent), 'space', 0, 0, tile...  5.14 us
    unnamed x10, local copies, waits for them, and re-layouts  2.31 us
    pallas_call x1, Pallas kernels, shards(): call(model_kernel, [(parts * LINES, 128), (3, 3 * depth * height, extent)...  2.24 us
    ppermute x1, starting transfers between devices, shards(): far = lax.ppermute(near, 'space', [(i, i ^ 1) for i in range(parts)])  1.92 us
  transfers between devices with their start and end apart: 4, of which 3 were waited for; matrix products, arithmetic and copies ran while one was open for 1% of the time, Pallas kernels for 3%

profile of v7, /device:TPU:8, one launch (start us, length us, event | category | flops | bytes accessed | tf_op | source)
XLA Modules:
  0.0 90.0 jit_solution(5276253149810905766)
XLA Ops:
  0.0 0.0 collective-permute-start
  0.0 8.5 %collective-permute-start.1 = (f32[3,2,48,128]{3,2,1,0:T(8,128)}, f32[3,2,48,128]{3,2,1,0:T(8,128)S(1)}, u32[]{:S(2)}, u32[]{:S(2)}) collective-permute-start(f32[3,2,48,128]{3,2,1,0:T(8,128)} %bitcast.24), channel_id=1, source_target_pairs={{1,0},{2,1},{3,2},{4,3},{5,4},{6,5},{7,6},{8,7},{9,8},{10,9},{11,1... | collective-permute-start | bytes 442376 | tf_op jit(solution)/shard_map/ppermute | solution.py:425
  8.5 0.0 copy-start
  8.5 0.9 %copy-done = f32[1,3,2,48,128]{4,3,2,1,0:T(8,128)S(1)} copy-done((f32[1,3,2,48,128]{4,3,2,1,0:T(8,128)S(1)}, f32[1,3,2,48,128]{4,3,2,1,0:T(8,128)}, u32[]{:S(2)}) %copy-start) | copy-done | bytes 147480
  9.4 0.0 copy-start.1
  9.4 0.7 copy-done.1
  10.1 0.0 copy-start.2
  10.1 0.7 copy-done.2
  10.8 0.0 copy-start.3
  10.8 0.0 copy-start.4
  10.8 0.6 shard_map.73
  11.4 0.1 collective-permute-done.before
  11.5 0.0 collective-permute-done.1.after
  11.5 2.2 %shard_map.74 = (f32[384,128]{1,0:T(8,128)}, f32[3,288,128]{2,1,0:T(8,128)S(1)}) custom-call(f32[3,2,48,128]{3,2,1,0:T(8,128)S(1)} %collective-permute-done.before, f32[3,2,48,128]{3,2,1,0:T(8,128)S(1)} %get-tuple-element.19.own, f32[3,2,48,128]{3,2,1,0:T(8,128)S(1)} %collective-permute-done.1.after, s32[1,512]{1,0:T(1,128)S(1)} %bitcast.29, ...), custom_call_target="tpu_custom_call" | custom-call | tf_op jit(solution)/shard_map/pallas_call | solution.py:426
  13.8 5.1 %all-to-all-start = ((f32[16,24,128]{2,1,0:T(8,128)}), f32[16,24,128]{2,1,0:T(8,128)S(1)}, u32[]{:S(2)}, u32[]{:S(2)}) async-start(f32[16,24,128]{2,1,0:T(8,128)} %bitcast.3), calls=%async_computation | async-start | bytes 393216 | tf_op jit(solution)/shard_map/all_to_all | solution.py:429
  18.9 0.8 fusion.6
  19.7 1.1 %shard_map.75.weights = f32[4096,128]{1,0:T(8,128)S(1)} custom-call(s32[32,128]{1,0:T(8,128)S(1)} %get-tuple-element.34.code), custom_call_target="tpu_custom_call" | custom-call | tf_op jit(solution)/shard_map/pallas_call | solution.py:430
  20.8 0.0 copy-done.3
  20.8 0.0 copy-done.4
  20.8 8.0 %all-to-all-done = f32[16,24,128]{2,1,0:T(8,128)S(1)} async-done(((f32[16,24,128]{2,1,0:T(8,128)}), f32[16,24,128]{2,1,0:T(8,128)S(1)}, u32[]{:S(2)}, u32[]{:S(2)}) %all-to-all-start) | async-done | bytes 196640 | tf_op jit(solution)/shard_map/all_to_all | solution.py:429
  28.9 0.3 shard_map.76
  29.1 31.4 %all_to_all.15 = f32[32,1,5248]{2,1,0:T(1,128)S(1)} all-to-all(f32[32,1,5248]{2,1,0:T(1,128)S(1)} %bitcast.19), channel_id=1, replica_groups=mesh['member'=32,'space'=16] {'member'}, dimensions={0} | all-to-all | bytes 1343488 | tf_op jit(solution)/shard_map/all_to_all | solution.py:394
  60.6 0.2 shard_map.77.near
  60.8 1.9 %collective-permute-start.2 = (f32[1024,128]{1,0:T(8,128)S(1)}, f32[1024,128]{1,0:T(8,128)S(1)}, u32[]{:S(2)}, u32[]{:S(2)}) collective-permute-start(f32[1024,128]{1,0:T(8,128)S(1)} %shard_map.77.near), channel_id=1, source_target_pairs={{0,1},{1,0},{2,3},{3,2},{4,5},{5,4},{6,7},{7,6},{8,9},{9,8},{10,11... | collective-permute-start | bytes 1572872 | tf_op jit(solution)/shard_map/ppermute | solution.py:443
  62.7 0.8 shard_map.78
  63.5 1.1 %collective-permute-done.2.far = f32[1024,128]{1,0:T(8,128)S(1)} collective-permute-done((f32[1024,128]{1,0:T(8,128)S(1)}, f32[1024,128]{1,0:T(8,128)S(1)}, u32[]{:S(2)}, u32[]{:S(2)}) %collective-permute-start.2) | collective-permute-done | bytes 524320 | tf_op jit(solution)/shard_map/ppermute | solution.py:443
  64.6 9.4 %shard_map.79 = f32[288,128]{1,0:T(8,128)S(1)} custom-call(s32[4096]{0:T(1024)S(1)} %get-tuple-element.23.places, f32[4096,128]{1,0:T(8,128)S(1)} %shard_map.75.weights, f32[1024,128]{1,0:T(8,128)S(1)} %shard_map.77.near, f32[1024,128]{1,0:T(8,128)S(1)} %collective-permute-done.2.far, bf16[4,256,576]{2,1,0:T(8,128)(2,1)S(1)} %get-tuple-element.29.tiles, ...), custom_call_target="tpu_custom_call" | custom-call | tf_op jit(solution)/shard_map/pallas_call | solution.py:450
  74.0 15.3 %all_to_all.16 = f32[32,1,1152]{2,1,0:T(1,128)S(1)} all-to-all(f32[32,1,1152]{2,1,0:T(1,128)S(1)} %bitcast.21), channel_id=1, replica_groups=mesh['member'=32,'space'=16] {'member'}, dimensions={0} | all-to-all | bytes 294912 | tf_op jit(solution)/shard_map/all_to_all | solution.py:394
  89.3 0.7 shard_map.80
  (1 shorter events, 0.0 us)
Async XLA Ops:
  0.0 11.5 %collective-permute-start = (f32[3,2,48,128]{3,2,1,0:T(8,128)}, f32[3,2,48,128]{3,2,1,0:T(8,128)S(1)}, u32[]{:S(2)}, u32[]{:S(2)}) collective-permute-start(f32[3,2,48,128]{3,2,1,0:T(8,128)} %bitcast.23), channel_id=1, source_target_pairs={{0,1},{1,2},{2,3},{3,4},{4,5},{5,6},{6,7},{7,8},{8,9},{9,10},{10,1... | collective-permute-start | bytes 442376 | tf_op jit(solution)/shard_map/ppermute | solution.py:424
  0.0 11.5 %collective-permute-start.1 = (f32[3,2,48,128]{3,2,1,0:T(8,128)}, f32[3,2,48,128]{3,2,1,0:T(8,128)S(1)}, u32[]{:S(2)}, u32[]{:S(2)}) collective-permute-start(f32[3,2,48,128]{3,2,1,0:T(8,128)} %bitcast.24), channel_id=1, source_target_pairs={{1,0},{2,1},{3,2},{4,3},{5,4},{6,5},{7,6},{8,7},{9,8},{10,9},{11,1... | collective-permute-start | bytes 442376 | tf_op jit(solution)/shard_map/ppermute | solution.py:425
  8.5 0.9 %copy-start = (f32[1,3,2,48,128]{4,3,2,1,0:T(8,128)S(1)}, f32[1,3,2,48,128]{4,3,2,1,0:T(8,128)}, u32[]{:S(2)}) copy-start(f32[1,3,2,48,128]{4,3,2,1,0:T(8,128)} %param.7) | copy-start | bytes 442372
  9.4 0.7 copy-start.1
  10.1 0.7 copy-start.2
  10.8 10.0 %copy-start.3 = (f32[8192]{0:T(1024)S(1)}, f32[8192]{0:T(1024)}, u32[]{:S(2)}) copy-start(f32[8192]{0:T(1024)} %param.11) | copy-start | bytes 98308
  10.8 10.0 %copy-start.4 = (f32[8192]{0:T(1024)S(1)}, f32[8192]{0:T(1024)}, u32[]{:S(2)}) copy-start(f32[8192]{0:T(1024)} %param.10) | copy-start | bytes 98308
  13.8 15.1 %all-to-all-start = ((f32[16,24,128]{2,1,0:T(8,128)}), f32[16,24,128]{2,1,0:T(8,128)S(1)}, u32[]{:S(2)}, u32[]{:S(2)}) async-start(f32[16,24,128]{2,1,0:T(8,128)} %bitcast.3), calls=%async_computation | async-start | bytes 393216 | tf_op jit(solution)/shard_map/all_to_all | solution.py:429
  60.8 3.8 %collective-permute-start.2 = (f32[1024,128]{1,0:T(8,128)S(1)}, f32[1024,128]{1,0:T(8,128)S(1)}, u32[]{:S(2)}, u32[]{:S(2)}) collective-permute-start(f32[1024,128]{1,0:T(8,128)S(1)} %shard_map.77.near), channel_id=1, source_target_pairs={{0,1},{1,0},{2,3},{3,2},{4,5},{5,4},{6,7},{7,6},{8,9},{9,8},{10,11... | collective-permute-start | bytes 1572872 | tf_op jit(solution)/shard_map/ppermute | solution.py:443

commit v8 on v6

--- a/solution.py
+++ b/solution.py
@@ -423,12 +423,14 @@
     )(field, cell, obs_comp.reshape(1, 512))
     before = lax.ppermute(field, "space", up)
     after = lax.ppermute(field, "space", down)
+    (weights,) = call(weight_kernel, [(CHUNKS * LOC, 128)], [VMEM])(code)
+    own, weights, places, value, precision, core = lax.optimization_barrier(
+        (own, weights, places, value, precision, core)
+    )
     message, terms = call(
         model_kernel, [(parts * LINES, 128), (3, 3 * depth * height, extent)], [VMEM] * 6
     )(before, own, after, cell, chosen, ready)
     message = lax.all_to_all(message.reshape(parts, LINES, extent), "space", 0, 0, tiled=True)
-    (weights,) = call(weight_kernel, [(CHUNKS * LOC, 128)], [VMEM])(code)
-    message, weights, places = lax.optimization_barrier((message, weights, places))
     message = message.reshape(parts * LINES, extent)
     (send,) = call(
         functools.partial(forecast_kernel, depth * parts * extent),

time: 92.9 us -> 89.4 us (0.962)
  blocking collectives: 15.3 us -> 61.7 us
  waiting for transfers between devices: 33.6 us -> 1.55 us
  starting transfers between devices: 24.1 us -> 10.4 us
  local copies, waits for them, and re-layouts: 2.33 us -> 0.04 us
  Pallas kernels: 16.1 us -> 14.6 us
    all_to_all x1 -> x2, blocking collectives: 15.3 us -> 46.8 us  [exchange(): sent = lax.all_to_all(rows.reshape(count, 1, width), axis, 0, 0, tiled=True)]
    all_to_all x2 -> x0, waiting for transfers between devices: 29.4 us -> none  [the longest x1 21.5 us: exchange(): sent = lax.all_to_all(rows.reshape(count, 1, width), axis, 0, 0, tiled=True)]
    all_to_all x0 -> x1, blocking collectives: none -> 14.9 us  [shards(): lax.all_to_all(message.reshape(parts, LINES, extent), 'space', 0, 0, tile...]
    all_to_all x2 -> x0, starting transfers between devices: 13.7 us -> none  [the longest x1 10.2 us: exchange(): sent = lax.all_to_all(rows.reshape(count, 1, width), axis, 0, 0, tiled=True)]
    ppermute x1, waiting for transfers between devices: 3 us -> 0.43 us  [shards(): before = lax.ppermute(field, 'space', up)]
    unnamed x10, local copies, waits for them, and re-layouts: 2.31 us -> 0.02 us
  transfers between devices with their start and end apart: 5 -> 3, of which waited for: 5 -> 2; matrix products, arithmetic and copies ran while one was open for 1% -> 1% of each run, Pallas kernels for 3% -> 3%
where the time goes in v8:
time: 89.4 us; the launch traced here: 89.1 us
  blocking collectives  61.7 us (69%)
  Pallas kernels  14.6 us (16%)
  starting transfers between devices  10.4 us (12%)
  waiting for transfers between devices  1.55 us (2%)
    all_to_all x2, blocking collectives, exchange(): sent = lax.all_to_all(rows.reshape(count, 1, width), axis, 0, 0, tiled=True)  46.8 us
    all_to_all x1, blocking collectives, shards(): lax.all_to_all(message.reshape(parts, LINES, extent), 'space', 0, 0, tile...  14.9 us
    pallas_call x1, Pallas kernels, shards(): call(analysis_kernel, [(K * BACK, 128)], [SMEM] + [VMEM] * 7, SCRATCH, 32...  9.37 us
    ppermute x1, starting transfers between devices, shards(): after = lax.ppermute(field, 'space', down)  8.49 us
    ppermute x1, starting transfers between devices, shards(): far = lax.ppermute(near, 'space', [(i, i ^ 1) for i in range(parts)])  1.92 us
  transfers between devices with their start and end apart: 3, of which 2 were waited for; matrix products, arithmetic and copies ran while one was open for 1% of the time, Pallas kernels for 3%

profile of v8, /device:TPU:8, one launch (start us, length us, event | category | flops | bytes accessed | tf_op | source)
XLA Modules:
  0.0 89.1 jit_solution(9470760854009424784)
XLA Ops:
  0.0 0.0 copy-start
  0.0 0.0 copy-start.1
  0.0 0.0 copy-start.2
  0.0 0.0 copy-start.4
  0.0 0.0 copy-start.3
  0.0 0.0 collective-permute-start
  0.1 8.5 %collective-permute-start.1 = (f32[3,2,48,128]{3,2,1,0:T(8,128)}, f32[3,2,48,128]{3,2,1,0:T(8,128)S(1)}, u32[]{:S(2)}, u32[]{:S(2)}) collective-permute-start(f32[3,2,48,128]{3,2,1,0:T(8,128)} %bitcast.25), channel_id=1, source_target_pairs={{1,0},{2,1},{3,2},{4,3},{5,4},{6,5},{7,6},{8,7},{9,8},{10,9},{11,1... | collective-permute-start | bytes 442376 | tf_op jit(solution)/shard_map/ppermute | solution.py:425
  8.5 0.8 fusion.6
  9.3 1.1 %shard_map.74.weights = f32[4096,128]{1,0:T(8,128)S(1)} custom-call(s32[32,128]{1,0:T(8,128)S(1)} %get-tuple-element.36.code), custom_call_target="tpu_custom_call" | custom-call | tf_op jit(solution)/shard_map/pallas_call | solution.py:426
  10.4 0.0 copy-done
  10.5 0.0 copy-done.1
  10.5 0.0 copy-done.2
  10.5 0.6 shard_map.73
  11.1 0.0 copy-done.4
  11.1 0.0 copy-done.3
  11.2 0.4 collective-permute-done.before
  11.6 0.0 collective-permute-done.1.after
  11.6 1.5 %shard_map.75 = (f32[384,128]{1,0:T(8,128)S(1)}, f32[3,288,128]{2,1,0:T(8,128)S(1)}) custom-call(f32[3,2,48,128]{3,2,1,0:T(8,128)S(1)} %collective-permute-done.before, f32[3,2,48,128]{3,2,1,0:T(8,128)S(1)} %get-tuple-element.24.own, f32[3,2,48,128]{3,2,1,0:T(8,128)S(1)} %collective-permute-done.1.after, s32[1,512]{1,0:T(1,128)S(1)} %bitcast.30, ...), custom_call_target="tpu_custom_call" | custom-call | tf_op jit(solution)/shard_map/pallas_call | solution.py:430
  13.1 14.9 %all_to_all.15 = f32[16,24,128]{2,1,0:T(8,128)S(1)} all-to-all(f32[16,24,128]{2,1,0:T(8,128)S(1)} %bitcast.23), channel_id=1, replica_groups=mesh['member'=32,'space'=16] {'space'}, dimensions={0} | all-to-all | bytes 393216 | tf_op jit(solution)/shard_map/all_to_all | solution.py:433
  28.0 0.3 shard_map.76
  28.3 31.4 %all_to_all.16 = f32[32,1,5248]{2,1,0:T(1,128)S(1)} all-to-all(f32[32,1,5248]{2,1,0:T(1,128)S(1)} %bitcast.19), channel_id=1, replica_groups=mesh['member'=32,'space'=16] {'member'}, dimensions={0} | all-to-all | bytes 1343488 | tf_op jit(solution)/shard_map/all_to_all | solution.py:394
  59.7 0.2 shard_map.77.near
  59.9 1.9 %collective-permute-start.2 = (f32[1024,128]{1,0:T(8,128)S(1)}, f32[1024,128]{1,0:T(8,128)S(1)}, u32[]{:S(2)}, u32[]{:S(2)}) collective-permute-start(f32[1024,128]{1,0:T(8,128)S(1)} %shard_map.77.near), channel_id=1, source_target_pairs={{0,1},{1,0},{2,3},{3,2},{4,5},{5,4},{6,7},{7,6},{8,9},{9,8},{10,11... | collective-permute-start | bytes 1572872 | tf_op jit(solution)/shard_map/ppermute | solution.py:443
  61.8 0.8 shard_map.78
  62.6 1.1 %collective-permute-done.2.far = f32[1024,128]{1,0:T(8,128)S(1)} collective-permute-done((f32[1024,128]{1,0:T(8,128)S(1)}, f32[1024,128]{1,0:T(8,128)S(1)}, u32[]{:S(2)}, u32[]{:S(2)}) %collective-permute-start.2) | collective-permute-done | bytes 524320 | tf_op jit(solution)/shard_map/ppermute | solution.py:443
  63.7 9.4 %shard_map.79 = f32[288,128]{1,0:T(8,128)S(1)} custom-call(s32[4096]{0:T(1024)S(1)} %get-tuple-element.21.places, f32[4096,128]{1,0:T(8,128)S(1)} %shard_map.74.weights, f32[1024,128]{1,0:T(8,128)S(1)} %shard_map.77.near, f32[1024,128]{1,0:T(8,128)S(1)} %collective-permute-done.2.far, bf16[4,256,576]{2,1,0:T(8,128)(2,1)S(1)} %get-tuple-element.31.tiles, ...), custom_call_target="tpu_custom_call" | custom-call | tf_op jit(solution)/shard_map/pallas_call | solution.py:450
  73.1 15.3 %all_to_all.17 = f32[32,1,1152]{2,1,0:T(1,128)S(1)} all-to-all(f32[32,1,1152]{2,1,0:T(1,128)S(1)} %bitcast.21), channel_id=1, replica_groups=mesh['member'=32,'space'=16] {'member'}, dimensions={0} | all-to-all | bytes 294912 | tf_op jit(solution)/shard_map/all_to_all | solution.py:394
  88.4 0.7 shard_map.80
  (1 shorter events, 0.0 us)
Async XLA Ops:
  0.0 10.4 %copy-start = (f32[1,3,2,48,128]{4,3,2,1,0:T(8,128)S(1)}, f32[1,3,2,48,128]{4,3,2,1,0:T(8,128)}, u32[]{:S(2)}) copy-start(f32[1,3,2,48,128]{4,3,2,1,0:T(8,128)} %param.7) | copy-start | bytes 442372
  0.0 10.5 %copy-start.1 = (s32[512]{0:T(512)S(1)}, s32[512]{0:T(512)}, u32[]{:S(2)}) copy-start(s32[512]{0:T(512)} %param.8) | copy-start | bytes 6148
  0.0 10.5 %copy-start.2 = (s32[512]{0:T(512)S(1)}, s32[512]{0:T(512)}, u32[]{:S(2)}) copy-start(s32[512]{0:T(512)} %param.9) | copy-start | bytes 6148
  0.0 11.1 %copy-start.4 = (f32[8192]{0:T(1024)S(1)}, f32[8192]{0:T(1024)}, u32[]{:S(2)}) copy-start(f32[8192]{0:T(1024)} %param.10) | copy-start | bytes 98308
  0.0 11.1 %copy-start.3 = (f32[8192]{0:T(1024)S(1)}, f32[8192]{0:T(1024)}, u32[]{:S(2)}) copy-start(f32[8192]{0:T(1024)} %param.11) | copy-start | bytes 98308
  0.0 11.6 %collective-permute-start = (f32[3,2,48,128]{3,2,1,0:T(8,128)}, f32[3,2,48,128]{3,2,1,0:T(8,128)S(1)}, u32[]{:S(2)}, u32[]{:S(2)}) collective-permute-start(f32[3,2,48,128]{3,2,1,0:T(8,128)} %bitcast.24), channel_id=1, source_target_pairs={{0,1},{1,2},{2,3},{3,4},{4,5},{5,6},{6,7},{7,8},{8,9},{9,10},{10,1... | collective-permute-start | bytes 442376 | tf_op jit(solution)/shard_map/ppermute | solution.py:424
  0.1 11.5 %collective-permute-start.1 = (f32[3,2,48,128]{3,2,1,0:T(8,128)}, f32[3,2,48,128]{3,2,1,0:T(8,128)S(1)}, u32[]{:S(2)}, u32[]{:S(2)}) collective-permute-start(f32[3,2,48,128]{3,2,1,0:T(8,128)} %bitcast.25), channel_id=1, source_target_pairs={{1,0},{2,1},{3,2},{4,3},{5,4},{6,5},{7,6},{8,7},{9,8},{10,9},{11,1... | collective-permute-start | bytes 442376 | tf_op jit(solution)/shard_map/ppermute | solution.py:425
  59.9 3.8 %collective-permute-start.2 = (f32[1024,128]{1,0:T(8,128)S(1)}, f32[1024,128]{1,0:T(8,128)S(1)}, u32[]{:S(2)}, u32[]{:S(2)}) collective-permute-start(f32[1024,128]{1,0:T(8,128)S(1)} %shard_map.77.near), channel_id=1, source_target_pairs={{0,1},{1,0},{2,3},{3,2},{4,5},{5,4},{6,7},{7,6},{8,9},{9,8},{10,11... | collective-permute-start | bytes 1572872 | tf_op jit(solution)/shard_map/ppermute | solution.py:443

commit v9 on v8

--- a/solution.py
+++ b/solution.py
@@ -305,11 +305,15 @@
 
     quarter = iota((LOC, 128), 1) // 32
 
+    half = CHUNKS * LOC // 2
+
     def fetch(at, carry):
-        picked[pl.ds(at, 1), :] = table[pl.ds(places[at], 1), :]
+        both = places[at]
+        picked[pl.ds(at, 1), :] = table[pl.ds(both & 65535, 1), :]
+        picked[pl.ds(at + half, 1), :] = table[pl.ds(both >> 16, 1), :]
         return carry
 
-    lax.fori_loop(0, CHUNKS * LOC, fetch, 0, unroll=True)
+    lax.fori_loop(0, half, fetch, 0, unroll=True)
     grams = []
     for four in range(CHUNKS // 4):
         pack = None
@@ -406,7 +410,7 @@
     slab = loc_obs // 512
     within = loc_obs % 512
     places = (slab // 2) * 128 + ((slab + here) % 2) * 1024 + within % 128
-    places = places.reshape(CHUNKS * LOC)
+    places = (places[: CHUNKS // 2] + places[CHUNKS // 2 :] * 65536).reshape(CHUNKS * LOC // 2)
     code = (within // 128) * 16 + loc_level
     core = here & 1
     value = lax.dynamic_index_in_dim(obs_value.reshape(parts // 2, 2, 4, 128), core, 1, keepdims=False)

time: 89.4 us -> 90.3 us (1.010)
  no operation moved by 1% of the time
where the time goes in v9:
time: 90.3 us; the launch traced here: 90 us
  blocking collectives  61.6 us (68%)
  Pallas kernels  15.5 us (17%)
  starting transfers between devices  10.6 us (12%)
  waiting for transfers between devices  1.35 us (1%)
    all_to_all x2, blocking collectives, exchange(): sent = lax.all_to_all(rows.reshape(count, 1, width), axis, 0, 0, tiled=True)  46.8 us
    all_to_all x1, blocking collectives, shards(): lax.all_to_all(message.reshape(parts, LINES, extent), 'space', 0, 0, tile...  14.9 us
    pallas_call x1, Pallas kernels, shards(): call(analysis_kernel, [(K * BACK, 128)], [SMEM] + [VMEM] * 7, SCRATCH, 32...  10.3 us
    ppermute x1, starting transfers between devices, shards(): after = lax.ppermute(field, 'space', down)  8.49 us
    ppermute x1, starting transfers between devices, shards(): far = lax.ppermute(near, 'space', [(i, i ^ 1) for i in range(parts)])  2.1 us
  transfers between devices with their start and end apart: 3, of which 2 were waited for; matrix products, arithmetic and copies ran while one was open for 1% of the time, Pallas kernels for 3%

profile of v9, /device:TPU:8, one launch (start us, length us, event | category | flops | bytes accessed | tf_op | source)
XLA Modules:
  0.0 90.0 jit_solution(10887635192033638725)
XLA Ops:
  0.0 0.0 copy-start
  0.0 0.0 copy-start.1
  0.0 0.0 copy-start.2
  0.0 0.0 copy-start.4
  0.0 0.0 copy-start.3
  0.0 0.0 collective-permute-start
  0.1 8.5 %collective-permute-start.1 = (f32[3,2,48,128]{3,2,1,0:T(8,128)}, f32[3,2,48,128]{3,2,1,0:T(8,128)S(1)}, u32[]{:S(2)}, u32[]{:S(2)}) collective-permute-start(f32[3,2,48,128]{3,2,1,0:T(8,128)} %bitcast.25), channel_id=1, source_target_pairs={{1,0},{2,1},{3,2},{4,3},{5,4},{6,5},{7,6},{8,7},{9,8},{10,9},{11,1... | collective-permute-start | bytes 442376 | tf_op jit(solution)/shard_map/ppermute | solution.py:429
  8.5 0.8 fusion.5
  9.3 1.1 %shard_map.74.weights = f32[4096,128]{1,0:T(8,128)S(1)} custom-call(s32[32,128]{1,0:T(8,128)S(1)} %get-tuple-element.36.code), custom_call_target="tpu_custom_call" | custom-call | tf_op jit(solution)/shard_map/pallas_call | solution.py:430
  10.5 0.0 copy-done
  10.5 0.0 copy-done.1
  10.5 0.0 copy-done.2
  10.5 0.6 shard_map.73
  11.1 0.0 copy-done.4
  11.1 0.0 copy-done.3
  11.2 0.4 collective-permute-done.before
  11.6 0.0 collective-permute-done.1.after
  11.6 1.5 %shard_map.75 = (f32[384,128]{1,0:T(8,128)S(1)}, f32[3,288,128]{2,1,0:T(8,128)S(1)}) custom-call(f32[3,2,48,128]{3,2,1,0:T(8,128)S(1)} %collective-permute-done.before, f32[3,2,48,128]{3,2,1,0:T(8,128)S(1)} %get-tuple-element.24.own, f32[3,2,48,128]{3,2,1,0:T(8,128)S(1)} %collective-permute-done.1.after, s32[1,512]{1,0:T(1,128)S(1)} %bitcast.30, ...), custom_call_target="tpu_custom_call" | custom-call | tf_op jit(solution)/shard_map/pallas_call | solution.py:434
  13.1 14.9 %all_to_all.15 = f32[16,24,128]{2,1,0:T(8,128)S(1)} all-to-all(f32[16,24,128]{2,1,0:T(8,128)S(1)} %bitcast.23), channel_id=1, replica_groups=mesh['member'=32,'space'=16] {'space'}, dimensions={0} | all-to-all | bytes 393216 | tf_op jit(solution)/shard_map/all_to_all | solution.py:437
  28.0 0.3 shard_map.76
  28.3 31.4 %all_to_all.16 = f32[32,1,5248]{2,1,0:T(1,128)S(1)} all-to-all(f32[32,1,5248]{2,1,0:T(1,128)S(1)} %bitcast.19), channel_id=1, replica_groups=mesh['member'=32,'space'=16] {'member'}, dimensions={0} | all-to-all | bytes 1343488 | tf_op jit(solution)/shard_map/all_to_all | solution.py:398
  59.7 0.2 shard_map.77.near
  59.9 2.1 %collective-permute-start.2 = (f32[1024,128]{1,0:T(8,128)S(1)}, f32[1024,128]{1,0:T(8,128)S(1)}, u32[]{:S(2)}, u32[]{:S(2)}) collective-permute-start(f32[1024,128]{1,0:T(8,128)S(1)} %shard_map.77.near), channel_id=1, source_target_pairs={{0,1},{1,0},{2,3},{3,2},{4,5},{5,4},{6,7},{7,6},{8,9},{9,8},{10,11... | collective-permute-start | bytes 1572872 | tf_op jit(solution)/shard_map/ppermute | solution.py:447
  62.0 0.8 shard_map.78
  62.8 0.9 %collective-permute-done.2.far = f32[1024,128]{1,0:T(8,128)S(1)} collective-permute-done((f32[1024,128]{1,0:T(8,128)S(1)}, f32[1024,128]{1,0:T(8,128)S(1)}, u32[]{:S(2)}, u32[]{:S(2)}) %collective-permute-start.2) | collective-permute-done | bytes 524320 | tf_op jit(solution)/shard_map/ppermute | solution.py:447
  63.7 10.3 %shard_map.79 = f32[288,128]{1,0:T(8,128)S(1)} custom-call(s32[2048]{0:T(1024)S(1)} %fusion.15.places, f32[4096,128]{1,0:T(8,128)S(1)} %shard_map.74.weights, f32[1024,128]{1,0:T(8,128)S(1)} %shard_map.77.near, f32[1024,128]{1,0:T(8,128)S(1)} %collective-permute-done.2.far, bf16[4,256,576]{2,1,0:T(8,128)(2,1)S(1)} %get-tuple-element.31.tiles, ...), custom_call_target="tpu_custom_call" | custom-call | tf_op jit(solution)/shard_map/pallas_call | solution.py:454
  74.0 15.3 %all_to_all.17 = f32[32,1,1152]{2,1,0:T(1,128)S(1)} all-to-all(f32[32,1,1152]{2,1,0:T(1,128)S(1)} %bitcast.21), channel_id=1, replica_groups=mesh['member'=32,'space'=16] {'member'}, dimensions={0} | all-to-all | bytes 294912 | tf_op jit(solution)/shard_map/all_to_all | solution.py:398
  89.3 0.7 shard_map.80
  (2 shorter events, 0.0 us)
Async XLA Ops:
  0.0 10.5 %copy-start = (f32[1,3,2,48,128]{4,3,2,1,0:T(8,128)S(1)}, f32[1,3,2,48,128]{4,3,2,1,0:T(8,128)}, u32[]{:S(2)}) copy-start(f32[1,3,2,48,128]{4,3,2,1,0:T(8,128)} %param.7) | copy-start | bytes 442372
  0.0 10.5 %copy-start.1 = (s32[512]{0:T(512)S(1)}, s32[512]{0:T(512)}, u32[]{:S(2)}) copy-start(s32[512]{0:T(512)} %param.8) | copy-start | bytes 6148
  0.0 10.5 %copy-start.2 = (s32[512]{0:T(512)S(1)}, s32[512]{0:T(512)}, u32[]{:S(2)}) copy-start(s32[512]{0:T(512)} %param.9) | copy-start | bytes 6148
  0.0 11.1 %copy-start.4 = (f32[8192]{0:T(1024)S(1)}, f32[8192]{0:T(1024)}, u32[]{:S(2)}) copy-start(f32[8192]{0:T(1024)} %param.10) | copy-start | bytes 98308
  0.0 11.1 %copy-start.3 = (f32[8192]{0:T(1024)S(1)}, f32[8192]{0:T(1024)}, u32[]{:S(2)}) copy-start(f32[8192]{0:T(1024)} %param.11) | copy-start | bytes 98308
  0.0 11.6 %collective-permute-start = (f32[3,2,48,128]{3,2,1,0:T(8,128)}, f32[3,2,48,128]{3,2,1,0:T(8,128)S(1)}, u32[]{:S(2)}, u32[]{:S(2)}) collective-permute-start(f32[3,2,48,128]{3,2,1,0:T(8,128)} %bitcast.24), channel_id=1, source_target_pairs={{0,1},{1,2},{2,3},{3,4},{4,5},{5,6},{6,7},{7,8},{8,9},{9,10},{10,1... | collective-permute-start | bytes 442376 | tf_op jit(solution)/shard_map/ppermute | solution.py:428
  0.1 11.5 %collective-permute-start.1 = (f32[3,2,48,128]{3,2,1,0:T(8,128)}, f32[3,2,48,128]{3,2,1,0:T(8,128)S(1)}, u32[]{:S(2)}, u32[]{:S(2)}) collective-permute-start(f32[3,2,48,128]{3,2,1,0:T(8,128)} %bitcast.25), channel_id=1, source_target_pairs={{1,0},{2,1},{3,2},{4,3},{5,4},{6,5},{7,6},{8,7},{9,8},{10,9},{11,1... | collective-permute-start | bytes 442376 | tf_op jit(solution)/shard_map/ppermute | solution.py:429
  59.9 3.8 %collective-permute-start.2 = (f32[1024,128]{1,0:T(8,128)S(1)}, f32[1024,128]{1,0:T(8,128)S(1)}, u32[]{:S(2)}, u32[]{:S(2)}) collective-permute-start(f32[1024,128]{1,0:T(8,128)S(1)} %shard_map.77.near), channel_id=1, source_target_pairs={{0,1},{1,0},{2,3},{3,2},{4,5},{5,4},{6,7},{7,6},{8,9},{9,8},{10,11... | collective-permute-start | bytes 1572872 | tf_op jit(solution)/shard_map/ppermute | solution.py:447
